TPU v7x, 32 devices: a whole 2x2x4 slice. The times are simulated.
32 devices in a mesh: dp: 2 (over y), expert: 16 (over z, x, core).
Axes of the slice: x: 2, y: 2, z: 4, core: 2. Of those that a mesh axis runs over, the one named last changes fastest.
Arguments:
- tokens: bfloat16 [4096, 2048], P(('dp', 'expert')), may hold values from -6 to 6
- routes: int32 [4096, 2], P(('dp', 'expert')), may hold values from 0 to 15, all different within a row; in each aligned block of 128 rows (0 to 127, 128 to 255, ...) at most 24 rows name the same one
- gates: float32 [4096, 2], P(('dp', 'expert')), may hold values from 0.05 to 1
- grad_out: bfloat16 [4096, 2048], P(('dp', 'expert')), may hold values from -6 to 6
- w_gate: bfloat16 [16, 2048, 768], P('expert', 'dp'), may hold values from -0.125 to 0.125
- w_up: bfloat16 [16, 2048, 768], P('expert', 'dp'), may hold values from -0.125 to 0.125
- w_down: bfloat16 [16, 768, 2048], P('expert', None, 'dp'), may hold values from -0.21875 to 0.21875
Outputs:
- grad_tokens: bfloat16 [4096, 2048], P(('dp', 'expert'))
- grad_gates: float32 [4096, 2], P(('dp', 'expert'))
- grad_down: float32 [16, 768, 2048], P('expert', None, 'dp')
Inputs may be any that keep to these rules, and one draw needn't show every extreme that they name: Within the rows of one device no expert is named by more than 24 routes, a bound that some block reaches; the 2 experts of a token differ.
All inputs are finite; a program needn't handle non-finite values.
Results may differ from a plain program's by a relative error of at most 0.015.
Values may be sent and summed in bfloat16 or wider, within the bound.
No kernel may reach another device: no remote copies, remote signals or barrier semaphores. Data moves between devices by JAX's collectives and lax.ppermute only.
A program may use at most 128 MiB of HBM per device.

v0:
```python
import functools

import jax
import jax.numpy as jnp
from jax import lax
from jax.experimental import pallas as pl
from jax.experimental.pallas import tpu as pltpu
from jax.sharding import PartitionSpec as P

LANES = 128
VMEM_BYTES = 24 * 1024 * 1024


def contract_last(left, right):
    return lax.dot_general(
        left, right, (((1,), (1,)), ((), ())), preferred_element_type=jnp.float32
    )


def contract_first(left, right):
    return lax.dot_general(
        left, right, (((0,), (0,)), ((), ())), preferred_element_type=jnp.float32
    )


def tile_of(extent, most):
    return most if extent % most == 0 else extent


def slot_positions(routes, experts, stride, base):
    top, count = routes.shape
    labels = lax.broadcasted_iota(jnp.int32, (experts, count), 0)
    named = [labels == routes[k : k + 1, :] for k in range(top)]
    marks = sum(jnp.where(m, 1.0, 0.0) for m in named)
    earlier = lax.broadcasted_iota(jnp.int32, (count, count), 0) < lax.broadcasted_iota(
        jnp.int32, (count, count), 1
    )
    rank = jnp.dot(
        marks.astype(jnp.bfloat16),
        jnp.where(earlier, 1.0, 0.0).astype(jnp.bfloat16),
        preferred_element_type=jnp.float32,
    )
    slot = rank + (labels * stride + base).astype(jnp.float32)
    return [
        jnp.sum(jnp.where(m, slot, 0.0), axis=0, keepdims=True).astype(jnp.int32) for m in named
    ]


def rows_of(ref, groups, cap, which):
    value = ref[...].astype(jnp.float32)
    count, width = value.shape
    value = value.reshape(count // (groups * cap), groups, cap, width)[:, which]
    return value.reshape(count // groups, width).astype(ref.dtype)


def dispatch_tokens(experts, cap, place_ref, routes_ref, tokens_ref, out_ref, pos_ref, pick_ref):
    @pl.when(pl.program_id(0) == 0)
    def _():
        pos = slot_positions(routes_ref[...], experts, cap, 0)
        rows = lax.broadcasted_iota(jnp.int32, pick_ref.shape, 0)
        pick_ref[...] = sum(jnp.where(rows == p, 1.0, 0.0) for p in pos).astype(jnp.bfloat16)
        for k, p in enumerate(pos):
            pos_ref[k : k + 1, :] = p

    out_ref[...] = jnp.dot(
        pick_ref[...], tokens_ref[...], preferred_element_type=jnp.float32
    ).astype(out_ref.dtype)


def dispatch_scaled(experts, cap, groups, place_ref, *refs):
    routes_refs, gate_refs = refs[:groups], refs[groups : 2 * groups]
    grad_refs, (out_ref, pick_ref, scale_ref) = refs[2 * groups : 3 * groups], refs[3 * groups :]
    count = grad_refs[0].shape[0]
    slots = out_ref.shape[0]

    @pl.when(pl.program_id(0) == 0)
    def _():
        rows = lax.broadcasted_iota(jnp.int32, (slots, count), 0)
        total = jnp.zeros((slots, 1), jnp.float32)
        for q in range(groups):
            pos = slot_positions(routes_refs[q][...], experts, groups * cap, q * cap)
            hit = jnp.zeros((slots, count), jnp.float32)
            weight = jnp.zeros((slots, count), jnp.float32)
            for k, p in enumerate(pos):
                here = rows == p
                hit = hit + jnp.where(here, 1.0, 0.0)
                weight = weight + jnp.where(here, gate_refs[q][k : k + 1, :], 0.0)
            pick_ref[:, q * count : (q + 1) * count] = hit.astype(jnp.bfloat16)
            total = total + jnp.sum(weight, axis=1, keepdims=True)
        scale_ref[...] = jnp.broadcast_to(total, scale_ref.shape)

    grads = jnp.concatenate([ref[...] for ref in grad_refs], axis=0)
    rows = jnp.dot(pick_ref[...], grads, preferred_element_type=jnp.float32)
    out_ref[...] = (scale_ref[:, :1] * rows).astype(out_ref.dtype)


def back_kernel(groups, cap, rows_ref, down_ref, own_ref, *rest):
    others, all_ref = rest[: groups - 1], rest[groups - 1]
    slots, hidden = own_ref.shape
    for q in range(groups):
        all_ref[q * slots : (q + 1) * slots, :] = rows_of(rows_ref, groups, cap, q)
    step = tile_of(hidden, 256)

    @pl.loop(0, hidden // step)
    def _(j):
        cols = pl.ds(pl.multiple_of(j * step, step), step)
        for q, ref in enumerate((own_ref, *others)):
            part = contract_last(all_ref[q * slots : (q + 1) * slots, :], down_ref[cols, :])
            ref[:, cols] = part.astype(ref.dtype)


def weight_views(refs):
    gates, ups = [refs[0]], [refs[1]]
    share = refs[0].shape[0]
    for ref in refs[2:]:
        gates.append(ref.at[:share])
        ups.append(ref.at[share:])
    return gates, ups


def forward_kernel(groups, x_ref, *refs):
    gates, ups = weight_views(refs[: groups + 1])
    pre_gate_ref, pre_up_ref, hidden_ref, held_ref, sems = refs[groups + 1 :]
    share, hidden = gates[0].shape
    step = tile_of(hidden, 256)
    spans = [slice(at, at + step) for at in range(0, hidden, step)]
    copies = [
        [
            pltpu.make_async_copy(ref.at[:, cols], held_ref.at[i, :, cols], sems.at[i, j])
            for i, ref in enumerate(gates + ups)
        ]
        for j, cols in enumerate(spans)
    ]
    for column in copies:
        for copy in column:
            copy.start()

    def against(first, cols):
        return sum(
            jnp.dot(
                x_ref[:, k * share : (k + 1) * share],
                held_ref[first + k, :, cols],
                preferred_element_type=jnp.float32,
            )
            for k in range(groups)
        )

    for column, cols in zip(copies, spans):
        for copy in column:
            copy.wait()
        pre_gate = against(0, cols)
        pre_up = against(groups, cols)
        pre_gate_ref[:, cols] = pre_gate
        pre_up_ref[:, cols] = pre_up
        hidden_ref[:, cols] = (pre_gate * jax.nn.sigmoid(pre_gate) * pre_up).astype(jnp.bfloat16)


def backward_kernel(groups, pre_gate_ref, pre_up_ref, *refs):
    parts, weights = refs[:groups], refs[groups : 2 * groups + 1]
    out_ref, d_gate_ref, d_up_ref, held_ref, rows_ref, sems, out_sems = refs[2 * groups + 1 :]
    gates, ups = weight_views(weights)
    share, hidden = gates[0].shape
    width = groups * share
    block = tile_of(share, 512)
    pieces = [(k, at) for k in range(groups) for at in range(0, share, block)]
    copies = [
        [
            pltpu.make_async_copy(
                ref.at[at : at + block], held_ref.at[i, at : at + block], sems.at[h, n]
            )
            for h, (i, ref) in enumerate(((k, gates[k]), (groups + k, ups[k])))
        ]
        for n, (k, at) in enumerate(pieces)
    ]
    for pair in copies:
        for copy in pair:
            copy.start()
    pre_gate, pre_up = pre_gate_ref[...], pre_up_ref[...]
    back = sum(part[...].astype(jnp.float32) for part in parts)
    sig = jax.nn.sigmoid(pre_gate)
    act = pre_gate * sig
    slope = sig * (1.0 + pre_gate * (1.0 - sig))
    score = jnp.sum(back * (act * pre_up), axis=1, keepdims=True)
    d_gate_ref[...] = (back * pre_up * slope).astype(jnp.bfloat16)
    d_up_ref[...] = (back * act).astype(jnp.bfloat16)
    rows_ref[:, width:] = jnp.broadcast_to(score, (score.shape[0], LANES)).astype(rows_ref.dtype)
    outs = []

    def send(cols):
        copy = pltpu.make_async_copy(
            rows_ref.at[:, cols], out_ref.at[:, cols], out_sems.at[len(outs)]
        )
        copy.start()
        outs.append(copy)

    send(slice(width, width + LANES))
    for (k, at), pair in zip(pieces, copies):
        for copy in pair:
            copy.wait()
        cols = slice(k * share + at, k * share + at + block)
        grad = contract_last(d_gate_ref[...], held_ref[k, at : at + block])
        grad += contract_last(d_up_ref[...], held_ref[groups + k, at : at + block])
        rows_ref[:, cols] = grad.astype(rows_ref.dtype)
        send(cols)
    for copy in outs:
        copy.wait()


def combine_kernel(groups, place_ref, pos_ref, gate_ref, rows_ref, tokens_ref, gates_ref):
    top, count = pos_ref.shape
    slots = rows_ref.shape[0]
    width = tokens_ref.shape[1]
    share = width // groups
    places = lax.broadcasted_iota(jnp.int32, (slots, count), 0)
    picks = [
        jnp.where(places == pos_ref[k : k + 1, :], 1.0, 0.0).astype(jnp.bfloat16)
        for k in range(top)
    ]
    both = sum(picks)
    for k in range(groups):
        at = lax.rem(place_ref[0] - k + groups, groups) * share
        tokens_ref[:, pl.ds(pl.multiple_of(at, share), share)] = contract_first(
            both, rows_ref[:, k * share : (k + 1) * share]
        ).astype(tokens_ref.dtype)
    for k in range(top):
        score = contract_first(rows_ref[:, width:], picks[k])
        gates_ref[k : k + 1, :] = score[:1, :] / gate_ref[k : k + 1, :]


def per_device(tokens, routes, gates, grad_out, w_gate, w_up, w_down):
    experts = lax.axis_size("expert")
    groups = lax.axis_size("dp")
    group = lax.axis_index("dp")
    count, width = tokens.shape
    top = routes.shape[1]
    cap = 3 * count * top // (2 * experts)
    slots = experts * cap
    share = width // groups
    hidden = w_gate.shape[2]
    params = pltpu.CompilerParams(vmem_limit_bytes=VMEM_BYTES)
    place = group.astype(jnp.int32).reshape(1)

    def shifted(value, by):
        return lax.ppermute(value, "dp", [(i, (i + by) % groups) for i in range(groups)])

    def exchanged(rows):
        split = rows.reshape(experts, rows.shape[0] // experts, rows.shape[1])
        moved = lax.all_to_all(split, "expert", split_axis=0, concat_axis=0, tiled=True)
        return moved.reshape(rows.shape)

    routes_t, gates_t = jnp.transpose(routes), jnp.transpose(gates)
    routes_all = [routes_t] + [shifted(routes_t, k) for k in range(1, groups)]
    gates_all = [gates_t] + [shifted(gates_t, k) for k in range(1, groups)]
    grads = [
        shifted(
            lax.dynamic_slice(grad_out, (0, lax.rem(group + k, groups) * share), (count, share)), k
        )
        for k in range(1, groups)
    ]
    both = jnp.concatenate([w_gate[0], w_up[0]], axis=0)
    weights = [w_gate[0], w_up[0]] + [shifted(both, k) for k in range(1, groups)]

    def in_hbm(value):
        return pltpu.with_memory_space_constraint(value, pltpu.HBM)

    block = tile_of(share, 512)
    steps = share // block
    small_spec = pl.BlockSpec((top, count), lambda c, g: (0, 0))
    scaled = pl.pallas_call(
        functools.partial(dispatch_scaled, experts, cap, groups),
        out_shape=pltpu.HBM((groups * slots, share), jnp.bfloat16),
        grid_spec=pltpu.PrefetchScalarGridSpec(
            num_scalar_prefetch=1,
            grid=(steps,),
            in_specs=[small_spec] * (2 * groups)
            + [pl.BlockSpec((count, block), lambda c, g: (0, g[0] * steps + c))]
            + [pl.BlockSpec((count, block), lambda c, g: (0, c))] * (groups - 1),
            out_specs=pl.BlockSpec((groups * slots, block), lambda c, g: (0, c)),
            scratch_shapes=[
                pltpu.VMEM((groups * slots, groups * count), jnp.bfloat16),
                pltpu.VMEM((groups * slots, LANES), jnp.float32),
            ],
        ),
        compiler_params=params,
        name="dispatch_scaled",
    )(place, in_hbm(routes_t), *routes_all[1:], in_hbm(gates_t), *gates_all[1:], in_hbm(grad_out), *grads)
    scaled_rows = exchanged(scaled)

    sent, pos = pl.pallas_call(
        functools.partial(dispatch_tokens, experts, cap),
        out_shape=(
            pltpu.HBM((slots, width), jnp.bfloat16),
            jax.ShapeDtypeStruct((top, count), jnp.int32),
        ),
        grid_spec=pltpu.PrefetchScalarGridSpec(
            num_scalar_prefetch=1,
            grid=(groups,),
            in_specs=[
                small_spec,
                pl.BlockSpec(
                    (count, share), lambda k, g: (0, lax.rem(g[0] - k + groups, groups))
                ),
            ],
            out_specs=(pl.BlockSpec((slots, share), lambda k, g: (0, k)), small_spec),
            scratch_shapes=[pltpu.VMEM((slots, count), jnp.bfloat16)],
        ),
        compiler_params=params,
        name="dispatch_tokens",
    )(place, in_hbm(routes_t), in_hbm(tokens))
    x_rows = exchanged(sent)

    back_own, *rest = pl.pallas_call(
        functools.partial(back_kernel, groups, cap),
        out_shape=[pltpu.HBM((slots, hidden), jnp.float32)]
        + [pltpu.HBM((slots, hidden), jnp.bfloat16)] * (groups - 1)
        + [pltpu.HBM((groups * slots, share), jnp.bfloat16)],
        compiler_params=params,
        name="back",
    )(scaled_rows, in_hbm(w_down[0]))
    scaled_all = rest[-1]
    back_parts = [back_own] + [shifted(rest[k - 1], -k) for k in range(1, groups)]

    whole_spec = pl.BlockSpec(memory_space=pltpu.VMEM)
    weight_spec = pl.BlockSpec(memory_space=pl.ANY)
    weights = [in_hbm(value) for value in weights]
    held = pltpu.VMEM((2 * groups, share, hidden), jnp.bfloat16)
    pre_gate, pre_up, hidden_own = pl.pallas_call(
        functools.partial(forward_kernel, groups),
        out_shape=[
            jax.ShapeDtypeStruct((slots, hidden), jnp.float32),
            jax.ShapeDtypeStruct((slots, hidden), jnp.float32),
            pltpu.HBM((slots, hidden), jnp.bfloat16),
        ],
        in_specs=[pl.BlockSpec()] + [weight_spec] * (groups + 1),
        scratch_shapes=[
            held,
            pltpu.SemaphoreType.DMA((2 * groups, hidden // tile_of(hidden, 256))),
        ],
        compiler_params=params,
        name="forward",
    )(x_rows, *weights)

    pieces = groups * (share // tile_of(share, 512))
    returning = pl.pallas_call(
        functools.partial(backward_kernel, groups),
        out_shape=pltpu.HBM((slots, width + LANES), jnp.bfloat16),
        in_specs=[pl.BlockSpec()] * (2 + groups) + [weight_spec] * (groups + 1),
        out_specs=pl.BlockSpec(memory_space=pl.ANY),
        scratch_shapes=[
            pltpu.VMEM((slots, hidden), jnp.bfloat16),
            pltpu.VMEM((slots, hidden), jnp.bfloat16),
            held,
            pltpu.VMEM((slots, width + LANES), jnp.bfloat16),
            pltpu.SemaphoreType.DMA((2, pieces)),
            pltpu.SemaphoreType.DMA((pieces + 1,)),
        ],
        compiler_params=params,
        name="backward",
    )(pre_gate, pre_up, *back_parts, *weights)
    returned = exchanged(returning)

    hiddens = [hidden_own] + [shifted(hidden_own, k) for k in range(1, groups)]
    grad_down = contract_first(jnp.concatenate(hiddens, axis=0), scaled_all)[None]

    grad_tokens, grad_gates = pl.pallas_call(
        functools.partial(combine_kernel, groups),
        out_shape=(
            jax.ShapeDtypeStruct((count, width), jnp.bfloat16),
            jax.ShapeDtypeStruct((top, count), jnp.float32),
        ),
        in_specs=[pl.BlockSpec(memory_space=pltpu.SMEM)] + [whole_spec] * 3,
        compiler_params=params,
        name="combine",
    )(place, pos, gates_t, returned)
    return (grad_tokens, jnp.transpose(grad_gates), grad_down)


def solution(mesh):
    placed = (
        P(("dp", "expert"), None),
        P(("dp", "expert"), None),
        P(("dp", "expert"), None),
        P(("dp", "expert"), None),
        P("expert", "dp", None),
        P("expert", "dp", None),
        P("expert", None, "dp"),
    )
    return jax.shard_map(
        per_device,
        mesh=mesh,
        in_specs=placed,
        out_specs=(P(("dp", "expert"), None), P(("dp", "expert"), None), P("expert", None, "dp")),
        check_vma=False,
    )
```

profile of v0, /device:TPU:11, one launch (start us, length us, event | category | flops | bytes accessed | tf_op | source)
XLA Modules:
  0.0 157.8 jit_solution(6272760840328795355)
XLA Ops:
  0.6 1.0 constant_dynamic-slice_fusion
  1.6 1.3 collective-permute-start.3
  2.9 0.2 collective-permute-start.1
  3.1 1.2 collective-permute-start.2
  4.4 4.5 %collective-permute-done.1.refs_1_ = s32[2,128]{1,0:T(2,128)S(1)} collective-permute-done((s32[2,128]{1,0:T(2,128)}, s32[2,128]{1,0:T(2,128)S(1)}, u32[]{:S(2)}, u32[]{:S(2)}) %collective-permute-start.1) | collective-permute-done | bytes 1056 | tf_op jit(solution)/shard_map/ppermute | solution.py:244
  8.9 0.0 collective-permute-done.2.refs_3_
  8.9 0.0 collective-permute-done.3.refs_5_
  8.9 3.1 %dispatch_scaled.1 = bf16[768,1024]{1,0:T(8,128)(2,1)} custom-call(s32[1]{0:T(128)} %bitcast.place_ref, s32[2,128]{1,0:T(2,128)} %bitcast.33, s32[2,128]{1,0:T(2,128)S(1)} %collective-permute-done.1.refs_1_, f32[2,128]{1,0:T(2,128)} %bitcast.20, f32[2,128]{1,0:T(2,128)S(1)} %collective-permute-done.2.refs_3_, bf16[128,2048]{1,0:T(8,128)(2,1)} %refs_4_.1, ...), custom_call_target="tpu_custom_call" | custom-call | tf_op jit(solution)/shard_map/dispatch_scaled/pallas_call | solution.py:269
  12.0 7.6 %all-to-all-start.1 = ((bf16[16,48,1024]{2,1,0:T(8,128)(2,1)}), bf16[16,48,1024]{2,1,0:T(8,128)(2,1)S(1)}, u32[]{:S(2)}, u32[]{:S(2)}) async-start(bf16[16,48,1024]{2,1,0:T(8,128)(2,1)} %bitcast.29), calls=%async_computation.1 | async-start | bytes 3145728 | tf_op jit(solution)/shard_map/all_to_all | solution.py:248
  19.6 0.0 copy-done.2
  19.6 3.3 %pad_maximum_fusion = bf16[2048,768]{1,0:T(8,128)(2,1)} fusion(bf16[1024,768]{1,0:T(8,128)(2,1)} %bitcast.25, bf16[1024,768]{1,0:T(8,128)(2,1)S(1)} %bitcast.24), kind=kLoop, calls=%fused_computation | loop fusion | flops 6291456 | bytes 6291456 | tf_op jit(solution)/shard_map/concatenate | solution.py:260
  22.9 1.2 collective-permute-start
  24.1 2.8 %dispatch_tokens.1 = (bf16[384,2048]{1,0:T(8,128)(2,1)}, s32[2,128]{1,0:T(2,128)S(1)}) custom-call(s32[1]{0:T(128)} %bitcast.place_ref, s32[2,128]{1,0:T(2,128)} %bitcast.34, bf16[128,2048]{1,0:T(8,128)(2,1)} %tokens_ref.1), custom_call_target="tpu_custom_call" | custom-call | tf_op jit(solution)/shard_map/dispatch_tokens/pallas_call | solution.py:289
  27.0 29.2 %all-to-all-done.1 = bf16[16,48,1024]{2,1,0:T(8,128)(2,1)S(1)} async-done(((bf16[16,48,1024]{2,1,0:T(8,128)(2,1)}), bf16[16,48,1024]{2,1,0:T(8,128)(2,1)S(1)}, u32[]{:S(2)}, u32[]{:S(2)}) %all-to-all-start.1) | async-done | bytes 1572896 | tf_op jit(solution)/shard_map/all_to_all | solution.py:248
  56.2 4.5 %all-to-all-start = ((bf16[16,24,2048]{2,1,0:T(8,128)(2,1)}), bf16[16,24,2048]{2,1,0:T(8,128)(2,1)S(1)}, u32[]{:S(2)}, u32[]{:S(2)}) async-start(bf16[16,24,2048]{2,1,0:T(8,128)(2,1)} %bitcast.31), calls=%async_computation | async-start | bytes 3145728 | tf_op jit(solution)/shard_map/all_to_all | solution.py:248
  60.7 5.0 %back.1 = (f32[384,768]{1,0:T(8,128)}, bf16[384,768]{1,0:T(8,128)(2,1)}, bf16[768,1024]{1,0:T(8,128)(2,1)}) custom-call(bf16[768,1024]{1,0:T(8,128)(2,1)S(1)} %bitcast.17, bf16[768,1024]{1,0:T(8,128)(2,1)} %bitcast.30), custom_call_target="tpu_custom_call" | custom-call | tf_op jit(solution)/shard_map/back/pallas_call | solution.py:312
  65.7 1.2 collective-permute-start.4
  67.0 30.2 %all-to-all-done = bf16[16,24,2048]{2,1,0:T(8,128)(2,1)S(1)} async-done(((bf16[16,24,2048]{2,1,0:T(8,128)(2,1)}), bf16[16,24,2048]{2,1,0:T(8,128)(2,1)S(1)}, u32[]{:S(2)}, u32[]{:S(2)}) %all-to-all-start) | async-done | bytes 1572896 | tf_op jit(solution)/shard_map/all_to_all | solution.py:248
  97.2 0.0 collective-permute-done.refs_2_.refs_4_
  97.2 5.6 %forward.1 = (f32[384,768]{1,0:T(8,128)S(1)}, f32[384,768]{1,0:T(8,128)S(1)}, bf16[384,768]{1,0:T(8,128)(2,1)}) custom-call(bf16[384,2048]{1,0:T(8,128)(2,1)S(1)} %bitcast.18, bf16[1024,768]{1,0:T(8,128)(2,1)} %bitcast.22, bf16[1024,768]{1,0:T(8,128)(2,1)} %bitcast.26, bf16[2048,768]{1,0:T(8,128)(2,1)} %collective-permute-done.refs_2_.refs_4_), custom_call_target="tpu_custom_call" | custom-call | tf_op jit(solution)/shard_map/forward/pallas_call | solution.py:327
  102.8 2.3 %collective-permute-done.4.refs_1_ = bf16[384,768]{1,0:T(8,128)(2,1)S(1)} collective-permute-done((bf16[384,768]{1,0:T(8,128)(2,1)}, bf16[384,768]{1,0:T(8,128)(2,1)S(1)}, u32[]{:S(2)}, u32[]{:S(2)}) %collective-permute-start.4) | collective-permute-done | bytes 589856 | tf_op jit(solution)/shard_map/ppermute | solution.py:244
  105.1 0.0 copy-done
  105.1 6.2 %backward.1 = bf16[384,2176]{1,0:T(8,128)(2,1)} custom-call(f32[384,768]{1,0:T(8,128)S(1)} %get-tuple-element.15.pre_gate_ref, f32[384,768]{1,0:T(8,128)S(1)} %get-tuple-element.16.pre_up_ref, f32[384,768]{1,0:T(8,128)S(1)} %copy-done, bf16[384,768]{1,0:T(8,128)(2,1)S(1)} %collective-permute-done.4.refs_1_, bf16[1024,768]{1,0:T(8,128)(2,1)} %bitcast.23, ...), custom_call_target="tpu_custom_call" | custom-call | tf_op jit(solution)/shard_map/backward/pallas_call | solution.py:344
  111.3 0.0 copy-start.3
  111.3 7.0 %all-to-all-start.2 = ((bf16[16,24,2176]{2,1,0:T(8,128)(2,1)}), bf16[16,24,2176]{2,1,0:T(8,128)(2,1)S(1)}, u32[]{:S(2)}, u32[]{:S(2)}) async-start(bf16[16,24,2176]{2,1,0:T(8,128)(2,1)} %bitcast.28), calls=%async_computation.2 | async-start | bytes 3342336 | tf_op jit(solution)/shard_map/all_to_all | solution.py:248
  118.3 1.2 collective-permute-start.5
  119.5 13.5 %collective-permute-done.5 = bf16[384,768]{1,0:T(8,128)(2,1)S(1)} collective-permute-done((bf16[384,768]{1,0:T(8,128)(2,1)}, bf16[384,768]{1,0:T(8,128)(2,1)S(1)}, u32[]{:S(2)}, u32[]{:S(2)}) %collective-permute-start.5) | collective-permute-done | bytes 589856 | tf_op jit(solution)/shard_map/ppermute | solution.py:244
  133.0 0.0 copy-done.3
  133.0 4.2 %convolution_bitcast_fusion = f32[1,768,1024]{2,1,0:T(8,128)} fusion(bf16[768,1024]{1,0:T(8,128)(2,1)S(1)} %copy-done.3, bf16[384,768]{1,0:T(8,128)(2,1)S(1)} %collective-permute-done.5, bf16[384,768]{1,0:T(8,128)(2,1)} %get-tuple-element.21), kind=kOutput, calls=%fused_computation.1 | convolution fusion | flops 1210318848 | bytes 5898240 | tf_op jit(solution)/shard_map/dot_general | solution.py:21
  137.2 19.3 %all-to-all-done.2 = bf16[16,24,2176]{2,1,0:T(8,128)(2,1)S(1)} async-done(((bf16[16,24,2176]{2,1,0:T(8,128)(2,1)}), bf16[16,24,2176]{2,1,0:T(8,128)(2,1)S(1)}, u32[]{:S(2)}, u32[]{:S(2)}) %all-to-all-start.2) | async-done | bytes 1671200 | tf_op jit(solution)/shard_map/all_to_all | solution.py:248
  156.6 0.0 copy-done.1
  156.6 1.3 combine.1
  (3 shorter events, 0.0 us)
Async XLA Ops:
  1.6 7.3 %collective-permute-start.3 = (bf16[128,1024]{1,0:T(8,128)(2,1)S(1)}, bf16[128,1024]{1,0:T(8,128)(2,1)S(1)}, u32[]{:S(2)}, u32[]{:S(2)}) collective-permute-start(bf16[128,1024]{1,0:T(8,128)(2,1)S(1)} %constant_dynamic-slice_fusion), channel_id=1, source_target_pairs={{0,16},{16,0},{1,17},{17,1},{2,18},{18,2},{3,19},{19,3},{4,20},{20... | collective-permute-start | bytes 786440 | tf_op jit(solution)/shard_map/ppermute | solution.py:244
  2.9 6.0 %collective-permute-start.1 = (s32[2,128]{1,0:T(2,128)}, s32[2,128]{1,0:T(2,128)S(1)}, u32[]{:S(2)}, u32[]{:S(2)}) collective-permute-start(s32[2,128]{1,0:T(2,128)} %bitcast.32), channel_id=1, source_target_pairs={{0,16},{16,0},{1,17},{17,1},{2,18},{18,2},{3,19},{19,3},{4,20},{20... | collective-permute-start | bytes 3080 | tf_op jit(solution)/shard_map/ppermute | solution.py:244
  3.1 5.7 %collective-permute-start.2 = (f32[2,128]{1,0:T(2,128)}, f32[2,128]{1,0:T(2,128)S(1)}, u32[]{:S(2)}, u32[]{:S(2)}) collective-permute-start(f32[2,128]{1,0:T(2,128)} %bitcast.19), channel_id=1, source_target_pairs={{0,16},{16,0},{1,17},{17,1},{2,18},{18,2},{3,19},{19,3},{4,20},{20... | collective-permute-start | bytes 3080 | tf_op jit(solution)/shard_map/ppermute | solution.py:244
  12.0 7.6 %copy-start.2 = (bf16[1,1024,768]{2,1,0:T(8,128)(2,1)S(1)}, bf16[1,1024,768]{2,1,0:T(8,128)(2,1)}, u32[]{:S(2)}) copy-start(bf16[1,1024,768]{2,1,0:T(8,128)(2,1)} %param.11) | copy-start | bytes 4718596
  12.0 44.2 %all-to-all-start.1 = ((bf16[16,48,1024]{2,1,0:T(8,128)(2,1)}), bf16[16,48,1024]{2,1,0:T(8,128)(2,1)S(1)}, u32[]{:S(2)}, u32[]{:S(2)}) async-start(bf16[16,48,1024]{2,1,0:T(8,128)(2,1)} %bitcast.29), calls=%async_computation.1 | async-start | bytes 3145728 | tf_op jit(solution)/shard_map/all_to_all | solution.py:248
  22.9 74.3 %collective-permute-start = (bf16[2048,768]{1,0:T(8,128)(2,1)}, bf16[2048,768]{1,0:T(8,128)(2,1)}, u32[]{:S(2)}, u32[]{:S(2)}) collective-permute-start(bf16[2048,768]{1,0:T(8,128)(2,1)} %pad_maximum_fusion), channel_id=1, source_target_pairs={{0,16},{16,0},{1,17},{17,1},{2,18},{18,2},{3,19},{19,3},{4,20},{20... | collective-permute-start | bytes 9437192 | tf_op jit(solution)/shard_map/ppermute | solution.py:244
  56.2 41.0 %all-to-all-start = ((bf16[16,24,2048]{2,1,0:T(8,128)(2,1)}), bf16[16,24,2048]{2,1,0:T(8,128)(2,1)S(1)}, u32[]{:S(2)}, u32[]{:S(2)}) async-start(bf16[16,24,2048]{2,1,0:T(8,128)(2,1)} %bitcast.31), calls=%async_computation | async-start | bytes 3145728 | tf_op jit(solution)/shard_map/all_to_all | solution.py:248
  65.7 39.3 %collective-permute-start.4 = (bf16[384,768]{1,0:T(8,128)(2,1)}, bf16[384,768]{1,0:T(8,128)(2,1)S(1)}, u32[]{:S(2)}, u32[]{:S(2)}) collective-permute-start(bf16[384,768]{1,0:T(8,128)(2,1)} %get-tuple-element.18), channel_id=1, source_target_pairs={{0,16},{16,0},{1,17},{17,1},{2,18},{18,2},{3,19},{19,3},{4,20},{20... | collective-permute-start | bytes 1769480 | tf_op jit(solution)/shard_map/ppermute | solution.py:244
  97.2 7.9 %copy-start = (f32[384,768]{1,0:T(8,128)S(1)}, f32[384,768]{1,0:T(8,128)}, u32[]{:S(2)}) copy-start(f32[384,768]{1,0:T(8,128)} %get-tuple-element.17.refs_0_) | copy-start | bytes 3538948
  111.3 21.8 %copy-start.3 = (bf16[768,1024]{1,0:T(8,128)(2,1)S(1)}, bf16[768,1024]{1,0:T(8,128)(2,1)}, u32[]{:S(2)}) copy-start(bf16[768,1024]{1,0:T(8,128)(2,1)} %get-tuple-element.22) | copy-start | bytes 4718596
  111.3 45.3 %all-to-all-start.2 = ((bf16[16,24,2176]{2,1,0:T(8,128)(2,1)}), bf16[16,24,2176]{2,1,0:T(8,128)(2,1)S(1)}, u32[]{:S(2)}, u32[]{:S(2)}) async-start(bf16[16,24,2176]{2,1,0:T(8,128)(2,1)} %bitcast.28), calls=%async_computation.2 | async-start | bytes 3342336 | tf_op jit(solution)/shard_map/all_to_all | solution.py:248
  118.3 14.8 %collective-permute-start.5 = (bf16[384,768]{1,0:T(8,128)(2,1)}, bf16[384,768]{1,0:T(8,128)(2,1)S(1)}, u32[]{:S(2)}, u32[]{:S(2)}) collective-permute-start(bf16[384,768]{1,0:T(8,128)(2,1)} %get-tuple-element.21), channel_id=1, source_target_pairs={{0,16},{16,0},{1,17},{17,1},{2,18},{18,2},{3,19},{19,3},{4,20},{20... | collective-permute-start | bytes 1769480 | tf_op jit(solution)/shard_map/ppermute | solution.py:244
  133.0 23.5 %copy-start.1 = (f32[128,2]{0,1:T(2,128)S(1)}, f32[128,2]{0,1:T(2,128)}, u32[]{:S(2)}) copy-start(f32[128,2]{0,1:T(2,128)} %param.9) | copy-start | bytes 3076
where the time goes:
time: 158 us
  waiting for transfers between devices  99.1 us (63%)
  starting transfers between devices  25.6 us (16%)
  Pallas kernels  24 us (15%)
  matrix products  4.19 us (3%)
  other arithmetic  3.28 us (2%)
    all_to_all x3, waiting for transfers between devices, exchanged(): lax.all_to_all(split, 'expert', split_axis=0, concat_axis=0, tiled=True)  78.8 us
    ppermute x6, waiting for transfers between devices, shifted(): lax.ppermute(value, 'dp', [(i, (i + by) % groups) for i in range(groups)])  20.3 us
    all_to_all x3, starting transfers between devices, exchanged(): lax.all_to_all(split, 'expert', split_axis=0, concat_axis=0, tiled=True)  19.1 us
    ppermute x6, starting transfers between devices, shifted(): lax.ppermute(value, 'dp', [(i, (i + by) % groups) for i in range(groups)])  6.49 us
    pallas_call x1, Pallas kernels, per_device(): pl.pallas_call(functools.partial(backward_kernel, groups), out_shape=pltp...  6.18 us
    pallas_call x1, Pallas kernels, per_device(): pl.pallas_call(functools.partial(forward_kernel, groups), out_shape=[jax....  5.6 us
    pallas_call x1, Pallas kernels, per_device(): pl.pallas_call(functools.partial(back_kernel, groups, cap), out_shape=[pl...  5.03 us
    dot_general x1, matrix products, contract_first(): lax.dot_general(left, right, (((0,), (0,)), ((), ())), preferred_element_...  4.19 us
  transfers between devices with their start and end apart: 9, of which 6 were waited for; matrix products, arithmetic and copies ran while one was open for 5% of the time, Pallas kernels for 9%

commit v1 on v0

--- a/solution.py
+++ b/solution.py
@@ -40,9 +40,10 @@
         jnp.where(earlier, 1.0, 0.0).astype(jnp.bfloat16),
         preferred_element_type=jnp.float32,
     )
-    slot = rank + (labels * stride + base).astype(jnp.float32)
+    slot = rank + (labels * stride + base + 1).astype(jnp.float32)
     return [
-        jnp.sum(jnp.where(m, slot, 0.0), axis=0, keepdims=True).astype(jnp.int32) for m in named
+        jnp.sum(jnp.where(m, slot, 0.0), axis=0, keepdims=True).astype(jnp.int32) - 1
+        for m in named
     ]
 
 
@@ -109,80 +110,65 @@
             ref[:, cols] = part.astype(ref.dtype)
 
 
-def weight_views(refs):
-    gates, ups = [refs[0]], [refs[1]]
-    share = refs[0].shape[0]
-    for ref in refs[2:]:
-        gates.append(ref.at[:share])
-        ups.append(ref.at[share:])
-    return gates, ups
-
-
-def forward_kernel(groups, x_ref, *refs):
-    gates, ups = weight_views(refs[: groups + 1])
-    pre_gate_ref, pre_up_ref, hidden_ref, held_ref, sems = refs[groups + 1 :]
-    share, hidden = gates[0].shape
+def hold_kernel(groups, *refs):
+    (own_gate, own_up), others = refs[:2], refs[2 : groups + 1]
+    held_ref, sems = refs[groups + 1 :]
+    share = own_gate.shape[0]
+    sources = [own_gate, *[ref.at[:share] for ref in others]]
+    sources += [own_up, *[ref.at[share:] for ref in others]]
+    copies = [
+        pltpu.make_async_copy(ref, held_ref.at[i], sems.at[i]) for i, ref in enumerate(sources)
+    ]
+    for copy in copies:
+        copy.start()
+    for copy in copies:
+        copy.wait()
+
+
+def forward_kernel(groups, x_ref, held_ref, *refs):
+    act_ref, slope_ref, value_ref, hidden_ref, rows_ref, sems = refs
+    share, hidden = held_ref.shape[1:]
     step = tile_of(hidden, 256)
-    spans = [slice(at, at + step) for at in range(0, hidden, step)]
-    copies = [
-        [
-            pltpu.make_async_copy(ref.at[:, cols], held_ref.at[i, :, cols], sems.at[i, j])
-            for i, ref in enumerate(gates + ups)
-        ]
-        for j, cols in enumerate(spans)
-    ]
-    for column in copies:
-        for copy in column:
-            copy.start()
+    copies = []
+    for k in range(groups):
+        cols = slice(k * share, (k + 1) * share)
+        copies.append(pltpu.make_async_copy(x_ref.at[:, cols], rows_ref.at[:, cols], sems.at[k]))
+        copies[k].start()
+    for copy in copies:
+        copy.wait()
 
     def against(first, cols):
         return sum(
             jnp.dot(
-                x_ref[:, k * share : (k + 1) * share],
+                rows_ref[:, k * share : (k + 1) * share],
                 held_ref[first + k, :, cols],
                 preferred_element_type=jnp.float32,
             )
             for k in range(groups)
         )
 
-    for column, cols in zip(copies, spans):
-        for copy in column:
-            copy.wait()
+    for at in range(0, hidden, step):
+        cols = slice(at, at + step)
         pre_gate = against(0, cols)
         pre_up = against(groups, cols)
-        pre_gate_ref[:, cols] = pre_gate
-        pre_up_ref[:, cols] = pre_up
-        hidden_ref[:, cols] = (pre_gate * jax.nn.sigmoid(pre_gate) * pre_up).astype(jnp.bfloat16)
-
-
-def backward_kernel(groups, pre_gate_ref, pre_up_ref, *refs):
-    parts, weights = refs[:groups], refs[groups : 2 * groups + 1]
-    out_ref, d_gate_ref, d_up_ref, held_ref, rows_ref, sems, out_sems = refs[2 * groups + 1 :]
-    gates, ups = weight_views(weights)
-    share, hidden = gates[0].shape
+        sig = jax.nn.sigmoid(pre_gate)
+        act = pre_gate * sig
+        hidden_f = act * pre_up
+        act_ref[:, cols] = act
+        slope_ref[:, cols] = pre_up * (sig * (1.0 + pre_gate * (1.0 - sig)))
+        value_ref[:, cols] = hidden_f
+        hidden_ref[:, cols] = hidden_f.astype(hidden_ref.dtype)
+
+
+def backward_kernel(groups, act_ref, slope_ref, value_ref, held_ref, *refs):
+    parts, (out_ref, d_gate_ref, d_up_ref, rows_ref, out_sems) = refs[:groups], refs[groups:]
+    share = held_ref.shape[1]
     width = groups * share
     block = tile_of(share, 512)
-    pieces = [(k, at) for k in range(groups) for at in range(0, share, block)]
-    copies = [
-        [
-            pltpu.make_async_copy(
-                ref.at[at : at + block], held_ref.at[i, at : at + block], sems.at[h, n]
-            )
-            for h, (i, ref) in enumerate(((k, gates[k]), (groups + k, ups[k])))
-        ]
-        for n, (k, at) in enumerate(pieces)
-    ]
-    for pair in copies:
-        for copy in pair:
-            copy.start()
-    pre_gate, pre_up = pre_gate_ref[...], pre_up_ref[...]
     back = sum(part[...].astype(jnp.float32) for part in parts)
-    sig = jax.nn.sigmoid(pre_gate)
-    act = pre_gate * sig
-    slope = sig * (1.0 + pre_gate * (1.0 - sig))
-    score = jnp.sum(back * (act * pre_up), axis=1, keepdims=True)
-    d_gate_ref[...] = (back * pre_up * slope).astype(jnp.bfloat16)
-    d_up_ref[...] = (back * act).astype(jnp.bfloat16)
+    score = jnp.sum(back * value_ref[...], axis=1, keepdims=True)
+    d_gate_ref[...] = (back * slope_ref[...]).astype(jnp.bfloat16)
+    d_up_ref[...] = (back * act_ref[...]).astype(jnp.bfloat16)
     rows_ref[:, width:] = jnp.broadcast_to(score, (score.shape[0], LANES)).astype(rows_ref.dtype)
     outs = []
 
@@ -194,14 +180,13 @@
         outs.append(copy)
 
     send(slice(width, width + LANES))
-    for (k, at), pair in zip(pieces, copies):
-        for copy in pair:
-            copy.wait()
-        cols = slice(k * share + at, k * share + at + block)
-        grad = contract_last(d_gate_ref[...], held_ref[k, at : at + block])
-        grad += contract_last(d_up_ref[...], held_ref[groups + k, at : at + block])
-        rows_ref[:, cols] = grad.astype(rows_ref.dtype)
-        send(cols)
+    for k in range(groups):
+        for at in range(0, share, block):
+            cols = slice(k * share + at, k * share + at + block)
+            grad = contract_last(d_gate_ref[...], held_ref[k, at : at + block])
+            grad += contract_last(d_up_ref[...], held_ref[groups + k, at : at + block])
+            rows_ref[:, cols] = grad.astype(rows_ref.dtype)
+            send(cols)
     for copy in outs:
         copy.wait()
 
@@ -258,6 +243,7 @@
         for k in range(1, groups)
     ]
     both = jnp.concatenate([w_gate[0], w_up[0]], axis=0)
+    both, gates_own = lax.optimization_barrier((both, gates_t))
     weights = [w_gate[0], w_up[0]] + [shifted(both, k) for k in range(1, groups)]
 
     def in_hbm(value):
@@ -283,7 +269,7 @@
         ),
         compiler_params=params,
         name="dispatch_scaled",
-    )(place, in_hbm(routes_t), *routes_all[1:], in_hbm(gates_t), *gates_all[1:], in_hbm(grad_out), *grads)
+    )(place, in_hbm(routes_t), *routes_all[1:], in_hbm(gates_own), *gates_all[1:], in_hbm(grad_out), *grads)
     scaled_rows = exchanged(scaled)
 
     sent, pos = pl.pallas_call(
@@ -321,42 +307,44 @@
     back_parts = [back_own] + [shifted(rest[k - 1], -k) for k in range(1, groups)]
 
     whole_spec = pl.BlockSpec(memory_space=pltpu.VMEM)
-    weight_spec = pl.BlockSpec(memory_space=pl.ANY)
-    weights = [in_hbm(value) for value in weights]
-    held = pltpu.VMEM((2 * groups, share, hidden), jnp.bfloat16)
-    pre_gate, pre_up, hidden_own = pl.pallas_call(
+    any_spec = pl.BlockSpec(memory_space=pl.ANY)
+    held = pl.pallas_call(
+        functools.partial(hold_kernel, groups),
+        out_shape=pltpu.VMEM((2 * groups, share, hidden), jnp.bfloat16),
+        in_specs=[any_spec] * (groups + 1),
+        scratch_shapes=[pltpu.SemaphoreType.DMA((2 * groups,))],
+        compiler_params=params,
+        name="hold",
+    )(*[in_hbm(value) for value in weights])
+
+    *factors, hidden_own = pl.pallas_call(
         functools.partial(forward_kernel, groups),
-        out_shape=[
-            jax.ShapeDtypeStruct((slots, hidden), jnp.float32),
-            jax.ShapeDtypeStruct((slots, hidden), jnp.float32),
-            pltpu.HBM((slots, hidden), jnp.bfloat16),
+        out_shape=[pltpu.VMEM((slots, hidden), jnp.float32)] * 3
+        + [pltpu.HBM((slots, hidden), jnp.bfloat16)],
+        in_specs=[any_spec, whole_spec],
+        scratch_shapes=[
+            pltpu.VMEM((slots, width), jnp.bfloat16),
+            pltpu.SemaphoreType.DMA((groups,)),
         ],
-        in_specs=[pl.BlockSpec()] + [weight_spec] * (groups + 1),
-        scratch_shapes=[
-            held,
-            pltpu.SemaphoreType.DMA((2 * groups, hidden // tile_of(hidden, 256))),
-        ],
         compiler_params=params,
         name="forward",
-    )(x_rows, *weights)
+    )(in_hbm(x_rows), held)
 
     pieces = groups * (share // tile_of(share, 512))
     returning = pl.pallas_call(
         functools.partial(backward_kernel, groups),
         out_shape=pltpu.HBM((slots, width + LANES), jnp.bfloat16),
-        in_specs=[pl.BlockSpec()] * (2 + groups) + [weight_spec] * (groups + 1),
-        out_specs=pl.BlockSpec(memory_space=pl.ANY),
+        in_specs=[whole_spec] * (4 + groups),
+        out_specs=any_spec,
         scratch_shapes=[
             pltpu.VMEM((slots, hidden), jnp.bfloat16),
             pltpu.VMEM((slots, hidden), jnp.bfloat16),
-            held,
             pltpu.VMEM((slots, width + LANES), jnp.bfloat16),
-            pltpu.SemaphoreType.DMA((2, pieces)),
             pltpu.SemaphoreType.DMA((pieces + 1,)),
         ],
         compiler_params=params,
         name="backward",
-    )(pre_gate, pre_up, *back_parts, *weights)
+    )(*factors, held, *back_parts)
     returned = exchanged(returning)
 
     hiddens = [hidden_own] + [shifted(hidden_own, k) for k in range(1, groups)]

time: 158 us -> 157 us (level)
  waiting for transfers between devices: 99.1 us -> 91.6 us
  local copies, waits for them, and re-layouts: 0.99 us -> 7.56 us
    all_to_all x3, waiting for transfers between devices: 78.8 us -> 54.2 us  [exchanged(): lax.all_to_all(split, 'expert', split_axis=0, concat_axis=0, tiled=True)]
    ppermute x6, waiting for transfers between devices: 20.3 us -> 37.4 us  [shifted(): lax.ppermute(value, 'dp', [(i, (i + by) % groups) for i in range(groups)])]
    unnamed x8 -> x12, local copies, waits for them, and re-layouts: 0.02 us -> 6.59 us
    pallas_call x1, Pallas kernels: 6.18 us -> 3.59 us  [per_device(): pl.pallas_call(functools.partial(backward_kernel, groups), out_shape=pltp...]
    pallas_call x1 -> x2, Pallas kernels: 5.6 us -> 7.88 us  [the longest x1 5.02 us: per_device(): pl.pallas_call(functools.partial(forward_kernel, groups), out_shape=[pltp...]
  transfers between devices with their start and end apart: 9 -> 9, of which waited for: 6 -> 6; matrix products, arithmetic and copies ran while one was open for 5% -> 6% of each run, Pallas kernels for 9% -> 10%
where the time goes in v1:
time: 157 us; the launch traced here: 156 us
  waiting for transfers between devices  91.6 us (58%)
  starting transfers between devices  24.4 us (16%)
  Pallas kernels  23.9 us (15%)
  local copies, waits for them, and re-layouts  7.56 us (5%)
  matrix products  4.19 us (3%)
  other arithmetic  3.75 us (2%)
    all_to_all x3, waiting for transfers between devices, exchanged(): lax.all_to_all(split, 'expert', split_axis=0, concat_axis=0, tiled=True)  54.2 us
    ppermute x6, waiting for transfers between devices, shifted(): lax.ppermute(value, 'dp', [(i, (i + by) % groups) for i in range(groups)])  37.4 us
    all_to_all x3, starting transfers between devices, exchanged(): lax.all_to_all(split, 'expert', split_axis=0, concat_axis=0, tiled=True)  17.9 us
    unnamed x12, local copies, waits for them, and re-layouts  6.59 us
    ppermute x6, starting transfers between devices, shifted(): lax.ppermute(value, 'dp', [(i, (i + by) % groups) for i in range(groups)])  6.49 us
    pallas_call x1, Pallas kernels, per_device(): pl.pallas_call(functools.partial(back_kernel, groups, cap), out_shape=[pl...  5.12 us
    pallas_call x1, Pallas kernels, per_device(): pl.pallas_call(functools.partial(forward_kernel, groups), out_shape=[pltp...  5.02 us
    dot_general x1, matrix products, contract_first(): lax.dot_general(left, right, (((0,), (0,)), ((), ())), preferred_element_...  4.19 us
  transfers between devices with their start and end apart: 9, of which 6 were waited for; matrix products, arithmetic and copies ran while one was open for 6% of the time, Pallas kernels for 10%

profile of v1, /device:TPU:11, one launch (start us, length us, event | category | flops | bytes accessed | tf_op | source)
XLA Modules:
  0.0 156.1 jit_solution(3769624340362770629)
XLA Ops:
  0.6 1.3 collective-permute-start.1
  1.9 0.2 collective-permute-start.2
  2.2 1.0 constant_dynamic-slice_fusion
  3.1 1.3 collective-permute-start.3
  4.4 3.7 %pad_maximum_fusion = bf16[2048,768]{1,0:T(8,128)(2,1)} fusion(bf16[1024,768]{1,0:T(8,128)(2,1)} %bitcast.24, bf16[1024,768]{1,0:T(8,128)(2,1)} %bitcast.22), kind=kLoop, calls=%fused_computation | loop fusion | flops 6291456 | bytes 6291456 | tf_op jit(solution)/shard_map/concatenate | solution.py:245
  8.2 0.0 collective-permute-done.1.refs_1_
  8.2 0.0 collective-permute-done.2.refs_3_
  8.2 1.6 %collective-permute-done.3.refs_5_ = bf16[128,1024]{1,0:T(8,128)(2,1)S(1)} collective-permute-done((bf16[128,1024]{1,0:T(8,128)(2,1)S(1)}, bf16[128,1024]{1,0:T(8,128)(2,1)S(1)}, u32[]{:S(2)}, u32[]{:S(2)}) %collective-permute-start.3) | collective-permute-done | bytes 262176 | tf_op jit(solution)/shard_map/ppermute | solution.py:229
  9.8 3.1 %dispatch_scaled.1 = bf16[768,1024]{1,0:T(8,128)(2,1)} custom-call(s32[1]{0:T(128)} %bitcast.place_ref, s32[2,128]{1,0:T(2,128)} %bitcast.31, s32[2,128]{1,0:T(2,128)S(1)} %collective-permute-done.1.refs_1_, f32[2,128]{1,0:T(2,128)} %bitcast.19, f32[2,128]{1,0:T(2,128)S(1)} %collective-permute-done.2.refs_3_, bf16[128,2048]{1,0:T(8,128)(2,1)} %refs_4_.1, ...), custom_call_target="tpu_custom_call" | custom-call | tf_op jit(solution)/shard_map/dispatch_scaled/pallas_call | solution.py:255
  12.9 8.0 %all-to-all-start.1 = ((bf16[16,48,1024]{2,1,0:T(8,128)(2,1)}), bf16[16,48,1024]{2,1,0:T(8,128)(2,1)S(1)}, u32[]{:S(2)}, u32[]{:S(2)}) async-start(bf16[16,48,1024]{2,1,0:T(8,128)(2,1)} %bitcast.26), calls=%async_computation.1 | async-start | bytes 3145728 | tf_op jit(solution)/shard_map/all_to_all | solution.py:233
  20.9 1.2 collective-permute-start
  22.2 2.8 %dispatch_tokens.1 = (bf16[384,2048]{1,0:T(8,128)(2,1)}, s32[2,128]{1,0:T(2,128)S(1)}) custom-call(s32[1]{0:T(128)} %bitcast.place_ref, s32[2,128]{1,0:T(2,128)} %bitcast.32, bf16[128,2048]{1,0:T(8,128)(2,1)} %tokens_ref.1), custom_call_target="tpu_custom_call" | custom-call | tf_op jit(solution)/shard_map/dispatch_tokens/pallas_call | solution.py:275
  25.0 32.5 %all-to-all-done.1 = bf16[16,48,1024]{2,1,0:T(8,128)(2,1)S(1)} async-done(((bf16[16,48,1024]{2,1,0:T(8,128)(2,1)}), bf16[16,48,1024]{2,1,0:T(8,128)(2,1)S(1)}, u32[]{:S(2)}, u32[]{:S(2)}) %all-to-all-start.1) | async-done | bytes 1572896 | tf_op jit(solution)/shard_map/all_to_all | solution.py:233
  57.5 4.5 %all-to-all-start = ((bf16[16,24,2048]{2,1,0:T(8,128)(2,1)}), bf16[16,24,2048]{2,1,0:T(8,128)(2,1)S(1)}, u32[]{:S(2)}, u32[]{:S(2)}) async-start(bf16[16,24,2048]{2,1,0:T(8,128)(2,1)} %bitcast.29), calls=%async_computation | async-start | bytes 3145728 | tf_op jit(solution)/shard_map/all_to_all | solution.py:233
  62.0 5.1 %back.1 = (f32[384,768]{1,0:T(8,128)}, bf16[384,768]{1,0:T(8,128)(2,1)}, bf16[768,1024]{1,0:T(8,128)(2,1)}) custom-call(bf16[768,1024]{1,0:T(8,128)(2,1)S(1)} %bitcast.17, bf16[768,1024]{1,0:T(8,128)(2,1)} %bitcast.28), custom_call_target="tpu_custom_call" | custom-call | tf_op jit(solution)/shard_map/back/pallas_call | solution.py:298
  67.2 1.2 collective-permute-start.4
  68.4 22.2 %collective-permute-done.refs_2_ = bf16[2048,768]{1,0:T(8,128)(2,1)} collective-permute-done((bf16[2048,768]{1,0:T(8,128)(2,1)}, bf16[2048,768]{1,0:T(8,128)(2,1)}, u32[]{:S(2)}, u32[]{:S(2)}) %collective-permute-start) | collective-permute-done | bytes 3145760 | tf_op jit(solution)/shard_map/ppermute | solution.py:229
  90.6 2.9 %hold.1.held_ref = bf16[4,1024,768]{2,1,0:T(8,128)(2,1)S(1)} custom-call(bf16[1024,768]{1,0:T(8,128)(2,1)} %bitcast.23, bf16[1024,768]{1,0:T(8,128)(2,1)} %bitcast.25, bf16[2048,768]{1,0:T(8,128)(2,1)} %collective-permute-done.refs_2_), custom_call_target="tpu_custom_call" | custom-call | tf_op jit(solution)/shard_map/hold/pallas_call | solution.py:311
  93.5 0.0 copy-start
  93.5 2.7 %copy-done = bf16[4,1024,768]{2,1,0:T(8,128)(2,1)} copy-done((bf16[4,1024,768]{2,1,0:T(8,128)(2,1)}, bf16[4,1024,768]{2,1,0:T(8,128)(2,1)S(1)}, u32[]{:S(2)}) %copy-start) | copy-done | bytes 6291480
  96.1 2.4 %all-to-all-done = bf16[16,24,2048]{2,1,0:T(8,128)(2,1)S(1)} async-done(((bf16[16,24,2048]{2,1,0:T(8,128)(2,1)}), bf16[16,24,2048]{2,1,0:T(8,128)(2,1)S(1)}, u32[]{:S(2)}, u32[]{:S(2)}) %all-to-all-start) | async-done | bytes 1572896 | tf_op jit(solution)/shard_map/all_to_all | solution.py:233
  98.5 1.1 copy-done.4
  99.7 2.8 %copy-done.1 = bf16[4,1024,768]{2,1,0:T(8,128)(2,1)S(1)} copy-done((bf16[4,1024,768]{2,1,0:T(8,128)(2,1)S(1)}, bf16[4,1024,768]{2,1,0:T(8,128)(2,1)}, u32[]{:S(2)}) %copy-start.1) | copy-done | bytes 6291480
  102.4 5.0 %forward.1 = (f32[384,768]{1,0:T(8,128)S(1)}, f32[384,768]{1,0:T(8,128)S(1)}, f32[384,768]{1,0:T(8,128)S(1)}, bf16[384,768]{1,0:T(8,128)(2,1)}) custom-call(bf16[384,2048]{1,0:T(8,128)(2,1)} %bitcast.27, bf16[4,1024,768]{2,1,0:T(8,128)(2,1)S(1)} %copy-done.1), custom_call_target="tpu_custom_call" | custom-call | tf_op jit(solution)/shard_map/forward/pallas_call | solution.py:320
  107.5 0.0 collective-permute-done.4.refs_1_
  107.5 3.6 %backward.1 = bf16[384,2176]{1,0:T(8,128)(2,1)} custom-call(f32[384,768]{1,0:T(8,128)S(1)} %get-tuple-element.19.act_ref, f32[384,768]{1,0:T(8,128)S(1)} %get-tuple-element.20.slope_ref, f32[384,768]{1,0:T(8,128)S(1)} %get-tuple-element.21.value_ref, bf16[4,1024,768]{2,1,0:T(8,128)(2,1)S(1)} %copy-done.1, f32[384,768]{1,0:T(8,128)S(1)} %copy-done.2, ...), custom_call_target="tpu_custom_call" | custom-call | tf_op jit(solution)/shard_map/backward/pallas_call | solution.py:334
  111.1 5.4 %all-to-all-start.2 = ((bf16[16,24,2176]{2,1,0:T(8,128)(2,1)}), bf16[16,24,2176]{2,1,0:T(8,128)(2,1)S(1)}, u32[]{:S(2)}, u32[]{:S(2)}) async-start(bf16[16,24,2176]{2,1,0:T(8,128)(2,1)} %bitcast.21), calls=%async_computation.2 | async-start | bytes 3342336 | tf_op jit(solution)/shard_map/all_to_all | solution.py:233
  116.5 1.2 collective-permute-start.5
  117.7 13.5 %collective-permute-done.5 = bf16[384,768]{1,0:T(8,128)(2,1)S(1)} collective-permute-done((bf16[384,768]{1,0:T(8,128)(2,1)}, bf16[384,768]{1,0:T(8,128)(2,1)S(1)}, u32[]{:S(2)}, u32[]{:S(2)}) %collective-permute-start.5) | collective-permute-done | bytes 589856 | tf_op jit(solution)/shard_map/ppermute | solution.py:229
  131.2 4.2 %convolution_bitcast_fusion = f32[1,768,1024]{2,1,0:T(8,128)} fusion(bf16[768,1024]{1,0:T(8,128)(2,1)S(1)} %copy-done.5, bf16[384,768]{1,0:T(8,128)(2,1)S(1)} %collective-permute-done.5, bf16[384,768]{1,0:T(8,128)(2,1)} %get-tuple-element.27), kind=kOutput, calls=%fused_computation.1 | convolution fusion | flops 1210318848 | bytes 5898240 | tf_op jit(solution)/shard_map/dot_general | solution.py:21
  135.4 19.3 %all-to-all-done.2 = bf16[16,24,2176]{2,1,0:T(8,128)(2,1)S(1)} async-done(((bf16[16,24,2176]{2,1,0:T(8,128)(2,1)}), bf16[16,24,2176]{2,1,0:T(8,128)(2,1)S(1)}, u32[]{:S(2)}, u32[]{:S(2)}) %all-to-all-start.2) | async-done | bytes 1671200 | tf_op jit(solution)/shard_map/all_to_all | solution.py:233
  154.8 1.3 combine.1
  (8 shorter events, 0.0 us)
Async XLA Ops:
  0.6 7.6 %collective-permute-start.1 = (s32[2,128]{1,0:T(2,128)}, s32[2,128]{1,0:T(2,128)S(1)}, u32[]{:S(2)}, u32[]{:S(2)}) collective-permute-start(s32[2,128]{1,0:T(2,128)} %bitcast.30), channel_id=1, source_target_pairs={{0,16},{16,0},{1,17},{17,1},{2,18},{18,2},{3,19},{19,3},{4,20},{20... | collective-permute-start | bytes 3080 | tf_op jit(solution)/shard_map/ppermute | solution.py:229
  1.9 6.3 %collective-permute-start.2 = (f32[2,128]{1,0:T(2,128)}, f32[2,128]{1,0:T(2,128)S(1)}, u32[]{:S(2)}, u32[]{:S(2)}) collective-permute-start(f32[2,128]{1,0:T(2,128)} %bitcast.18), channel_id=1, source_target_pairs={{0,16},{16,0},{1,17},{17,1},{2,18},{18,2},{3,19},{19,3},{4,20},{20... | collective-permute-start | bytes 3080 | tf_op jit(solution)/shard_map/ppermute | solution.py:229
  3.1 6.6 %collective-permute-start.3 = (bf16[128,1024]{1,0:T(8,128)(2,1)S(1)}, bf16[128,1024]{1,0:T(8,128)(2,1)S(1)}, u32[]{:S(2)}, u32[]{:S(2)}) collective-permute-start(bf16[128,1024]{1,0:T(8,128)(2,1)S(1)} %constant_dynamic-slice_fusion), channel_id=1, source_target_pairs={{0,16},{16,0},{1,17},{17,1},{2,18},{18,2},{3,19},{19,3},{4,20},{20... | collective-permute-start | bytes 786440 | tf_op jit(solution)/shard_map/ppermute | solution.py:229
  12.9 44.6 %all-to-all-start.1 = ((bf16[16,48,1024]{2,1,0:T(8,128)(2,1)}), bf16[16,48,1024]{2,1,0:T(8,128)(2,1)S(1)}, u32[]{:S(2)}, u32[]{:S(2)}) async-start(bf16[16,48,1024]{2,1,0:T(8,128)(2,1)} %bitcast.26), calls=%async_computation.1 | async-start | bytes 3145728 | tf_op jit(solution)/shard_map/all_to_all | solution.py:233
  20.9 69.6 %collective-permute-start = (bf16[2048,768]{1,0:T(8,128)(2,1)}, bf16[2048,768]{1,0:T(8,128)(2,1)}, u32[]{:S(2)}, u32[]{:S(2)}) collective-permute-start(bf16[2048,768]{1,0:T(8,128)(2,1)} %pad_maximum_fusion), channel_id=1, source_target_pairs={{0,16},{16,0},{1,17},{17,1},{2,18},{18,2},{3,19},{19,3},{4,20},{20... | collective-permute-start | bytes 9437192 | tf_op jit(solution)/shard_map/ppermute | solution.py:229
  57.5 41.0 %all-to-all-start = ((bf16[16,24,2048]{2,1,0:T(8,128)(2,1)}), bf16[16,24,2048]{2,1,0:T(8,128)(2,1)S(1)}, u32[]{:S(2)}, u32[]{:S(2)}) async-start(bf16[16,24,2048]{2,1,0:T(8,128)(2,1)} %bitcast.29), calls=%async_computation | async-start | bytes 3145728 | tf_op jit(solution)/shard_map/all_to_all | solution.py:233
  67.2 40.3 %collective-permute-start.4 = (bf16[384,768]{1,0:T(8,128)(2,1)}, bf16[384,768]{1,0:T(8,128)(2,1)S(1)}, u32[]{:S(2)}, u32[]{:S(2)}) collective-permute-start(bf16[384,768]{1,0:T(8,128)(2,1)} %get-tuple-element.24), channel_id=1, source_target_pairs={{0,16},{16,0},{1,17},{17,1},{2,18},{18,2},{3,19},{19,3},{4,20},{20... | collective-permute-start | bytes 1769480 | tf_op jit(solution)/shard_map/ppermute | solution.py:229
  93.5 2.7 %copy-start = (bf16[4,1024,768]{2,1,0:T(8,128)(2,1)}, bf16[4,1024,768]{2,1,0:T(8,128)(2,1)S(1)}, u32[]{:S(2)}) copy-start(bf16[4,1024,768]{2,1,0:T(8,128)(2,1)S(1)} %hold.1.held_ref) | copy-start | bytes 18874372
  98.5 1.1 copy-start.4
  99.7 2.8 %copy-start.1 = (bf16[4,1024,768]{2,1,0:T(8,128)(2,1)S(1)}, bf16[4,1024,768]{2,1,0:T(8,128)(2,1)}, u32[]{:S(2)}) copy-start(bf16[4,1024,768]{2,1,0:T(8,128)(2,1)} %copy-done) | copy-start | bytes 18874372
  102.4 5.0 %copy-start.2 = (f32[384,768]{1,0:T(8,128)S(1)}, f32[384,768]{1,0:T(8,128)}, u32[]{:S(2)}) copy-start(f32[384,768]{1,0:T(8,128)} %get-tuple-element.23.refs_0_) | copy-start | bytes 3538948
  111.1 20.2 %copy-start.5 = (bf16[768,1024]{1,0:T(8,128)(2,1)S(1)}, bf16[768,1024]{1,0:T(8,128)(2,1)}, u32[]{:S(2)}) copy-start(bf16[768,1024]{1,0:T(8,128)(2,1)} %get-tuple-element.28) | copy-start | bytes 4718596
  111.1 43.7 %all-to-all-start.2 = ((bf16[16,24,2176]{2,1,0:T(8,128)(2,1)}), bf16[16,24,2176]{2,1,0:T(8,128)(2,1)S(1)}, u32[]{:S(2)}, u32[]{:S(2)}) async-start(bf16[16,24,2176]{2,1,0:T(8,128)(2,1)} %bitcast.21), calls=%async_computation.2 | async-start | bytes 3342336 | tf_op jit(solution)/shard_map/all_to_all | solution.py:233
  116.5 14.8 %collective-permute-start.5 = (bf16[384,768]{1,0:T(8,128)(2,1)}, bf16[384,768]{1,0:T(8,128)(2,1)S(1)}, u32[]{:S(2)}, u32[]{:S(2)}) collective-permute-start(bf16[384,768]{1,0:T(8,128)(2,1)} %get-tuple-element.27), channel_id=1, source_target_pairs={{0,16},{16,0},{1,17},{17,1},{2,18},{18,2},{3,19},{19,3},{4,20},{20... | collective-permute-start | bytes 1769480 | tf_op jit(solution)/shard_map/ppermute | solution.py:229
  131.2 23.5 %copy-start.3 = (f32[128,2]{0,1:T(2,128)S(1)}, f32[128,2]{0,1:T(2,128)}, u32[]{:S(2)}) copy-start(f32[128,2]{0,1:T(2,128)} %param.9) | copy-start | bytes 3076

commit v2 on v1

--- a/solution.py
+++ b/solution.py
@@ -110,54 +110,66 @@
             ref[:, cols] = part.astype(ref.dtype)
 
 
-def hold_kernel(groups, *refs):
+def forward_kernel(groups, x_ref, *refs):
     (own_gate, own_up), others = refs[:2], refs[2 : groups + 1]
-    held_ref, sems = refs[groups + 1 :]
-    share = own_gate.shape[0]
-    sources = [own_gate, *[ref.at[:share] for ref in others]]
-    sources += [own_up, *[ref.at[share:] for ref in others]]
-    copies = [
-        pltpu.make_async_copy(ref, held_ref.at[i], sems.at[i]) for i, ref in enumerate(sources)
-    ]
-    for copy in copies:
-        copy.start()
-    for copy in copies:
-        copy.wait()
-
-
-def forward_kernel(groups, x_ref, held_ref, *refs):
-    act_ref, slope_ref, value_ref, hidden_ref, rows_ref, sems = refs
+    act_ref, slope_ref, value_ref, hidden_ref, held_ref = refs[groups + 1 : groups + 6]
+    rows_ref, gate_sum_ref, up_sum_ref, sems, row_sems = refs[groups + 6 :]
     share, hidden = held_ref.shape[1:]
-    step = tile_of(hidden, 256)
-    copies = []
+    step = tile_of(hidden, 384)
+    gates = [own_gate, *[ref.at[:share] for ref in others]]
+    ups = [own_up, *[ref.at[share:] for ref in others]]
+
+    def load(ref, i):
+        return pltpu.make_async_copy(ref, held_ref.at[i], sems.at[i])
+
+    def columns(k):
+        return slice(k * share, (k + 1) * share)
+
+    stages = []
     for k in range(groups):
-        cols = slice(k * share, (k + 1) * share)
-        copies.append(pltpu.make_async_copy(x_ref.at[:, cols], rows_ref.at[:, cols], sems.at[k]))
-        copies[k].start()
-    for copy in copies:
-        copy.wait()
-
-    def against(first, cols):
-        return sum(
-            jnp.dot(
-                rows_ref[:, k * share : (k + 1) * share],
-                held_ref[first + k, :, cols],
-                preferred_element_type=jnp.float32,
+        cols = columns(k)
+        rows = pltpu.make_async_copy(x_ref.at[:, cols], rows_ref.at[:, cols], row_sems.at[k])
+        stages.append([rows, load(gates[k], k)])
+        stages.append([load(ups[k], groups + k)])
+
+    def start(n):
+        for copy in stages[n] if n < len(stages) else ():
+            copy.start()
+
+    def finish(n):
+        for copy in stages[n]:
+            copy.wait()
+
+    start(0)
+    start(1)
+    for k in range(groups):
+        x = rows_ref.at[:, columns(k)]
+        finish(2 * k)
+        start(2 * k + 2)
+        for at in range(0, hidden, step):
+            cols = slice(at, at + step)
+            part = jnp.dot(x[...], held_ref[k, :, cols], preferred_element_type=jnp.float32)
+            gate_sum_ref[:, cols] = part if k == 0 else gate_sum_ref[:, cols] + part
+        finish(2 * k + 1)
+        start(2 * k + 3)
+        for at in range(0, hidden, step):
+            cols = slice(at, at + step)
+            pre_up = jnp.dot(
+                x[...], held_ref[groups + k, :, cols], preferred_element_type=jnp.float32
             )
-            for k in range(groups)
-        )
-
-    for at in range(0, hidden, step):
-        cols = slice(at, at + step)
-        pre_gate = against(0, cols)
-        pre_up = against(groups, cols)
-        sig = jax.nn.sigmoid(pre_gate)
-        act = pre_gate * sig
-        hidden_f = act * pre_up
-        act_ref[:, cols] = act
-        slope_ref[:, cols] = pre_up * (sig * (1.0 + pre_gate * (1.0 - sig)))
-        value_ref[:, cols] = hidden_f
-        hidden_ref[:, cols] = hidden_f.astype(hidden_ref.dtype)
+            if k > 0:
+                pre_up += up_sum_ref[:, cols]
+            if k < groups - 1:
+                up_sum_ref[:, cols] = pre_up
+                continue
+            pre_gate = gate_sum_ref[:, cols]
+            sig = jax.nn.sigmoid(pre_gate)
+            act = pre_gate * sig
+            hidden_f = act * pre_up
+            act_ref[:, cols] = act
+            slope_ref[:, cols] = pre_up * (sig * (1.0 + pre_gate * (1.0 - sig)))
+            value_ref[:, cols] = hidden_f
+            hidden_ref[:, cols] = hidden_f.astype(hidden_ref.dtype)
 
 
 def backward_kernel(groups, act_ref, slope_ref, value_ref, held_ref, *refs):
@@ -308,27 +320,24 @@
 
     whole_spec = pl.BlockSpec(memory_space=pltpu.VMEM)
     any_spec = pl.BlockSpec(memory_space=pl.ANY)
-    held = pl.pallas_call(
-        functools.partial(hold_kernel, groups),
-        out_shape=pltpu.VMEM((2 * groups, share, hidden), jnp.bfloat16),
-        in_specs=[any_spec] * (groups + 1),
-        scratch_shapes=[pltpu.SemaphoreType.DMA((2 * groups,))],
-        compiler_params=params,
-        name="hold",
-    )(*[in_hbm(value) for value in weights])
-
-    *factors, hidden_own = pl.pallas_call(
+    *factors, hidden_own, held = pl.pallas_call(
         functools.partial(forward_kernel, groups),
         out_shape=[pltpu.VMEM((slots, hidden), jnp.float32)] * 3
-        + [pltpu.HBM((slots, hidden), jnp.bfloat16)],
-        in_specs=[any_spec, whole_spec],
+        + [
+            pltpu.HBM((slots, hidden), jnp.bfloat16),
+            pltpu.VMEM((2 * groups, share, hidden), jnp.bfloat16),
+        ],
+        in_specs=[any_spec] * (groups + 2),
         scratch_shapes=[
             pltpu.VMEM((slots, width), jnp.bfloat16),
+            pltpu.VMEM((slots, hidden), jnp.float32),
+            pltpu.VMEM((slots, hidden), jnp.float32),
+            pltpu.SemaphoreType.DMA((2 * groups,)),
             pltpu.SemaphoreType.DMA((groups,)),
         ],
         compiler_params=params,
         name="forward",
-    )(in_hbm(x_rows), held)
+    )(in_hbm(x_rows), *[in_hbm(value) for value in weights])
 
     pieces = groups * (share // tile_of(share, 512))
     returning = pl.pallas_call(

time: 157 us -> 155 us (0.987)
  waiting for transfers between devices: 91.6 us -> 97.2 us
  local copies, waits for them, and re-layouts: 7.56 us -> 2.18 us
    all_to_all x3, waiting for transfers between devices: 54.2 us -> 82.1 us  [exchanged(): lax.all_to_all(split, 'expert', split_axis=0, concat_axis=0, tiled=True)]
    ppermute x6, waiting for transfers between devices: 37.4 us -> 15.1 us  [shifted(): lax.ppermute(value, 'dp', [(i, (i + by) % groups) for i in range(groups)])]
    unnamed x12 -> x8, local copies, waits for them, and re-layouts: 6.59 us -> 1.21 us
    pallas_call x1 -> x0, Pallas kernels: 2.87 us -> none  [per_device(): pl.pallas_call(functools.partial(hold_kernel, groups), out_shape=pltpu.VM...]
  transfers between devices with their start and end apart: 9 -> 9, of which waited for: 6 -> 5; matrix products, arithmetic and copies ran while one was open for 6% -> 6% of each run, Pallas kernels for 10% -> 9%
where the time goes in v2:
time: 155 us; the launch traced here: 154 us
  waiting for transfers between devices  97.2 us (63%)
  starting transfers between devices  23.8 us (15%)
  Pallas kernels  22.4 us (14%)
  matrix products  4.19 us (3%)
  other arithmetic  3.75 us (2%)
  local copies, waits for them, and re-layouts  2.18 us (1%)
    all_to_all x3, waiting for transfers between devices, exchanged(): lax.all_to_all(split, 'expert', split_axis=0, concat_axis=0, tiled=True)  82.1 us
    all_to_all x3, starting transfers between devices, exchanged(): lax.all_to_all(split, 'expert', split_axis=0, concat_axis=0, tiled=True)  17.3 us
    ppermute x6, waiting for transfers between devices, shifted(): lax.ppermute(value, 'dp', [(i, (i + by) % groups) for i in range(groups)])  15.1 us
    pallas_call x1, Pallas kernels, per_device(): pl.pallas_call(functools.partial(forward_kernel, groups), out_shape=[pltp...  6.55 us
    ppermute x6, starting transfers between devices, shifted(): lax.ppermute(value, 'dp', [(i, (i + by) % groups) for i in range(groups)])  6.52 us
    pallas_call x1, Pallas kernels, per_device(): pl.pallas_call(functools.partial(back_kernel, groups, cap), out_shape=[pl...  5.02 us
    dot_general x1, matrix products, contract_first(): lax.dot_general(left, right, (((0,), (0,)), ((), ())), preferred_element_...  4.19 us
    concatenate x1, other arithmetic, per_device(): both = jnp.concatenate([w_gate[0], w_up[0]], axis=0)  3.75 us
  transfers between devices with their start and end apart: 9, of which 5 were waited for; matrix products, arithmetic and copies ran while one was open for 6% of the time, Pallas kernels for 9%

profile of v2, /device:TPU:11, one launch (start us, length us, event | category | flops | bytes accessed | tf_op | source)
XLA Modules:
  0.0 154.2 jit_solution(3526271742907399572)
XLA Ops:
  0.6 1.3 collective-permute-start.1
  1.9 0.2 collective-permute-start.2
  2.2 1.0 constant_dynamic-slice_fusion
  3.1 1.3 collective-permute-start.3
  4.4 3.7 %pad_maximum_fusion = bf16[2048,768]{1,0:T(8,128)(2,1)} fusion(bf16[1024,768]{1,0:T(8,128)(2,1)} %bitcast.26, bf16[1024,768]{1,0:T(8,128)(2,1)} %bitcast.24), kind=kLoop, calls=%fused_computation | loop fusion | flops 6291456 | bytes 6291456 | tf_op jit(solution)/shard_map/concatenate | solution.py:257
  8.2 0.0 collective-permute-done.1.refs_1_
  8.2 0.0 collective-permute-done.2.refs_3_
  8.2 1.6 %collective-permute-done.3.refs_5_ = bf16[128,1024]{1,0:T(8,128)(2,1)S(1)} collective-permute-done((bf16[128,1024]{1,0:T(8,128)(2,1)S(1)}, bf16[128,1024]{1,0:T(8,128)(2,1)S(1)}, u32[]{:S(2)}, u32[]{:S(2)}) %collective-permute-start.3) | collective-permute-done | bytes 262176 | tf_op jit(solution)/shard_map/ppermute | solution.py:241
  9.8 3.1 %dispatch_scaled.1 = bf16[768,1024]{1,0:T(8,128)(2,1)} custom-call(s32[1]{0:T(128)} %bitcast.place_ref, s32[2,128]{1,0:T(2,128)} %bitcast.31, s32[2,128]{1,0:T(2,128)S(1)} %collective-permute-done.1.refs_1_, f32[2,128]{1,0:T(2,128)} %bitcast.19, f32[2,128]{1,0:T(2,128)S(1)} %collective-permute-done.2.refs_3_, bf16[128,2048]{1,0:T(8,128)(2,1)} %refs_4_.1, ...), custom_call_target="tpu_custom_call" | custom-call | tf_op jit(solution)/shard_map/dispatch_scaled/pallas_call | solution.py:267
  12.9 8.0 %all-to-all-start.1 = ((bf16[16,48,1024]{2,1,0:T(8,128)(2,1)}), bf16[16,48,1024]{2,1,0:T(8,128)(2,1)S(1)}, u32[]{:S(2)}, u32[]{:S(2)}) async-start(bf16[16,48,1024]{2,1,0:T(8,128)(2,1)} %bitcast.22), calls=%async_computation.1 | async-start | bytes 3145728 | tf_op jit(solution)/shard_map/all_to_all | solution.py:245
  20.9 1.2 collective-permute-start
  22.2 2.8 %dispatch_tokens.1 = (bf16[384,2048]{1,0:T(8,128)(2,1)}, s32[2,128]{1,0:T(2,128)S(1)}) custom-call(s32[1]{0:T(128)} %bitcast.place_ref, s32[2,128]{1,0:T(2,128)} %bitcast.32, bf16[128,2048]{1,0:T(8,128)(2,1)} %tokens_ref.1), custom_call_target="tpu_custom_call" | custom-call | tf_op jit(solution)/shard_map/dispatch_tokens/pallas_call | solution.py:287
  25.0 32.5 %all-to-all-done.1 = bf16[16,48,1024]{2,1,0:T(8,128)(2,1)S(1)} async-done(((bf16[16,48,1024]{2,1,0:T(8,128)(2,1)}), bf16[16,48,1024]{2,1,0:T(8,128)(2,1)S(1)}, u32[]{:S(2)}, u32[]{:S(2)}) %all-to-all-start.1) | async-done | bytes 1572896 | tf_op jit(solution)/shard_map/all_to_all | solution.py:245
  57.5 4.5 %all-to-all-start = ((bf16[16,24,2048]{2,1,0:T(8,128)(2,1)}), bf16[16,24,2048]{2,1,0:T(8,128)(2,1)S(1)}, u32[]{:S(2)}, u32[]{:S(2)}) async-start(bf16[16,24,2048]{2,1,0:T(8,128)(2,1)} %bitcast.29), calls=%async_computation | async-start | bytes 3145728 | tf_op jit(solution)/shard_map/all_to_all | solution.py:245
  62.0 5.0 %back.1 = (f32[384,768]{1,0:T(8,128)}, bf16[384,768]{1,0:T(8,128)(2,1)}, bf16[768,1024]{1,0:T(8,128)(2,1)}) custom-call(bf16[768,1024]{1,0:T(8,128)(2,1)S(1)} %bitcast.17, bf16[768,1024]{1,0:T(8,128)(2,1)} %bitcast.28), custom_call_target="tpu_custom_call" | custom-call | tf_op jit(solution)/shard_map/back/pallas_call | solution.py:310
  67.1 1.2 collective-permute-start.4
  68.3 30.2 %all-to-all-done = bf16[16,24,2048]{2,1,0:T(8,128)(2,1)S(1)} async-done(((bf16[16,24,2048]{2,1,0:T(8,128)(2,1)}), bf16[16,24,2048]{2,1,0:T(8,128)(2,1)S(1)}, u32[]{:S(2)}, u32[]{:S(2)}) %all-to-all-start) | async-done | bytes 1572896 | tf_op jit(solution)/shard_map/all_to_all | solution.py:245
  98.5 0.0 collective-permute-done.refs_2_
  98.5 1.2 copy-done.2
  99.7 6.5 %forward.1 = (f32[384,768]{1,0:T(8,128)S(1)}, f32[384,768]{1,0:T(8,128)S(1)}, f32[384,768]{1,0:T(8,128)S(1)}, bf16[384,768]{1,0:T(8,128)(2,1)}, bf16[4,1024,768]{2,1,0:T(8,128)(2,1)S(1)}) custom-call(bf16[384,2048]{1,0:T(8,128)(2,1)} %bitcast.23, bf16[1024,768]{1,0:T(8,128)(2,1)} %bitcast.25, bf16[1024,768]{1,0:T(8,128)(2,1)} %bitcast.27, ...), custom_call_target="tpu_custom_call" | custom-call | tf_op jit(solution)/shard_map/forward/pallas_call | solution.py:323
  106.3 0.0 collective-permute-done.4.refs_1_
  106.3 0.0 copy-done
  106.3 3.6 %backward.1 = bf16[384,2176]{1,0:T(8,128)(2,1)} custom-call(f32[384,768]{1,0:T(8,128)S(1)} %get-tuple-element.20.act_ref, f32[384,768]{1,0:T(8,128)S(1)} %get-tuple-element.21.slope_ref, f32[384,768]{1,0:T(8,128)S(1)} %get-tuple-element.22.value_ref, bf16[4,1024,768]{2,1,0:T(8,128)(2,1)S(1)} %get-tuple-element.23.held_ref, f32[384,768]{1,0:T(8,128)S(1)} %copy-done, ...), custom_call_target="tpu_custom_call" | custom-call | tf_op jit(solution)/shard_map/backward/pallas_call | solution.py:343
  109.9 0.0 copy-start.3
  109.9 4.8 %all-to-all-start.2 = ((bf16[16,24,2176]{2,1,0:T(8,128)(2,1)}), bf16[16,24,2176]{2,1,0:T(8,128)(2,1)S(1)}, u32[]{:S(2)}, u32[]{:S(2)}) async-start(bf16[16,24,2176]{2,1,0:T(8,128)(2,1)} %bitcast.21), calls=%async_computation.2 | async-start | bytes 3342336 | tf_op jit(solution)/shard_map/all_to_all | solution.py:245
  114.7 1.2 collective-permute-start.5
  115.9 13.5 %collective-permute-done.5 = bf16[384,768]{1,0:T(8,128)(2,1)S(1)} collective-permute-done((bf16[384,768]{1,0:T(8,128)(2,1)}, bf16[384,768]{1,0:T(8,128)(2,1)S(1)}, u32[]{:S(2)}, u32[]{:S(2)}) %collective-permute-start.5) | collective-permute-done | bytes 589856 | tf_op jit(solution)/shard_map/ppermute | solution.py:241
  129.4 0.0 copy-done.3
  129.4 4.2 %convolution_bitcast_fusion = f32[1,768,1024]{2,1,0:T(8,128)} fusion(bf16[768,1024]{1,0:T(8,128)(2,1)S(1)} %copy-done.3, bf16[384,768]{1,0:T(8,128)(2,1)S(1)} %collective-permute-done.5, bf16[384,768]{1,0:T(8,128)(2,1)} %get-tuple-element.29), kind=kOutput, calls=%fused_computation.1 | convolution fusion | flops 1210318848 | bytes 5898240 | tf_op jit(solution)/shard_map/dot_general | solution.py:21
  133.6 19.3 %all-to-all-done.2 = bf16[16,24,2176]{2,1,0:T(8,128)(2,1)S(1)} async-done(((bf16[16,24,2176]{2,1,0:T(8,128)(2,1)}), bf16[16,24,2176]{2,1,0:T(8,128)(2,1)S(1)}, u32[]{:S(2)}, u32[]{:S(2)}) %all-to-all-start.2) | async-done | bytes 1671200 | tf_op jit(solution)/shard_map/all_to_all | solution.py:245
  153.0 0.0 copy-done.1
  153.0 1.3 combine.1
  (3 shorter events, 0.0 us)
Async XLA Ops:
  0.6 7.6 %collective-permute-start.1 = (s32[2,128]{1,0:T(2,128)}, s32[2,128]{1,0:T(2,128)S(1)}, u32[]{:S(2)}, u32[]{:S(2)}) collective-permute-start(s32[2,128]{1,0:T(2,128)} %bitcast.30), channel_id=1, source_target_pairs={{0,16},{16,0},{1,17},{17,1},{2,18},{18,2},{3,19},{19,3},{4,20},{20... | collective-permute-start | bytes 3080 | tf_op jit(solution)/shard_map/ppermute | solution.py:241
  1.9 6.3 %collective-permute-start.2 = (f32[2,128]{1,0:T(2,128)}, f32[2,128]{1,0:T(2,128)S(1)}, u32[]{:S(2)}, u32[]{:S(2)}) collective-permute-start(f32[2,128]{1,0:T(2,128)} %bitcast.18), channel_id=1, source_target_pairs={{0,16},{16,0},{1,17},{17,1},{2,18},{18,2},{3,19},{19,3},{4,20},{20... | collective-permute-start | bytes 3080 | tf_op jit(solution)/shard_map/ppermute | solution.py:241
  3.1 6.6 %collective-permute-start.3 = (bf16[128,1024]{1,0:T(8,128)(2,1)S(1)}, bf16[128,1024]{1,0:T(8,128)(2,1)S(1)}, u32[]{:S(2)}, u32[]{:S(2)}) collective-permute-start(bf16[128,1024]{1,0:T(8,128)(2,1)S(1)} %constant_dynamic-slice_fusion), channel_id=1, source_target_pairs={{0,16},{16,0},{1,17},{17,1},{2,18},{18,2},{3,19},{19,3},{4,20},{20... | collective-permute-start | bytes 786440 | tf_op jit(solution)/shard_map/ppermute | solution.py:241
  12.9 44.6 %all-to-all-start.1 = ((bf16[16,48,1024]{2,1,0:T(8,128)(2,1)}), bf16[16,48,1024]{2,1,0:T(8,128)(2,1)S(1)}, u32[]{:S(2)}, u32[]{:S(2)}) async-start(bf16[16,48,1024]{2,1,0:T(8,128)(2,1)} %bitcast.22), calls=%async_computation.1 | async-start | bytes 3145728 | tf_op jit(solution)/shard_map/all_to_all | solution.py:245
  20.9 77.6 %collective-permute-start = (bf16[2048,768]{1,0:T(8,128)(2,1)}, bf16[2048,768]{1,0:T(8,128)(2,1)}, u32[]{:S(2)}, u32[]{:S(2)}) collective-permute-start(bf16[2048,768]{1,0:T(8,128)(2,1)} %pad_maximum_fusion), channel_id=1, source_target_pairs={{0,16},{16,0},{1,17},{17,1},{2,18},{18,2},{3,19},{19,3},{4,20},{20... | collective-permute-start | bytes 9437192 | tf_op jit(solution)/shard_map/ppermute | solution.py:241
  57.5 41.0 %all-to-all-start = ((bf16[16,24,2048]{2,1,0:T(8,128)(2,1)}), bf16[16,24,2048]{2,1,0:T(8,128)(2,1)S(1)}, u32[]{:S(2)}, u32[]{:S(2)}) async-start(bf16[16,24,2048]{2,1,0:T(8,128)(2,1)} %bitcast.29), calls=%async_computation | async-start | bytes 3145728 | tf_op jit(solution)/shard_map/all_to_all | solution.py:245
  67.1 39.2 %collective-permute-start.4 = (bf16[384,768]{1,0:T(8,128)(2,1)}, bf16[384,768]{1,0:T(8,128)(2,1)S(1)}, u32[]{:S(2)}, u32[]{:S(2)}) collective-permute-start(bf16[384,768]{1,0:T(8,128)(2,1)} %get-tuple-element.26), channel_id=1, source_target_pairs={{0,16},{16,0},{1,17},{17,1},{2,18},{18,2},{3,19},{19,3},{4,20},{20... | collective-permute-start | bytes 1769480 | tf_op jit(solution)/shard_map/ppermute | solution.py:241
  98.5 1.2 copy-start.2
  99.7 6.6 %copy-start = (f32[384,768]{1,0:T(8,128)S(1)}, f32[384,768]{1,0:T(8,128)}, u32[]{:S(2)}) copy-start(f32[384,768]{1,0:T(8,128)} %get-tuple-element.25.refs_0_) | copy-start | bytes 3538948
  109.9 19.5 %copy-start.3 = (bf16[768,1024]{1,0:T(8,128)(2,1)S(1)}, bf16[768,1024]{1,0:T(8,128)(2,1)}, u32[]{:S(2)}) copy-start(bf16[768,1024]{1,0:T(8,128)(2,1)} %get-tuple-element.30) | copy-start | bytes 4718596
  109.9 43.0 %all-to-all-start.2 = ((bf16[16,24,2176]{2,1,0:T(8,128)(2,1)}), bf16[16,24,2176]{2,1,0:T(8,128)(2,1)S(1)}, u32[]{:S(2)}, u32[]{:S(2)}) async-start(bf16[16,24,2176]{2,1,0:T(8,128)(2,1)} %bitcast.21), calls=%async_computation.2 | async-start | bytes 3342336 | tf_op jit(solution)/shard_map/all_to_all | solution.py:245
  114.7 14.8 %collective-permute-start.5 = (bf16[384,768]{1,0:T(8,128)(2,1)}, bf16[384,768]{1,0:T(8,128)(2,1)S(1)}, u32[]{:S(2)}, u32[]{:S(2)}) collective-permute-start(bf16[384,768]{1,0:T(8,128)(2,1)} %get-tuple-element.29), channel_id=1, source_target_pairs={{0,16},{16,0},{1,17},{17,1},{2,18},{18,2},{3,19},{19,3},{4,20},{20... | collective-permute-start | bytes 1769480 | tf_op jit(solution)/shard_map/ppermute | solution.py:241
  129.4 23.5 %copy-start.1 = (f32[128,2]{0,1:T(2,128)S(1)}, f32[128,2]{0,1:T(2,128)}, u32[]{:S(2)}) copy-start(f32[128,2]{0,1:T(2,128)} %param.9) | copy-start | bytes 3076

commit v3 on v2

--- a/solution.py
+++ b/solution.py
@@ -95,11 +95,13 @@
     out_ref[...] = (scale_ref[:, :1] * rows).astype(out_ref.dtype)
 
 
-def back_kernel(groups, cap, rows_ref, down_ref, own_ref, *rest):
+def back_kernel(groups, cap, mine_ref, rows_ref, down_ref, own_ref, *rest):
     others, all_ref = rest[: groups - 1], rest[groups - 1]
     slots, hidden = own_ref.shape
-    for q in range(groups):
-        all_ref[q * slots : (q + 1) * slots, :] = rows_of(rows_ref, groups, cap, q)
+    all_ref[:slots, :] = mine_ref[...]
+    for q in range(groups - 1):
+        rows = rows_ref[...] if groups == 2 else rows_of(rows_ref, groups - 1, cap, q)
+        all_ref[(q + 1) * slots : (q + 2) * slots, :] = rows
     step = tile_of(hidden, 256)
 
     @pl.loop(0, hidden // step)
@@ -110,53 +112,49 @@
             ref[:, cols] = part.astype(ref.dtype)
 
 
-def forward_kernel(groups, x_ref, *refs):
-    (own_gate, own_up), others = refs[:2], refs[2 : groups + 1]
-    act_ref, slope_ref, value_ref, hidden_ref, held_ref = refs[groups + 1 : groups + 6]
-    rows_ref, gate_sum_ref, up_sum_ref, sems, row_sems = refs[groups + 6 :]
+def forward_kernel(groups, x_ref, back_ref, *refs):
+    gates, (own_up, *others) = refs[:groups], refs[groups : 3 * groups - 1]
+    act_ref, slope_ref, value_ref, hidden_ref, held_ref, kept_ref = refs[
+        3 * groups - 1 : 3 * groups + 5
+    ]
+    gate_sum_ref, up_sum_ref, sems, back_sem = refs[3 * groups + 5 :]
     share, hidden = held_ref.shape[1:]
     step = tile_of(hidden, 384)
-    gates = [own_gate, *[ref.at[:share] for ref in others]]
-    ups = [own_up, *[ref.at[share:] for ref in others]]
-
-    def load(ref, i):
-        return pltpu.make_async_copy(ref, held_ref.at[i], sems.at[i])
-
-    def columns(k):
-        return slice(k * share, (k + 1) * share)
-
-    stages = []
+
+    def load(ref, i, to=0, n=0):
+        return pltpu.make_async_copy(ref, held_ref.at[i, to : to + ref.shape[0]], sems.at[n, i])
+
+    stages = [[load(gates[0], 0)], [load(own_up, groups)]]
+    for k in range(1, groups):
+        first, second = others[2 * k - 2 : 2 * k]
+        stages.append([load(gates[k], k)])
+        stages.append(
+            [load(first, groups + k), load(second, groups + k, first.shape[0], 1)]
+        )
+    kept = pltpu.make_async_copy(back_ref, kept_ref, back_sem.at[0])
+    for copies in (*stages, [kept]):
+        for copy in copies:
+            copy.start()
+
+    def against(i, cols):
+        k = i % groups
+        return jnp.dot(
+            x_ref[:, k * share : (k + 1) * share],
+            held_ref[i, :, cols],
+            preferred_element_type=jnp.float32,
+        )
+
+    spans = [slice(at, at + step) for at in range(0, hidden, step)]
     for k in range(groups):
-        cols = columns(k)
-        rows = pltpu.make_async_copy(x_ref.at[:, cols], rows_ref.at[:, cols], row_sems.at[k])
-        stages.append([rows, load(gates[k], k)])
-        stages.append([load(ups[k], groups + k)])
-
-    def start(n):
-        for copy in stages[n] if n < len(stages) else ():
-            copy.start()
-
-    def finish(n):
-        for copy in stages[n]:
+        for copy in stages[2 * k]:
             copy.wait()
-
-    start(0)
-    start(1)
-    for k in range(groups):
-        x = rows_ref.at[:, columns(k)]
-        finish(2 * k)
-        start(2 * k + 2)
-        for at in range(0, hidden, step):
-            cols = slice(at, at + step)
-            part = jnp.dot(x[...], held_ref[k, :, cols], preferred_element_type=jnp.float32)
+        for cols in spans:
+            part = against(k, cols)
             gate_sum_ref[:, cols] = part if k == 0 else gate_sum_ref[:, cols] + part
-        finish(2 * k + 1)
-        start(2 * k + 3)
-        for at in range(0, hidden, step):
-            cols = slice(at, at + step)
-            pre_up = jnp.dot(
-                x[...], held_ref[groups + k, :, cols], preferred_element_type=jnp.float32
-            )
+        for copy in stages[2 * k + 1]:
+            copy.wait()
+        for cols in spans:
+            pre_up = against(groups + k, cols)
             if k > 0:
                 pre_up += up_sum_ref[:, cols]
             if k < groups - 1:
@@ -170,6 +168,7 @@
             slope_ref[:, cols] = pre_up * (sig * (1.0 + pre_gate * (1.0 - sig)))
             value_ref[:, cols] = hidden_f
             hidden_ref[:, cols] = hidden_f.astype(hidden_ref.dtype)
+    kept.wait()
 
 
 def backward_kernel(groups, act_ref, slope_ref, value_ref, held_ref, *refs):
@@ -254,9 +253,10 @@
         )
         for k in range(1, groups)
     ]
-    both = jnp.concatenate([w_gate[0], w_up[0]], axis=0)
-    both, gates_own = lax.optimization_barrier((both, gates_t))
-    weights = [w_gate[0], w_up[0]] + [shifted(both, k) for k in range(1, groups)]
+    early = share * 3 // 16 if share % 256 == 0 else share // 2
+    gates_moved = [shifted(w_gate[0], k) for k in range(1, groups)]
+    ups_first = [shifted(w_up[0, :early], k) for k in range(1, groups)]
+    ups_second = [shifted(w_up[0, early:], k) for k in range(1, groups)]
 
     def in_hbm(value):
         return pltpu.with_memory_space_constraint(value, pltpu.HBM)
@@ -264,24 +264,36 @@
     block = tile_of(share, 512)
     steps = share // block
     small_spec = pl.BlockSpec((top, count), lambda c, g: (0, 0))
-    scaled = pl.pallas_call(
-        functools.partial(dispatch_scaled, experts, cap, groups),
-        out_shape=pltpu.HBM((groups * slots, share), jnp.bfloat16),
-        grid_spec=pltpu.PrefetchScalarGridSpec(
-            num_scalar_prefetch=1,
-            grid=(steps,),
-            in_specs=[small_spec] * (2 * groups)
-            + [pl.BlockSpec((count, block), lambda c, g: (0, g[0] * steps + c))]
-            + [pl.BlockSpec((count, block), lambda c, g: (0, c))] * (groups - 1),
-            out_specs=pl.BlockSpec((groups * slots, block), lambda c, g: (0, c)),
-            scratch_shapes=[
-                pltpu.VMEM((groups * slots, groups * count), jnp.bfloat16),
-                pltpu.VMEM((groups * slots, LANES), jnp.float32),
-            ],
-        ),
-        compiler_params=params,
-        name="dispatch_scaled",
-    )(place, in_hbm(routes_t), *routes_all[1:], in_hbm(gates_own), *gates_all[1:], in_hbm(grad_out), *grads)
+
+    def dispatched(routes_of, gates_of, grads_of, grads_map):
+        number = len(routes_of)
+        return pl.pallas_call(
+            functools.partial(dispatch_scaled, experts, cap, number),
+            out_shape=pltpu.HBM((number * slots, share), jnp.bfloat16),
+            grid_spec=pltpu.PrefetchScalarGridSpec(
+                num_scalar_prefetch=1,
+                grid=(steps,),
+                in_specs=[small_spec] * (2 * number)
+                + [pl.BlockSpec((count, block), grads_map)] * number,
+                out_specs=pl.BlockSpec((number * slots, block), lambda c, g: (0, c)),
+                scratch_shapes=[
+                    pltpu.VMEM((number * slots, number * count), jnp.bfloat16),
+                    pltpu.VMEM((number * slots, LANES), jnp.float32),
+                ],
+            ),
+            compiler_params=params,
+            name="dispatch_scaled",
+        )(place, *routes_of, *gates_of, *grads_of)
+
+    scaled_mine = dispatched(
+        [in_hbm(routes_t)],
+        [in_hbm(gates_t)],
+        [in_hbm(grad_out)],
+        lambda c, g: (0, g[0] * steps + c),
+    )
+    mine_rows = exchanged(scaled_mine)
+    scaled = dispatched(routes_all[1:], gates_all[1:], grads, lambda c, g: (0, c))
+    scaled, mine_rows = lax.optimization_barrier((scaled, mine_rows))
     scaled_rows = exchanged(scaled)
 
     sent, pos = pl.pallas_call(
@@ -305,6 +317,9 @@
         compiler_params=params,
         name="dispatch_tokens",
     )(place, in_hbm(routes_t), in_hbm(tokens))
+    sent, scaled_rows, gates_moved, ups_first = lax.optimization_barrier(
+        (sent, scaled_rows, gates_moved, ups_first)
+    )
     x_rows = exchanged(sent)
 
     back_own, *rest = pl.pallas_call(
@@ -314,30 +329,33 @@
         + [pltpu.HBM((groups * slots, share), jnp.bfloat16)],
         compiler_params=params,
         name="back",
-    )(scaled_rows, in_hbm(w_down[0]))
+    )(mine_rows, scaled_rows, in_hbm(w_down[0]))
     scaled_all = rest[-1]
-    back_parts = [back_own] + [shifted(rest[k - 1], -k) for k in range(1, groups)]
+    back_parts = [shifted(rest[k - 1], -k) for k in range(1, groups)]
 
     whole_spec = pl.BlockSpec(memory_space=pltpu.VMEM)
     any_spec = pl.BlockSpec(memory_space=pl.ANY)
-    *factors, hidden_own, held = pl.pallas_call(
+    weights = [w_gate[0], *gates_moved, w_up[0]]
+    for pair in zip(ups_first, ups_second):
+        weights.extend(pair)
+    *factors, hidden_own, held, back_kept = pl.pallas_call(
         functools.partial(forward_kernel, groups),
         out_shape=[pltpu.VMEM((slots, hidden), jnp.float32)] * 3
         + [
             pltpu.HBM((slots, hidden), jnp.bfloat16),
             pltpu.VMEM((2 * groups, share, hidden), jnp.bfloat16),
+            pltpu.VMEM((slots, hidden), jnp.float32),
         ],
-        in_specs=[any_spec] * (groups + 2),
+        in_specs=[whole_spec] + [any_spec] * (3 * groups),
         scratch_shapes=[
-            pltpu.VMEM((slots, width), jnp.bfloat16),
             pltpu.VMEM((slots, hidden), jnp.float32),
             pltpu.VMEM((slots, hidden), jnp.float32),
-            pltpu.SemaphoreType.DMA((2 * groups,)),
-            pltpu.SemaphoreType.DMA((groups,)),
+            pltpu.SemaphoreType.DMA((2, 2 * groups)),
+            pltpu.SemaphoreType.DMA((1,)),
         ],
         compiler_params=params,
         name="forward",
-    )(in_hbm(x_rows), *[in_hbm(value) for value in weights])
+    )(x_rows, in_hbm(back_own), *[in_hbm(value) for value in weights])
 
     pieces = groups * (share // tile_of(share, 512))
     returning = pl.pallas_call(
@@ -353,7 +371,7 @@
         ],
         compiler_params=params,
         name="backward",
-    )(*factors, held, *back_parts)
+    )(*factors, held, back_kept, *back_parts)
     returned = exchanged(returning)
 
     hiddens = [hidden_own] + [shifted(hidden_own, k) for k in range(1, groups)]

time: 155 us -> 178 us (1.15)
  waiting for transfers between devices: 97.2 us -> 114 us
  starting transfers between devices: 23.8 us -> 32.5 us
  other arithmetic: 3.75 us -> 0 us
    ppermute x6 -> x8, waiting for transfers between devices: 15.1 us -> 79.4 us  [shifted(): lax.ppermute(value, 'dp', [(i, (i + by) % groups) for i in range(groups)])]
    all_to_all x3 -> x4, waiting for transfers between devices: 82.1 us -> 34.7 us  [exchanged(): lax.all_to_all(split, 'expert', split_axis=0, concat_axis=0, tiled=True)]
    all_to_all x3 -> x4, starting transfers between devices: 17.3 us -> 25.3 us  [exchanged(): lax.all_to_all(split, 'expert', split_axis=0, concat_axis=0, tiled=True)]
    concatenate x1 -> x0, other arithmetic: 3.75 us -> none  [per_device(): both = jnp.concatenate([w_gate[0], w_up[0]], axis=0)]
    squeeze x0 -> x2, local copies, waits for them, and re-layouts: none -> 2.37 us  [the longest x1 1.39 us: per_device(): ups_second = [shifted(w_up[0, early:], k) for k in range(1, groups)]]
    pallas_call x1 -> x2, Pallas kernels: 3.14 us -> 4.26 us  [dispatched(): pl.pallas_call(functools.partial(dispatch_scaled, experts, cap, number),...]
    ppermute x6 -> x8, starting transfers between devices: 6.52 us -> 7.15 us  [shifted(): lax.ppermute(value, 'dp', [(i, (i + by) % groups) for i in range(groups)])]
  transfers between devices with their start and end apart: 9 -> 12, of which waited for: 5 -> 8; matrix products, arithmetic and copies ran while one was open for 6% -> 4% of each run, Pallas kernels for 9% -> 9%
where the time goes in v3:
time: 178 us
  waiting for transfers between devices  114 us (64%)
  starting transfers between devices  32.5 us (18%)
  Pallas kernels  23.4 us (13%)
  matrix products  4.5 us (3%)
  local copies, waits for them, and re-layouts  2.42 us (1%)
    ppermute x8, waiting for transfers between devices, shifted(): lax.ppermute(value, 'dp', [(i, (i + by) % groups) for i in range(groups)])  79.4 us
    all_to_all x4, waiting for transfers between devices, exchanged(): lax.all_to_all(split, 'expert', split_axis=0, concat_axis=0, tiled=True)  34.7 us
    all_to_all x4, starting transfers between devices, exchanged(): lax.all_to_all(split, 'expert', split_axis=0, concat_axis=0, tiled=True)  25.3 us
    ppermute x8, starting transfers between devices, shifted(): lax.ppermute(value, 'dp', [(i, (i + by) % groups) for i in range(groups)])  7.15 us
    pallas_call x1, Pallas kernels, per_device(): pl.pallas_call(functools.partial(forward_kernel, groups), out_shape=[pltp...  6.28 us
    pallas_call x1, Pallas kernels, per_device(): pl.pallas_call(functools.partial(back_kernel, groups, cap), out_shape=[pl...  5.1 us
    dot_general x1, matrix products, contract_first(): lax.dot_general(left, right, (((0,), (0,)), ((), ())), preferred_element_...  4.5 us
    pallas_call x2, Pallas kernels, dispatched(): pl.pallas_call(functools.partial(dispatch_scaled, experts, cap, number),...  4.26 us
  transfers between devices with their start and end apart: 12, of which 8 were waited for; matrix products, arithmetic and copies ran while one was open for 4% of the time, Pallas kernels for 9%

profile of v3, /device:TPU:11, one launch (start us, length us, event | category | flops | bytes accessed | tf_op | source)
XLA Modules:
  0.0 177.7 jit_solution(10628025890516259370)
XLA Ops:
  0.7 0.0 copy-start.4
  0.7 2.6 %dispatch_scaled.3 = bf16[384,1024]{1,0:T(8,128)(2,1)} custom-call(s32[1]{0:T(128)} %bitcast.place_ref, s32[2,128]{1,0:T(2,128)} %bitcast.37, f32[2,128]{1,0:T(2,128)} %bitcast.26, bf16[128,2048]{1,0:T(8,128)(2,1)} %refs_2_.1), custom_call_target="tpu_custom_call" | custom-call | tf_op jit(solution)/shard_map/dispatch_scaled/pallas_call | solution.py:270
  3.3 6.5 %all-to-all-start = ((bf16[16,24,1024]{2,1,0:T(8,128)(2,1)}), bf16[16,24,1024]{2,1,0:T(8,128)(2,1)S(1)}, u32[]{:S(2)}, u32[]{:S(2)}) async-start(bf16[16,24,1024]{2,1,0:T(8,128)(2,1)} %bitcast.31), calls=%async_computation | async-start | bytes 1572864 | tf_op jit(solution)/shard_map/all_to_all | solution.py:244
  9.9 1.3 collective-permute-start.2
  11.2 0.2 collective-permute-start.3
  11.4 1.2 collective-permute-start
  12.7 0.2 collective-permute-start.1
  12.9 38.4 %collective-permute-done.refs_0_ = s32[2,128]{1,0:T(2,128)S(1)} collective-permute-done((s32[2,128]{1,0:T(2,128)S(1)}, s32[2,128]{1,0:T(2,128)S(1)}, u32[]{:S(2)}, u32[]{:S(2)}) %collective-permute-start) | collective-permute-done | bytes 1056 | tf_op jit(solution)/shard_map/ppermute | solution.py:240
  51.3 0.0 collective-permute-done.1.refs_1_
  51.3 1.6 dispatch_scaled.2
  53.0 6.8 %all-to-all-start.1 = ((bf16[16,24,1024]{2,1,0:T(8,128)(2,1)}), bf16[16,24,1024]{2,1,0:T(8,128)(2,1)S(1)}, u32[]{:S(2)}, u32[]{:S(2)}) async-start(bf16[16,24,1024]{2,1,0:T(8,128)(2,1)} %bitcast.32), calls=%async_computation.1 | async-start | bytes 1572864 | tf_op jit(solution)/shard_map/all_to_all | solution.py:244
  59.8 1.0 slice_bitcast_fusion.1
  60.8 1.3 collective-permute-start.4
  62.1 2.8 %dispatch_tokens.1 = (bf16[384,2048]{1,0:T(8,128)(2,1)}, s32[2,128]{1,0:T(2,128)S(1)}) custom-call(s32[1]{0:T(128)} %bitcast.place_ref, s32[2,128]{1,0:T(2,128)} %bitcast.38, bf16[128,2048]{1,0:T(8,128)(2,1)} %tokens_ref.1), custom_call_target="tpu_custom_call" | custom-call | tf_op jit(solution)/shard_map/dispatch_tokens/pallas_call | solution.py:299
  64.9 4.2 %collective-permute-done.4.refs_3_ = bf16[192,768]{1,0:T(8,128)(2,1)S(1)} collective-permute-done((bf16[192,768]{1,0:T(8,128)(2,1)S(1)}, bf16[192,768]{1,0:T(8,128)(2,1)S(1)}, u32[]{:S(2)}, u32[]{:S(2)}) %collective-permute-start.4) | collective-permute-done | bytes 294944 | tf_op jit(solution)/shard_map/ppermute | solution.py:240
  69.1 9.9 %all-to-all-done.1 = bf16[16,24,1024]{2,1,0:T(8,128)(2,1)S(1)} async-done(((bf16[16,24,1024]{2,1,0:T(8,128)(2,1)}), bf16[16,24,1024]{2,1,0:T(8,128)(2,1)S(1)}, u32[]{:S(2)}, u32[]{:S(2)}) %all-to-all-start.1) | async-done | bytes 786464 | tf_op jit(solution)/shard_map/all_to_all | solution.py:244
  79.1 5.0 %all-to-all-start.2 = ((bf16[16,24,2048]{2,1,0:T(8,128)(2,1)}), bf16[16,24,2048]{2,1,0:T(8,128)(2,1)S(1)}, u32[]{:S(2)}, u32[]{:S(2)}) async-start(bf16[16,24,2048]{2,1,0:T(8,128)(2,1)} %bitcast.34), calls=%async_computation.2 | async-start | bytes 3145728 | tf_op jit(solution)/shard_map/all_to_all | solution.py:244
  84.0 1.4 slice_bitcast_fusion
  85.4 1.3 collective-permute-start.5
  86.7 5.1 %back.1 = (f32[384,768]{1,0:T(8,128)}, bf16[384,768]{1,0:T(8,128)(2,1)}, bf16[768,1024]{1,0:T(8,128)(2,1)}) custom-call(bf16[384,1024]{1,0:T(8,128)(2,1)S(1)} %bitcast.24, bf16[384,1024]{1,0:T(8,128)(2,1)S(1)} %bitcast.25, bf16[768,1024]{1,0:T(8,128)(2,1)} %bitcast.33), custom_call_target="tpu_custom_call" | custom-call | tf_op jit(solution)/shard_map/back/pallas_call | solution.py:325
  91.8 0.2 collective-permute-start.6
  92.0 22.8 %collective-permute-done.5.refs_4_ = bf16[832,768]{1,0:T(8,128)(2,1)} collective-permute-done((bf16[832,768]{1,0:T(8,128)(2,1)S(1)}, bf16[832,768]{1,0:T(8,128)(2,1)}, u32[]{:S(2)}, u32[]{:S(2)}) %collective-permute-start.5) | collective-permute-done | bytes 1277984 | tf_op jit(solution)/shard_map/ppermute | solution.py:240
  114.9 5.6 %all-to-all-done.2 = bf16[16,24,2048]{2,1,0:T(8,128)(2,1)S(1)} async-done(((bf16[16,24,2048]{2,1,0:T(8,128)(2,1)}), bf16[16,24,2048]{2,1,0:T(8,128)(2,1)S(1)}, u32[]{:S(2)}, u32[]{:S(2)}) %all-to-all-start.2) | async-done | bytes 1572896 | tf_op jit(solution)/shard_map/all_to_all | solution.py:244
  120.5 6.3 %forward.1 = (f32[384,768]{1,0:T(8,128)S(1)}, f32[384,768]{1,0:T(8,128)S(1)}, f32[384,768]{1,0:T(8,128)S(1)}, bf16[384,768]{1,0:T(8,128)(2,1)}, bf16[4,1024,768]...) custom-call(bf16[384,2048]{1,0:T(8,128)(2,1)S(1)} %bitcast.23, f32[384,768]{1,0:T(8,128)} %get-tuple-element.28.back_ref, ...), custom_call_target="tpu_custom_call" | custom-call | tf_op jit(solution)/shard_map/forward/pallas_call | solution.py:341
  126.8 0.6 collective-permute-done.6.refs_1_
  127.4 3.6 %backward.1 = bf16[384,2176]{1,0:T(8,128)(2,1)} custom-call(f32[384,768]{1,0:T(8,128)S(1)} %get-tuple-element.31.act_ref, f32[384,768]{1,0:T(8,128)S(1)} %get-tuple-element.32.slope_ref, f32[384,768]{1,0:T(8,128)S(1)} %get-tuple-element.33.value_ref, bf16[4,1024,768]{2,1,0:T(8,128)(2,1)S(1)} %get-tuple-element.34.held_ref, ...), custom_call_target="tpu_custom_call" | custom-call | tf_op jit(solution)/shard_map/backward/pallas_call | solution.py:361
  131.1 7.0 %all-to-all-start.3 = ((bf16[16,24,2176]{2,1,0:T(8,128)(2,1)}), bf16[16,24,2176]{2,1,0:T(8,128)(2,1)S(1)}, u32[]{:S(2)}, u32[]{:S(2)}) async-start(bf16[16,24,2176]{2,1,0:T(8,128)(2,1)} %bitcast.29), calls=%async_computation.3 | async-start | bytes 3342336 | tf_op jit(solution)/shard_map/all_to_all | solution.py:244
  138.1 1.3 collective-permute-start.7
  139.4 13.3 %collective-permute-done.7 = bf16[384,768]{1,0:T(8,128)(2,1)S(1)} collective-permute-done((bf16[384,768]{1,0:T(8,128)(2,1)S(1)}, bf16[384,768]{1,0:T(8,128)(2,1)S(1)}, u32[]{:S(2)}, u32[]{:S(2)}) %collective-permute-start.7) | collective-permute-done | bytes 589856 | tf_op jit(solution)/shard_map/ppermute | solution.py:240
  152.7 4.5 %convolution_bitcast_fusion = f32[1,768,1024]{2,1,0:T(8,128)} fusion(bf16[768,1024]{1,0:T(8,128)(2,1)} %get-tuple-element.40, bf16[384,768]{1,0:T(8,128)(2,1)S(1)} %collective-permute-done.7, bf16[384,768]{1,0:T(8,128)(2,1)S(1)} %copy-done.5), kind=kOutput, calls=%fused_computation | convolution fusion | flops 1210318848 | bytes 5898240 | tf_op jit(solution)/shard_map/dot_general | solution.py:21
  157.2 19.2 %all-to-all-done.3 = bf16[16,24,2176]{2,1,0:T(8,128)(2,1)S(1)} async-done(((bf16[16,24,2176]{2,1,0:T(8,128)(2,1)}), bf16[16,24,2176]{2,1,0:T(8,128)(2,1)S(1)}, u32[]{:S(2)}, u32[]{:S(2)}) %all-to-all-start.3) | async-done | bytes 1671200 | tf_op jit(solution)/shard_map/all_to_all | solution.py:244
  176.4 1.3 combine.1
  (15 shorter events, 0.1 us)
Async XLA Ops:
  0.6 9.2 %copy-start.2 = (bf16[128,2048]{1,0:T(8,128)(2,1)S(1)}, bf16[128,2048]{1,0:T(8,128)(2,1)}, u32[]{:S(2)}) copy-start(bf16[128,2048]{1,0:T(8,128)(2,1)} %refs_2_.1) | copy-start | bytes 1572868
  0.6 10.6 %copy-start.1 = (bf16[1,1024,768]{2,1,0:T(8,128)(2,1)S(1)}, bf16[1,1024,768]{2,1,0:T(8,128)(2,1)}, u32[]{:S(2)}) copy-start(bf16[1,1024,768]{2,1,0:T(8,128)(2,1)} %param.11) | copy-start | bytes 4718596
  0.7 10.8 %copy-start.4 = (s32[128,2]{0,1:T(2,128)S(1)}, s32[128,2]{0,1:T(2,128)}, u32[]{:S(2)}) copy-start(s32[128,2]{0,1:T(2,128)} %param.8) | copy-start | bytes 3076
  0.7 12.0 %copy-start = (f32[128,2]{0,1:T(2,128)S(1)}, f32[128,2]{0,1:T(2,128)}, u32[]{:S(2)}) copy-start(f32[128,2]{0,1:T(2,128)} %param.9) | copy-start | bytes 3076
  3.3 49.7 %all-to-all-start = ((bf16[16,24,1024]{2,1,0:T(8,128)(2,1)}), bf16[16,24,1024]{2,1,0:T(8,128)(2,1)S(1)}, u32[]{:S(2)}, u32[]{:S(2)}) async-start(bf16[16,24,1024]{2,1,0:T(8,128)(2,1)} %bitcast.31), calls=%async_computation | async-start | bytes 1572864 | tf_op jit(solution)/shard_map/all_to_all | solution.py:244
  9.9 41.4 %collective-permute-start.2 = (bf16[128,1024]{1,0:T(8,128)(2,1)S(1)}, bf16[128,1024]{1,0:T(8,128)(2,1)S(1)}, u32[]{:S(2)}, u32[]{:S(2)}) collective-permute-start(bf16[128,1024]{1,0:T(8,128)(2,1)S(1)} %constant_dynamic-slice_fusion), channel_id=1, source_target_pairs={{0,16},{16,0},{1,17},{17,1},{2,18},{18,2},{3,19},{19,3},{4,20},{20... | collective-permute-start | bytes 786440 | tf_op jit(solution)/shard_map/ppermute | solution.py:240
  11.2 57.9 %collective-permute-start.3 = (bf16[1024,768]{1,0:T(8,128)(2,1)S(1)}, bf16[1024,768]{1,0:T(8,128)(2,1)}, u32[]{:S(2)}, u32[]{:S(2)}) collective-permute-start(bf16[1024,768]{1,0:T(8,128)(2,1)S(1)} %bitcast.36), channel_id=1, source_target_pairs={{0,16},{16,0},{1,17},{17,1},{2,18},{18,2},{3,19},{19,3},{4,20},{20... | collective-permute-start | bytes 4718600 | tf_op jit(solution)/shard_map/ppermute | solution.py:240
  11.4 39.9 %collective-permute-start = (s32[2,128]{1,0:T(2,128)S(1)}, s32[2,128]{1,0:T(2,128)S(1)}, u32[]{:S(2)}, u32[]{:S(2)}) collective-permute-start(s32[2,128]{1,0:T(2,128)S(1)} %bitcast.39), channel_id=1, source_target_pairs={{0,16},{16,0},{1,17},{17,1},{2,18},{18,2},{3,19},{19,3},{4,20},{20... | collective-permute-start | bytes 3080 | tf_op jit(solution)/shard_map/ppermute | solution.py:240
  12.7 38.7 %collective-permute-start.1 = (f32[2,128]{1,0:T(2,128)S(1)}, f32[2,128]{1,0:T(2,128)S(1)}, u32[]{:S(2)}, u32[]{:S(2)}) collective-permute-start(f32[2,128]{1,0:T(2,128)S(1)} %bitcast.27), channel_id=1, source_target_pairs={{0,16},{16,0},{1,17},{17,1},{2,18},{18,2},{3,19},{19,3},{4,20},{20... | collective-permute-start | bytes 3080 | tf_op jit(solution)/shard_map/ppermute | solution.py:240
  53.0 26.1 %all-to-all-start.1 = ((bf16[16,24,1024]{2,1,0:T(8,128)(2,1)}), bf16[16,24,1024]{2,1,0:T(8,128)(2,1)S(1)}, u32[]{:S(2)}, u32[]{:S(2)}) async-start(bf16[16,24,1024]{2,1,0:T(8,128)(2,1)} %bitcast.32), calls=%async_computation.1 | async-start | bytes 1572864 | tf_op jit(solution)/shard_map/all_to_all | solution.py:244
  60.8 8.3 %collective-permute-start.4 = (bf16[192,768]{1,0:T(8,128)(2,1)S(1)}, bf16[192,768]{1,0:T(8,128)(2,1)S(1)}, u32[]{:S(2)}, u32[]{:S(2)}) collective-permute-start(bf16[192,768]{1,0:T(8,128)(2,1)S(1)} %slice_bitcast_fusion.1), channel_id=1, source_target_pairs={{0,16},{16,0},{1,17},{17,1},{2,18},{18,2},{3,19},{19,3},{4,20},{20... | collective-permute-start | bytes 884744 | tf_op jit(solution)/shard_map/ppermute | solution.py:240
  69.1 10.0 %copy-start.3 = (bf16[192,768]{1,0:T(8,128)(2,1)}, bf16[192,768]{1,0:T(8,128)(2,1)S(1)}, u32[]{:S(2)}) copy-start(bf16[192,768]{1,0:T(8,128)(2,1)S(1)} %collective-permute-done.4.refs_3_) | copy-start | bytes 884740
  79.1 41.4 %all-to-all-start.2 = ((bf16[16,24,2048]{2,1,0:T(8,128)(2,1)}), bf16[16,24,2048]{2,1,0:T(8,128)(2,1)S(1)}, u32[]{:S(2)}, u32[]{:S(2)}) async-start(bf16[16,24,2048]{2,1,0:T(8,128)(2,1)} %bitcast.34), calls=%async_computation.2 | async-start | bytes 3145728 | tf_op jit(solution)/shard_map/all_to_all | solution.py:244
  85.4 29.5 %collective-permute-start.5 = (bf16[832,768]{1,0:T(8,128)(2,1)S(1)}, bf16[832,768]{1,0:T(8,128)(2,1)}, u32[]{:S(2)}, u32[]{:S(2)}) collective-permute-start(bf16[832,768]{1,0:T(8,128)(2,1)S(1)} %slice_bitcast_fusion), channel_id=1, source_target_pairs={{0,16},{16,0},{1,17},{17,1},{2,18},{18,2},{3,19},{19,3},{4,20},{20... | collective-permute-start | bytes 3833864 | tf_op jit(solution)/shard_map/ppermute | solution.py:240
  91.8 35.6 %collective-permute-start.6 = (bf16[384,768]{1,0:T(8,128)(2,1)}, bf16[384,768]{1,0:T(8,128)(2,1)S(1)}, u32[]{:S(2)}, u32[]{:S(2)}) collective-permute-start(bf16[384,768]{1,0:T(8,128)(2,1)} %get-tuple-element.36), channel_id=1, source_target_pairs={{0,16},{16,0},{1,17},{17,1},{2,18},{18,2},{3,19},{19,3},{4,20},{20... | collective-permute-start | bytes 1769480 | tf_op jit(solution)/shard_map/ppermute | solution.py:240
  131.1 7.0 %copy-start.5 = (bf16[384,768]{1,0:T(8,128)(2,1)S(1)}, bf16[384,768]{1,0:T(8,128)(2,1)}, u32[]{:S(2)}) copy-start(bf16[384,768]{1,0:T(8,128)(2,1)} %get-tuple-element.39) | copy-start | bytes 1769476
  131.1 45.3 %all-to-all-start.3 = ((bf16[16,24,2176]{2,1,0:T(8,128)(2,1)}), bf16[16,24,2176]{2,1,0:T(8,128)(2,1)S(1)}, u32[]{:S(2)}, u32[]{:S(2)}) async-start(bf16[16,24,2176]{2,1,0:T(8,128)(2,1)} %bitcast.29), calls=%async_computation.3 | async-start | bytes 3342336 | tf_op jit(solution)/shard_map/all_to_all | solution.py:244
  138.1 14.6 %collective-permute-start.7 = (bf16[384,768]{1,0:T(8,128)(2,1)S(1)}, bf16[384,768]{1,0:T(8,128)(2,1)S(1)}, u32[]{:S(2)}, u32[]{:S(2)}) collective-permute-start(bf16[384,768]{1,0:T(8,128)(2,1)S(1)} %copy-done.5), channel_id=1, source_target_pairs={{0,16},{16,0},{1,17},{17,1},{2,18},{18,2},{3,19},{19,3},{4,20},{20... | collective-permute-start | bytes 1769480 | tf_op jit(solution)/shard_map/ppermute | solution.py:240

commit v4 on v2

--- a/solution.py
+++ b/solution.py
@@ -9,6 +9,7 @@
 
 LANES = 128
 VMEM_BYTES = 24 * 1024 * 1024
+BACK_COST_US = 30
 
 
 def contract_last(left, right):
@@ -110,53 +111,53 @@
             ref[:, cols] = part.astype(ref.dtype)
 
 
-def forward_kernel(groups, x_ref, *refs):
+def forward_kernel(groups, x_ref, back_ref, *refs):
     (own_gate, own_up), others = refs[:2], refs[2 : groups + 1]
-    act_ref, slope_ref, value_ref, hidden_ref, held_ref = refs[groups + 1 : groups + 6]
-    rows_ref, gate_sum_ref, up_sum_ref, sems, row_sems = refs[groups + 6 :]
+    act_ref, slope_ref, value_ref, hidden_ref, held_ref, kept_ref = refs[groups + 1 : groups + 7]
+    gate_sum_ref, up_sum_ref, sems, back_sem = refs[groups + 7 :]
     share, hidden = held_ref.shape[1:]
     step = tile_of(hidden, 384)
     gates = [own_gate, *[ref.at[:share] for ref in others]]
     ups = [own_up, *[ref.at[share:] for ref in others]]
-
-    def load(ref, i):
-        return pltpu.make_async_copy(ref, held_ref.at[i], sems.at[i])
-
-    def columns(k):
-        return slice(k * share, (k + 1) * share)
-
-    stages = []
+    spans = [slice(at, at + step) for at in range(0, hidden, step)]
+
+    loads = []
     for k in range(groups):
-        cols = columns(k)
-        rows = pltpu.make_async_copy(x_ref.at[:, cols], rows_ref.at[:, cols], row_sems.at[k])
-        stages.append([rows, load(gates[k], k)])
-        stages.append([load(ups[k], groups + k)])
-
-    def start(n):
-        for copy in stages[n] if n < len(stages) else ():
-            copy.start()
-
-    def finish(n):
-        for copy in stages[n]:
-            copy.wait()
-
-    start(0)
-    start(1)
+        for ref, i in ((gates[k], k), (ups[k], groups + k)):
+            for n, cols in enumerate(spans):
+                loads.append(
+                    pltpu.make_async_copy(
+                        ref.at[:, cols], held_ref.at[i, :, cols], sems.at[n, i]
+                    )
+                )
+    loads.append(pltpu.make_async_copy(back_ref, kept_ref, back_sem.at[0]))
+    flying = 3
+    for copy in loads[:flying]:
+        copy.start()
+    place = 0
+
+    def arrived():
+        nonlocal place
+        loads[place].wait()
+        if place + flying < len(loads):
+            loads[place + flying].start()
+        place += 1
+
+    def against(k, i, cols):
+        return jnp.dot(
+            x_ref[:, k * share : (k + 1) * share],
+            held_ref[i, :, cols],
+            preferred_element_type=jnp.float32,
+        )
+
     for k in range(groups):
-        x = rows_ref.at[:, columns(k)]
-        finish(2 * k)
-        start(2 * k + 2)
-        for at in range(0, hidden, step):
-            cols = slice(at, at + step)
-            part = jnp.dot(x[...], held_ref[k, :, cols], preferred_element_type=jnp.float32)
+        for cols in spans:
+            arrived()
+            part = against(k, k, cols)
             gate_sum_ref[:, cols] = part if k == 0 else gate_sum_ref[:, cols] + part
-        finish(2 * k + 1)
-        start(2 * k + 3)
-        for at in range(0, hidden, step):
-            cols = slice(at, at + step)
-            pre_up = jnp.dot(
-                x[...], held_ref[groups + k, :, cols], preferred_element_type=jnp.float32
-            )
+        for cols in spans:
+            arrived()
+            pre_up = against(k, groups + k, cols)
             if k > 0:
                 pre_up += up_sum_ref[:, cols]
             if k < groups - 1:
@@ -170,6 +171,7 @@
             slope_ref[:, cols] = pre_up * (sig * (1.0 + pre_gate * (1.0 - sig)))
             value_ref[:, cols] = hidden_f
             hidden_ref[:, cols] = hidden_f.astype(hidden_ref.dtype)
+    arrived()
 
 
 def backward_kernel(groups, act_ref, slope_ref, value_ref, held_ref, *refs):
@@ -256,7 +258,8 @@
     ]
     both = jnp.concatenate([w_gate[0], w_up[0]], axis=0)
     both, gates_own = lax.optimization_barrier((both, gates_t))
-    weights = [w_gate[0], w_up[0]] + [shifted(both, k) for k in range(1, groups)]
+    both, grads = lax.optimization_barrier((both, grads))
+    weights_moved = [shifted(both, k) for k in range(1, groups)]
 
     def in_hbm(value):
         return pltpu.with_memory_space_constraint(value, pltpu.HBM)
@@ -307,37 +310,43 @@
     )(place, in_hbm(routes_t), in_hbm(tokens))
     x_rows = exchanged(sent)
 
+    scaled_rows, weights_moved = lax.optimization_barrier((scaled_rows, weights_moved))
+    weights = [w_gate[0], w_up[0], *weights_moved]
+
     back_own, *rest = pl.pallas_call(
         functools.partial(back_kernel, groups, cap),
         out_shape=[pltpu.HBM((slots, hidden), jnp.float32)]
         + [pltpu.HBM((slots, hidden), jnp.bfloat16)] * (groups - 1)
         + [pltpu.HBM((groups * slots, share), jnp.bfloat16)],
+        cost_estimate=pl.CostEstimate(
+            flops=BACK_COST_US * 10**9, bytes_accessed=BACK_COST_US * 10**6, transcendentals=0
+        ),
         compiler_params=params,
         name="back",
     )(scaled_rows, in_hbm(w_down[0]))
     scaled_all = rest[-1]
-    back_parts = [back_own] + [shifted(rest[k - 1], -k) for k in range(1, groups)]
+    back_parts = [shifted(rest[k - 1], -k) for k in range(1, groups)]
 
     whole_spec = pl.BlockSpec(memory_space=pltpu.VMEM)
     any_spec = pl.BlockSpec(memory_space=pl.ANY)
-    *factors, hidden_own, held = pl.pallas_call(
+    *factors, hidden_own, held, back_kept = pl.pallas_call(
         functools.partial(forward_kernel, groups),
         out_shape=[pltpu.VMEM((slots, hidden), jnp.float32)] * 3
         + [
             pltpu.HBM((slots, hidden), jnp.bfloat16),
             pltpu.VMEM((2 * groups, share, hidden), jnp.bfloat16),
+            pltpu.VMEM((slots, hidden), jnp.float32),
         ],
-        in_specs=[any_spec] * (groups + 2),
+        in_specs=[whole_spec] + [any_spec] * (groups + 2),
         scratch_shapes=[
-            pltpu.VMEM((slots, width), jnp.bfloat16),
             pltpu.VMEM((slots, hidden), jnp.float32),
             pltpu.VMEM((slots, hidden), jnp.float32),
-            pltpu.SemaphoreType.DMA((2 * groups,)),
-            pltpu.SemaphoreType.DMA((groups,)),
+            pltpu.SemaphoreType.DMA((hidden // tile_of(hidden, 384), 2 * groups)),
+            pltpu.SemaphoreType.DMA((1,)),
         ],
         compiler_params=params,
         name="forward",
-    )(in_hbm(x_rows), *[in_hbm(value) for value in weights])
+    )(x_rows, in_hbm(back_own), *[in_hbm(value) for value in weights])
 
     pieces = groups * (share // tile_of(share, 512))
     returning = pl.pallas_call(
@@ -353,7 +362,7 @@
         ],
         compiler_params=params,
         name="backward",
-    )(*factors, held, *back_parts)
+    )(*factors, held, back_kept, *back_parts)
     returned = exchanged(returning)
 
     hiddens = [hidden_own] + [shifted(hidden_own, k) for k in range(1, groups)]

time: 155 us -> 221 us (1.43)
  waiting for transfers between devices: 97.2 us -> 164 us
    ppermute x6, waiting for transfers between devices: 15.1 us -> 81.2 us  [shifted(): lax.ppermute(value, 'dp', [(i, (i + by) % groups) for i in range(groups)])]
  transfers between devices with their start and end apart: 9 -> 9, of which waited for: 5 -> 6; matrix products, arithmetic and copies ran while one was open for 6% -> 4% of each run, Pallas kernels for 9% -> 8%
where the time goes in v4:
time: 221 us
  waiting for transfers between devices  164 us (74%)
  starting transfers between devices  24.9 us (11%)
  Pallas kernels  22.5 us (10%)
  matrix products  4.52 us (2%)
  other arithmetic  3.77 us (2%)
    all_to_all x3, waiting for transfers between devices, exchanged(): lax.all_to_all(split, 'expert', split_axis=0, concat_axis=0, tiled=True)  82.4 us
    ppermute x6, waiting for transfers between devices, shifted(): lax.ppermute(value, 'dp', [(i, (i + by) % groups) for i in range(groups)])  81.2 us
    all_to_all x3, starting transfers between devices, exchanged(): lax.all_to_all(split, 'expert', split_axis=0, concat_axis=0, tiled=True)  18.3 us
    ppermute x6, starting transfers between devices, shifted(): lax.ppermute(value, 'dp', [(i, (i + by) % groups) for i in range(groups)])  6.56 us
    pallas_call x1, Pallas kernels, per_device(): pl.pallas_call(functools.partial(forward_kernel, groups), out_shape=[pltp...  6.55 us
    pallas_call x1, Pallas kernels, per_device(): pl.pallas_call(functools.partial(back_kernel, groups, cap), out_shape=[pl...  5.07 us
    dot_general x1, matrix products, contract_first(): lax.dot_general(left, right, (((0,), (0,)), ((), ())), preferred_element_...  4.52 us
  transfers between devices with their start and end apart: 9, of which 6 were waited for; matrix products, arithmetic and copies ran while one was open for 4% of the time, Pallas kernels for 8%

profile of v4, /device:TPU:11, one launch (start us, length us, event | category | flops | bytes accessed | tf_op | source)
XLA Modules:
  0.0 220.8 jit_solution(14783568312752073736)
XLA Ops:
  0.6 1.0 constant_dynamic-slice_fusion
  1.6 1.3 collective-permute-start.2
  2.9 3.8 %pad_maximum_fusion = bf16[2048,768]{1,0:T(8,128)(2,1)} fusion(bf16[1024,768]{1,0:T(8,128)(2,1)} %bitcast.26, bf16[1024,768]{1,0:T(8,128)(2,1)} %bitcast.24), kind=kLoop, calls=%fused_computation | loop fusion | flops 6291456 | bytes 6291456 | tf_op jit(solution)/shard_map/concatenate | solution.py:259
  6.7 2.2 collective-permute-done.2.refs_5_
  8.9 1.2 collective-permute-start.3
  10.1 0.0 copy-done.2
  10.1 0.2 collective-permute-start
  10.3 0.0 copy-done
  10.3 1.2 collective-permute-start.1
  11.6 65.7 %collective-permute-done.refs_1_ = s32[2,128]{1,0:T(2,128)S(1)} collective-permute-done((s32[2,128]{1,0:T(2,128)S(1)}, s32[2,128]{1,0:T(2,128)S(1)}, u32[]{:S(2)}, u32[]{:S(2)}) %collective-permute-start) | collective-permute-done | bytes 1056 | tf_op jit(solution)/shard_map/ppermute | solution.py:243
  77.2 0.0 collective-permute-done.1.refs_3_
  77.3 3.1 %dispatch_scaled.1 = bf16[768,1024]{1,0:T(8,128)(2,1)} custom-call(s32[1]{0:T(128)} %bitcast.place_ref, s32[2,128]{1,0:T(2,128)} %bitcast.29, s32[2,128]{1,0:T(2,128)S(1)} %collective-permute-done.refs_1_, f32[2,128]{1,0:T(2,128)} %bitcast.19, f32[2,128]{1,0:T(2,128)S(1)} %collective-permute-done.1.refs_3_, bf16[128,2048]{1,0:T(8,128)(2,1)} %refs_4_.1, ...), custom_call_target="tpu_custom_call" | custom-call | tf_op jit(solution)/shard_map/dispatch_scaled/pallas_call | solution.py:270
  80.4 8.3 %all-to-all-start.1 = ((bf16[16,48,1024]{2,1,0:T(8,128)(2,1)}), bf16[16,48,1024]{2,1,0:T(8,128)(2,1)S(1)}, u32[]{:S(2)}, u32[]{:S(2)}) async-start(bf16[16,48,1024]{2,1,0:T(8,128)(2,1)} %bitcast.23), calls=%async_computation.1 | async-start | bytes 3145728 | tf_op jit(solution)/shard_map/all_to_all | solution.py:247
  88.7 2.8 %dispatch_tokens.1 = (bf16[384,2048]{1,0:T(8,128)(2,1)}, s32[2,128]{1,0:T(2,128)S(1)}) custom-call(s32[1]{0:T(128)} %bitcast.place_ref, s32[2,128]{1,0:T(2,128)} %bitcast.30, bf16[128,2048]{1,0:T(8,128)(2,1)} %tokens_ref.1), custom_call_target="tpu_custom_call" | custom-call | tf_op jit(solution)/shard_map/dispatch_tokens/pallas_call | solution.py:290
  91.6 33.4 %all-to-all-done.1 = bf16[16,48,1024]{2,1,0:T(8,128)(2,1)S(1)} async-done(((bf16[16,48,1024]{2,1,0:T(8,128)(2,1)}), bf16[16,48,1024]{2,1,0:T(8,128)(2,1)S(1)}, u32[]{:S(2)}, u32[]{:S(2)}) %all-to-all-start.1) | async-done | bytes 1572896 | tf_op jit(solution)/shard_map/all_to_all | solution.py:247
  124.9 4.9 %all-to-all-start = ((bf16[16,24,2048]{2,1,0:T(8,128)(2,1)}), bf16[16,24,2048]{2,1,0:T(8,128)(2,1)S(1)}, u32[]{:S(2)}, u32[]{:S(2)}) async-start(bf16[16,24,2048]{2,1,0:T(8,128)(2,1)} %bitcast.28), calls=%async_computation | async-start | bytes 3145728 | tf_op jit(solution)/shard_map/all_to_all | solution.py:247
  129.8 0.0 collective-permute-done.3.refs_2_
  129.8 5.1 %back.1 = (f32[384,768]{1,0:T(8,128)}, bf16[384,768]{1,0:T(8,128)(2,1)}, bf16[768,1024]{1,0:T(8,128)(2,1)}) custom-call(bf16[768,1024]{1,0:T(8,128)(2,1)S(1)} %bitcast.18, bf16[768,1024]{1,0:T(8,128)(2,1)} %bitcast.32), custom_call_target="tpu_custom_call" | custom-call | flops 30000001024 | bytes 30000000 | tf_op jit(solution)/shard_map/back/pallas_call | solution.py:316
  134.9 1.2 collective-permute-start.4
  136.1 29.9 %all-to-all-done = bf16[16,24,2048]{2,1,0:T(8,128)(2,1)S(1)} async-done(((bf16[16,24,2048]{2,1,0:T(8,128)(2,1)}), bf16[16,24,2048]{2,1,0:T(8,128)(2,1)S(1)}, u32[]{:S(2)}, u32[]{:S(2)}) %all-to-all-start) | async-done | bytes 1572896 | tf_op jit(solution)/shard_map/all_to_all | solution.py:247
  166.0 6.5 %forward.1 = (f32[384,768]{1,0:T(8,128)S(1)}, f32[384,768]{1,0:T(8,128)S(1)}, f32[384,768]{1,0:T(8,128)S(1)}, bf16[384,768]{1,0:T(8,128)(2,1)}, bf16[4,1024,768]...) custom-call(bf16[384,2048]{1,0:T(8,128)(2,1)S(1)} %bitcast.17, f32[384,768]{1,0:T(8,128)} %get-tuple-element.29.back_ref, ...), custom_call_target="tpu_custom_call" | custom-call | tf_op jit(solution)/shard_map/forward/pallas_call | solution.py:332
  172.6 0.0 collective-permute-done.4.refs_1_
  172.6 3.6 %backward.1 = bf16[384,2176]{1,0:T(8,128)(2,1)} custom-call(f32[384,768]{1,0:T(8,128)S(1)} %get-tuple-element.31.act_ref, f32[384,768]{1,0:T(8,128)S(1)} %get-tuple-element.32.slope_ref, f32[384,768]{1,0:T(8,128)S(1)} %get-tuple-element.33.value_ref, bf16[4,1024,768]{2,1,0:T(8,128)(2,1)S(1)} %get-tuple-element.34.held_ref, ...), custom_call_target="tpu_custom_call" | custom-call | tf_op jit(solution)/shard_map/backward/pallas_call | solution.py:352
  176.2 0.0 copy-start.3
  176.2 5.1 %all-to-all-start.2 = ((bf16[16,24,2176]{2,1,0:T(8,128)(2,1)}), bf16[16,24,2176]{2,1,0:T(8,128)(2,1)S(1)}, u32[]{:S(2)}, u32[]{:S(2)}) async-start(bf16[16,24,2176]{2,1,0:T(8,128)(2,1)} %bitcast.22), calls=%async_computation.2 | async-start | bytes 3342336 | tf_op jit(solution)/shard_map/all_to_all | solution.py:247
  181.2 0.0 copy-done.3
  181.2 1.3 collective-permute-start.5
  182.5 13.3 %collective-permute-done.5 = bf16[384,768]{1,0:T(8,128)(2,1)S(1)} collective-permute-done((bf16[384,768]{1,0:T(8,128)(2,1)S(1)}, bf16[384,768]{1,0:T(8,128)(2,1)S(1)}, u32[]{:S(2)}, u32[]{:S(2)}) %collective-permute-start.5) | collective-permute-done | bytes 589856 | tf_op jit(solution)/shard_map/ppermute | solution.py:243
  195.9 4.5 %convolution_bitcast_fusion = f32[1,768,1024]{2,1,0:T(8,128)} fusion(bf16[768,1024]{1,0:T(8,128)(2,1)} %get-tuple-element.40, bf16[384,768]{1,0:T(8,128)(2,1)S(1)} %collective-permute-done.5, bf16[384,768]{1,0:T(8,128)(2,1)S(1)} %copy-done.3), kind=kOutput, calls=%fused_computation.1 | convolution fusion | flops 1210318848 | bytes 5898240 | tf_op jit(solution)/shard_map/dot_general | solution.py:22
  200.4 19.1 %all-to-all-done.2 = bf16[16,24,2176]{2,1,0:T(8,128)(2,1)S(1)} async-done(((bf16[16,24,2176]{2,1,0:T(8,128)(2,1)}), bf16[16,24,2176]{2,1,0:T(8,128)(2,1)S(1)}, u32[]{:S(2)}, u32[]{:S(2)}) %all-to-all-start.2) | async-done | bytes 1671200 | tf_op jit(solution)/shard_map/all_to_all | solution.py:247
  219.5 0.0 copy-done.1
  219.5 1.3 combine.1
  (3 shorter events, 0.0 us)
Async XLA Ops:
  1.6 7.2 %collective-permute-start.2 = (bf16[128,1024]{1,0:T(8,128)(2,1)S(1)}, bf16[128,1024]{1,0:T(8,128)(2,1)S(1)}, u32[]{:S(2)}, u32[]{:S(2)}) collective-permute-start(bf16[128,1024]{1,0:T(8,128)(2,1)S(1)} %constant_dynamic-slice_fusion), channel_id=1, source_target_pairs={{0,16},{16,0},{1,17},{17,1},{2,18},{18,2},{3,19},{19,3},{4,20},{20... | collective-permute-start | bytes 786440 | tf_op jit(solution)/shard_map/ppermute | solution.py:243
  2.9 7.2 %copy-start.2 = (s32[128,2]{0,1:T(2,128)S(1)}, s32[128,2]{0,1:T(2,128)}, u32[]{:S(2)}) copy-start(s32[128,2]{0,1:T(2,128)} %param.8) | copy-start | bytes 3076
  2.9 7.4 %copy-start = (f32[128,2]{0,1:T(2,128)S(1)}, f32[128,2]{0,1:T(2,128)}, u32[]{:S(2)}) copy-start(f32[128,2]{0,1:T(2,128)} %param.9) | copy-start | bytes 3076
  8.9 121.0 %collective-permute-start.3 = (bf16[2048,768]{1,0:T(8,128)(2,1)}, bf16[2048,768]{1,0:T(8,128)(2,1)}, u32[]{:S(2)}, u32[]{:S(2)}) collective-permute-start(bf16[2048,768]{1,0:T(8,128)(2,1)} %pad_maximum_fusion), channel_id=1, source_target_pairs={{0,16},{16,0},{1,17},{17,1},{2,18},{18,2},{3,19},{19,3},{4,20},{20... | collective-permute-start | bytes 9437192 | tf_op jit(solution)/shard_map/ppermute | solution.py:243
  10.1 67.1 %collective-permute-start = (s32[2,128]{1,0:T(2,128)S(1)}, s32[2,128]{1,0:T(2,128)S(1)}, u32[]{:S(2)}, u32[]{:S(2)}) collective-permute-start(s32[2,128]{1,0:T(2,128)S(1)} %bitcast.31), channel_id=1, source_target_pairs={{0,16},{16,0},{1,17},{17,1},{2,18},{18,2},{3,19},{19,3},{4,20},{20... | collective-permute-start | bytes 3080 | tf_op jit(solution)/shard_map/ppermute | solution.py:243
  10.3 66.9 %collective-permute-start.1 = (f32[2,128]{1,0:T(2,128)S(1)}, f32[2,128]{1,0:T(2,128)S(1)}, u32[]{:S(2)}, u32[]{:S(2)}) collective-permute-start(f32[2,128]{1,0:T(2,128)S(1)} %bitcast.20), channel_id=1, source_target_pairs={{0,16},{16,0},{1,17},{17,1},{2,18},{18,2},{3,19},{19,3},{4,20},{20... | collective-permute-start | bytes 3080 | tf_op jit(solution)/shard_map/ppermute | solution.py:243
  80.4 44.5 %all-to-all-start.1 = ((bf16[16,48,1024]{2,1,0:T(8,128)(2,1)}), bf16[16,48,1024]{2,1,0:T(8,128)(2,1)S(1)}, u32[]{:S(2)}, u32[]{:S(2)}) async-start(bf16[16,48,1024]{2,1,0:T(8,128)(2,1)} %bitcast.23), calls=%async_computation.1 | async-start | bytes 3145728 | tf_op jit(solution)/shard_map/all_to_all | solution.py:247
  124.9 41.1 %all-to-all-start = ((bf16[16,24,2048]{2,1,0:T(8,128)(2,1)}), bf16[16,24,2048]{2,1,0:T(8,128)(2,1)S(1)}, u32[]{:S(2)}, u32[]{:S(2)}) async-start(bf16[16,24,2048]{2,1,0:T(8,128)(2,1)} %bitcast.28), calls=%async_computation | async-start | bytes 3145728 | tf_op jit(solution)/shard_map/all_to_all | solution.py:247
  134.9 37.7 %collective-permute-start.4 = (bf16[384,768]{1,0:T(8,128)(2,1)}, bf16[384,768]{1,0:T(8,128)(2,1)S(1)}, u32[]{:S(2)}, u32[]{:S(2)}) collective-permute-start(bf16[384,768]{1,0:T(8,128)(2,1)} %get-tuple-element.36), channel_id=1, source_target_pairs={{0,16},{16,0},{1,17},{17,1},{2,18},{18,2},{3,19},{19,3},{4,20},{20... | collective-permute-start | bytes 1769480 | tf_op jit(solution)/shard_map/ppermute | solution.py:243
  176.2 5.1 %copy-start.3 = (bf16[384,768]{1,0:T(8,128)(2,1)S(1)}, bf16[384,768]{1,0:T(8,128)(2,1)}, u32[]{:S(2)}) copy-start(bf16[384,768]{1,0:T(8,128)(2,1)} %get-tuple-element.39) | copy-start | bytes 1769476
  176.2 43.3 %all-to-all-start.2 = ((bf16[16,24,2176]{2,1,0:T(8,128)(2,1)}), bf16[16,24,2176]{2,1,0:T(8,128)(2,1)S(1)}, u32[]{:S(2)}, u32[]{:S(2)}) async-start(bf16[16,24,2176]{2,1,0:T(8,128)(2,1)} %bitcast.22), calls=%async_computation.2 | async-start | bytes 3342336 | tf_op jit(solution)/shard_map/all_to_all | solution.py:247
  181.2 14.6 %collective-permute-start.5 = (bf16[384,768]{1,0:T(8,128)(2,1)S(1)}, bf16[384,768]{1,0:T(8,128)(2,1)S(1)}, u32[]{:S(2)}, u32[]{:S(2)}) collective-permute-start(bf16[384,768]{1,0:T(8,128)(2,1)S(1)} %copy-done.3), channel_id=1, source_target_pairs={{0,16},{16,0},{1,17},{17,1},{2,18},{18,2},{3,19},{19,3},{4,20},{20... | collective-permute-start | bytes 1769480 | tf_op jit(solution)/shard_map/ppermute | solution.py:243
  195.8 23.7 %copy-start.1 = (f32[128,2]{0,1:T(2,128)S(1)}, f32[128,2]{0,1:T(2,128)}, u32[]{:S(2)}) copy-start(f32[128,2]{0,1:T(2,128)} %param.9) | copy-start | bytes 3076

commit v5 on v4

--- a/solution.py
+++ b/solution.py
@@ -48,24 +48,38 @@
     ]
 
 
-def rows_of(ref, groups, cap, which):
-    value = ref[...].astype(jnp.float32)
+def by_half(value, cap, half, paired):
     count, width = value.shape
-    value = value.reshape(count // (groups * cap), groups, cap, width)[:, which]
-    return value.reshape(count // groups, width).astype(ref.dtype)
-
-
-def dispatch_tokens(experts, cap, place_ref, routes_ref, tokens_ref, out_ref, pos_ref, pick_ref):
+    if paired:
+        value = value.reshape(count // (2 * cap), 2, cap, width)
+        own, other = value[:, 0], value[:, 1]
+    else:
+        value = value.reshape(2, count // (2 * cap), cap, width)
+        own, other = value[0], value[1]
+    first = jnp.where(half == 0, own, other)
+    second = jnp.where(half == 0, other, own)
+    return jnp.stack([first, second], axis=0 if paired else 1).reshape(count, width)
+
+
+def dispatch_tokens(experts, cap, place_ref, *refs):
+    routes_refs, tokens_refs, (out_ref, pos_ref, pick_ref) = refs[:2], refs[2:4], refs[4:]
+    count = tokens_refs[0].shape[0]
+
     @pl.when(pl.program_id(0) == 0)
     def _():
-        pos = slot_positions(routes_ref[...], experts, cap, 0)
-        rows = lax.broadcasted_iota(jnp.int32, pick_ref.shape, 0)
-        pick_ref[...] = sum(jnp.where(rows == p, 1.0, 0.0) for p in pos).astype(jnp.bfloat16)
-        for k, p in enumerate(pos):
+        rows = lax.broadcasted_iota(jnp.int32, (pick_ref.shape[0], count), 0)
+        for c, ref in enumerate(routes_refs):
+            near = ref[...] - place_ref[1] * (experts // 2)
+            pos = slot_positions(near, experts // 2, 2 * cap, c * cap)
+            pick_ref[:, c * count : (c + 1) * count] = sum(
+                jnp.where(rows == p, 1.0, 0.0) for p in pos
+            ).astype(jnp.bfloat16)
+        for k, p in enumerate(slot_positions(routes_refs[0][...], experts, cap, 0)):
             pos_ref[k : k + 1, :] = p
 
+    values = jnp.concatenate([ref[...] for ref in tokens_refs], axis=0)
     out_ref[...] = jnp.dot(
-        pick_ref[...], tokens_ref[...], preferred_element_type=jnp.float32
+        pick_ref[...], values, preferred_element_type=jnp.float32
     ).astype(out_ref.dtype)
 
 
@@ -96,11 +110,14 @@
     out_ref[...] = (scale_ref[:, :1] * rows).astype(out_ref.dtype)
 
 
-def back_kernel(groups, cap, rows_ref, down_ref, own_ref, *rest):
+def back_kernel(groups, cap, place_ref, rows_ref, down_ref, own_ref, *rest):
     others, all_ref = rest[: groups - 1], rest[groups - 1]
     slots, hidden = own_ref.shape
+    count, share = rows_ref.shape
+    rows = rows_ref[...].astype(jnp.float32).reshape(count // (groups * cap), groups, cap, share)
     for q in range(groups):
-        all_ref[q * slots : (q + 1) * slots, :] = rows_of(rows_ref, groups, cap, q)
+        ordered = by_half(rows[:, q].reshape(slots, share), cap, place_ref[1], False)
+        all_ref[q * slots : (q + 1) * slots, :] = ordered.astype(all_ref.dtype)
     step = tile_of(hidden, 256)
 
     @pl.loop(0, hidden // step)
@@ -174,16 +191,18 @@
     arrived()
 
 
-def backward_kernel(groups, act_ref, slope_ref, value_ref, held_ref, *refs):
+def backward_kernel(groups, cap, place_ref, act_ref, slope_ref, value_ref, held_ref, *refs):
     parts, (out_ref, d_gate_ref, d_up_ref, rows_ref, out_sems) = refs[:groups], refs[groups:]
     share = held_ref.shape[1]
     width = groups * share
     block = tile_of(share, 512)
+    half = place_ref[1]
     back = sum(part[...].astype(jnp.float32) for part in parts)
     score = jnp.sum(back * value_ref[...], axis=1, keepdims=True)
-    d_gate_ref[...] = (back * slope_ref[...]).astype(jnp.bfloat16)
-    d_up_ref[...] = (back * act_ref[...]).astype(jnp.bfloat16)
-    rows_ref[:, width:] = jnp.broadcast_to(score, (score.shape[0], LANES)).astype(rows_ref.dtype)
+    d_gate_ref[...] = by_half(back * slope_ref[...], cap, half, True).astype(jnp.bfloat16)
+    d_up_ref[...] = by_half(back * act_ref[...], cap, half, True).astype(jnp.bfloat16)
+    score = by_half(jnp.broadcast_to(score, (score.shape[0], LANES)), cap, half, True)
+    rows_ref[:, width:] = score.astype(rows_ref.dtype)
     outs = []
 
     def send(cols):
@@ -237,14 +256,23 @@
     share = width // groups
     hidden = w_gate.shape[2]
     params = pltpu.CompilerParams(vmem_limit_bytes=VMEM_BYTES)
-    place = group.astype(jnp.int32).reshape(1)
+    half = lax.div(lax.axis_index("expert"), experts // 2)
+    place = jnp.stack([group, half]).astype(jnp.int32)
+    halves = [list(range(experts // 2)), list(range(experts // 2, experts))]
 
     def shifted(value, by):
         return lax.ppermute(value, "dp", [(i, (i + by) % groups) for i in range(groups)])
 
-    def exchanged(rows):
-        split = rows.reshape(experts, rows.shape[0] // experts, rows.shape[1])
-        moved = lax.all_to_all(split, "expert", split_axis=0, concat_axis=0, tiled=True)
+    def across(value):
+        pairs = [(i, (i + experts // 2) % experts) for i in range(experts)]
+        return lax.ppermute(value, "expert", pairs)
+
+    def exchanged(rows, among=None):
+        count = experts if among is None else len(among[0])
+        split = rows.reshape(count, rows.shape[0] // count, rows.shape[1])
+        moved = lax.all_to_all(
+            split, "expert", split_axis=0, concat_axis=0, axis_index_groups=among, tiled=True
+        )
         return moved.reshape(rows.shape)
 
     routes_t, gates_t = jnp.transpose(routes), jnp.transpose(gates)
@@ -258,7 +286,10 @@
     ]
     both = jnp.concatenate([w_gate[0], w_up[0]], axis=0)
     both, gates_own = lax.optimization_barrier((both, gates_t))
-    both, grads = lax.optimization_barrier((both, grads))
+    both, grads, routes_all, gates_all = lax.optimization_barrier(
+        (both, grads, routes_all, gates_all)
+    )
+    tokens_across, routes_across = across(tokens), across(routes_t)
     weights_moved = [shifted(both, k) for k in range(1, groups)]
 
     def in_hbm(value):
@@ -285,6 +316,9 @@
         compiler_params=params,
         name="dispatch_scaled",
     )(place, in_hbm(routes_t), *routes_all[1:], in_hbm(gates_own), *gates_all[1:], in_hbm(grad_out), *grads)
+    scaled, tokens_across, routes_across = lax.optimization_barrier(
+        (scaled, tokens_across, routes_across)
+    )
     scaled_rows = exchanged(scaled)
 
     sent, pos = pl.pallas_call(
@@ -296,34 +330,38 @@
         grid_spec=pltpu.PrefetchScalarGridSpec(
             num_scalar_prefetch=1,
             grid=(groups,),
-            in_specs=[
-                small_spec,
+            in_specs=[small_spec] * 2
+            + [
                 pl.BlockSpec(
                     (count, share), lambda k, g: (0, lax.rem(g[0] - k + groups, groups))
-                ),
-            ],
+                )
+            ]
+            * 2,
             out_specs=(pl.BlockSpec((slots, share), lambda k, g: (0, k)), small_spec),
-            scratch_shapes=[pltpu.VMEM((slots, count), jnp.bfloat16)],
+            scratch_shapes=[pltpu.VMEM((slots, 2 * count), jnp.bfloat16)],
         ),
         compiler_params=params,
         name="dispatch_tokens",
-    )(place, in_hbm(routes_t), in_hbm(tokens))
-    x_rows = exchanged(sent)
+    )(place, in_hbm(routes_t), routes_across, in_hbm(tokens), in_hbm(tokens_across))
+    x_rows = exchanged(sent, halves)
 
     scaled_rows, weights_moved = lax.optimization_barrier((scaled_rows, weights_moved))
     weights = [w_gate[0], w_up[0], *weights_moved]
+
+    place_spec = pl.BlockSpec(memory_space=pltpu.SMEM)
 
     back_own, *rest = pl.pallas_call(
         functools.partial(back_kernel, groups, cap),
         out_shape=[pltpu.HBM((slots, hidden), jnp.float32)]
         + [pltpu.HBM((slots, hidden), jnp.bfloat16)] * (groups - 1)
         + [pltpu.HBM((groups * slots, share), jnp.bfloat16)],
+        in_specs=[place_spec, pl.BlockSpec(), pl.BlockSpec()],
         cost_estimate=pl.CostEstimate(
             flops=BACK_COST_US * 10**9, bytes_accessed=BACK_COST_US * 10**6, transcendentals=0
         ),
         compiler_params=params,
         name="back",
-    )(scaled_rows, in_hbm(w_down[0]))
+    )(place, scaled_rows, in_hbm(w_down[0]))
     scaled_all = rest[-1]
     back_parts = [shifted(rest[k - 1], -k) for k in range(1, groups)]
 
@@ -350,9 +388,9 @@
 
     pieces = groups * (share // tile_of(share, 512))
     returning = pl.pallas_call(
-        functools.partial(backward_kernel, groups),
+        functools.partial(backward_kernel, groups, cap),
         out_shape=pltpu.HBM((slots, width + LANES), jnp.bfloat16),
-        in_specs=[whole_spec] * (4 + groups),
+        in_specs=[place_spec] + [whole_spec] * (4 + groups),
         out_specs=any_spec,
         scratch_shapes=[
             pltpu.VMEM((slots, hidden), jnp.bfloat16),
@@ -362,7 +400,7 @@
         ],
         compiler_params=params,
         name="backward",
-    )(*factors, held, back_kept, *back_parts)
+    )(place, *factors, held, back_kept, *back_parts)
     returned = exchanged(returning)
 
     hiddens = [hidden_own] + [shifted(hidden_own, k) for k in range(1, groups)]

time: 221 us -> 152 us (0.69)
  waiting for transfers between devices: 164 us -> 89 us
  Pallas kernels: 22.5 us -> 25.1 us
    ppermute x6, waiting for transfers between devices: 81.2 us -> 17.8 us  [shifted(): lax.ppermute(value, 'dp', [(i, (i + by) % groups) for i in range(groups)])]
    all_to_all x3, waiting for transfers between devices: 82.4 us -> 60.5 us  [exchanged(): lax.all_to_all(split, 'expert', split_axis=0, concat_axis=0, axis_index_g...]
    ppermute x0 -> x2, waiting for transfers between devices: none -> 10.7 us  [across(): return lax.ppermute(value, 'expert', pairs)]
    ppermute x0 -> x2, starting transfers between devices: none -> 2.36 us  [across(): return lax.ppermute(value, 'expert', pairs)]
  transfers between devices with their start and end apart: 9 -> 11, of which waited for: 6 -> 7; matrix products, arithmetic and copies ran while one was open for 4% -> 6% of each run, Pallas kernels for 8% -> 13%
where the time goes in v5:
time: 152 us
  waiting for transfers between devices  89 us (59%)
  starting transfers between devices  26.7 us (18%)
  Pallas kernels  25.1 us (17%)
  matrix products  4.53 us (3%)
  other arithmetic  3.83 us (3%)
  local copies, waits for them, and re-layouts  1.77 us (1%)
    all_to_all x3, waiting for transfers between devices, exchanged(): lax.all_to_all(split, 'expert', split_axis=0, concat_axis=0, axis_index_g...  60.5 us
    ppermute x6, waiting for transfers between devices, shifted(): lax.ppermute(value, 'dp', [(i, (i + by) % groups) for i in range(groups)])  17.8 us
    all_to_all x3, starting transfers between devices, exchanged(): lax.all_to_all(split, 'expert', split_axis=0, concat_axis=0, axis_index_g...  17.7 us
    ppermute x2, waiting for transfers between devices, across(): return lax.ppermute(value, 'expert', pairs)  10.7 us
    ppermute x6, starting transfers between devices, shifted(): lax.ppermute(value, 'dp', [(i, (i + by) % groups) for i in range(groups)])  6.62 us
    pallas_call x1, Pallas kernels, per_device(): pl.pallas_call(functools.partial(forward_kernel, groups), out_shape=[pltp...  6.54 us
    pallas_call x1, Pallas kernels, per_device(): pl.pallas_call(functools.partial(back_kernel, groups, cap), out_shape=[pl...  5.26 us
    dot_general x1, matrix products, contract_first(): lax.dot_general(left, right, (((0,), (0,)), ((), ())), preferred_element_...  4.53 us
  transfers between devices with their start and end apart: 11, of which 7 were waited for; matrix products, arithmetic and copies ran while one was open for 6% of the time, Pallas kernels for 13%

profile of v5, /device:TPU:11, one launch (start us, length us, event | category | flops | bytes accessed | tf_op | source)
XLA Modules:
  0.0 151.7 jit_solution(14614611794354599457)
XLA Ops:
  0.6 1.3 collective-permute-start.1
  1.9 0.2 collective-permute-start.2
  2.2 2.3 %collective-permute-start.3 = (bf16[128,2048]{1,0:T(8,128)(2,1)}, bf16[128,2048]{1,0:T(8,128)(2,1)S(1)}, u32[]{:S(2)}, u32[]{:S(2)}) collective-permute-start(bf16[128,2048]{1,0:T(8,128)(2,1)} %refs_2_.1), channel_id=1, source_target_pairs={{0,8},{1,9},{2,10},{3,11},{4,12},{5,13},{6,14},{7,15},{8,0},{9,1},... | collective-permute-start | bytes 1572872 | tf_op jit(solution)/shard_map/ppermute | solution.py:268
  4.5 1.0 constant_dynamic-slice_fusion
  5.4 1.3 collective-permute-start
  6.7 3.8 %pad_maximum_fusion = bf16[2048,768]{1,0:T(8,128)(2,1)} fusion(bf16[1024,768]{1,0:T(8,128)(2,1)} %bitcast.27, bf16[1024,768]{1,0:T(8,128)(2,1)} %bitcast.25), kind=kLoop, calls=%fused_computation | loop fusion | flops 6291456 | bytes 6291456 | tf_op jit(solution)/shard_map/concatenate | solution.py:287
  10.5 0.0 collective-permute-done.1.refs_1_
  10.5 0.0 collective-permute-done.2.refs_3_
  10.5 1.3 collective-permute-done.refs_5_
  11.8 1.2 collective-permute-start.5
  13.0 0.1 collective-permute-start.4
  13.1 0.1 pad_add_fusion.place_ref
  13.2 3.7 %dispatch_scaled.1 = bf16[768,1024]{1,0:T(8,128)(2,1)} custom-call(s32[2]{0:T(128)S(1)} %pad_add_fusion.place_ref, s32[2,128]{1,0:T(2,128)} %bitcast.31, s32[2,128]{1,0:T(2,128)S(1)} %collective-permute-done.1.refs_1_, f32[2,128]{1,0:T(2,128)} %bitcast.21, f32[2,128]{1,0:T(2,128)S(1)} %collective-permute-done.2.refs_3_, bf16[128,2048]{1,0:T(8,128)(2,1)} %refs_4_.1, ...), custom_call_target="tpu_custom_call" | custom-call | tf_op jit(solution)/shard_map/dispatch_scaled/pallas_call | solution.py:301
  16.9 10.7 %collective-permute-done.4.refs_1_ = s32[2,128]{1,0:T(2,128)S(1)} collective-permute-done((s32[2,128]{1,0:T(2,128)S(1)}, s32[2,128]{1,0:T(2,128)S(1)}, u32[]{:S(2)}, u32[]{:S(2)}) %collective-permute-start.4) | collective-permute-done | bytes 1056 | tf_op jit(solution)/shard_map/ppermute | solution.py:268
  27.6 0.0 collective-permute-done.3.refs_3_
  27.6 0.8 copy-done.1
  28.4 7.1 %all-to-all-start.1 = ((bf16[16,48,1024]{2,1,0:T(8,128)(2,1)}), bf16[16,48,1024]{2,1,0:T(8,128)(2,1)S(1)}, u32[]{:S(2)}, u32[]{:S(2)}) async-start(bf16[16,48,1024]{2,1,0:T(8,128)(2,1)} %bitcast.24), calls=%async_computation.1 | async-start | bytes 3145728 | tf_op jit(solution)/shard_map/all_to_all | solution.py:273
  35.5 3.6 %dispatch_tokens.1 = (bf16[384,2048]{1,0:T(8,128)(2,1)}, s32[2,128]{1,0:T(2,128)S(1)}) custom-call(s32[2]{0:T(128)S(1)} %pad_add_fusion.place_ref, s32[2,128]{1,0:T(2,128)} %bitcast.32, s32[2,128]{1,0:T(2,128)S(1)} %collective-permute-done.4.refs_1_, bf16[128,2048]{1,0:T(8,128)(2,1)} %refs_2_.1, bf16[128,2048]{1,0:T(8,128)(2,1)} %copy-done.1), custom_call_target="tpu_custom_call" | custom-call | tf_op jit(solution)/shard_map/dispatch_tokens/pallas_call | solution.py:324
  39.1 33.0 %all-to-all-done.1 = bf16[16,48,1024]{2,1,0:T(8,128)(2,1)S(1)} async-done(((bf16[16,48,1024]{2,1,0:T(8,128)(2,1)}), bf16[16,48,1024]{2,1,0:T(8,128)(2,1)S(1)}, u32[]{:S(2)}, u32[]{:S(2)}) %all-to-all-start.1) | async-done | bytes 1572896 | tf_op jit(solution)/shard_map/all_to_all | solution.py:273
  72.1 4.0 %all-to-all-start = ((bf16[8,48,2048]{2,1,0:T(8,128)(2,1)}), bf16[8,48,2048]{2,1,0:T(8,128)(2,1)S(1)}, u32[]{:S(2)}, u32[]{:S(2)}) async-start(bf16[8,48,2048]{2,1,0:T(8,128)(2,1)} %bitcast.29), calls=%async_computation | async-start | bytes 3145728 | tf_op jit(solution)/shard_map/all_to_all | solution.py:273
  76.0 3.2 %collective-permute-done.5.refs_2_ = bf16[2048,768]{1,0:T(8,128)(2,1)} collective-permute-done((bf16[2048,768]{1,0:T(8,128)(2,1)}, bf16[2048,768]{1,0:T(8,128)(2,1)}, u32[]{:S(2)}, u32[]{:S(2)}) %collective-permute-start.5) | collective-permute-done | bytes 3145760 | tf_op jit(solution)/shard_map/ppermute | solution.py:264
  79.3 5.3 %back.1 = (f32[384,768]{1,0:T(8,128)}, bf16[384,768]{1,0:T(8,128)(2,1)}, bf16[768,1024]{1,0:T(8,128)(2,1)}) custom-call(s32[2]{0:T(128)S(1)} %pad_add_fusion.place_ref, bf16[768,1024]{1,0:T(8,128)(2,1)S(1)} %bitcast.19, bf16[768,1024]{1,0:T(8,128)(2,1)} %bitcast.34), custom_call_target="tpu_custom_call" | custom-call | flops 30000001024 | bytes 30000000 | tf_op jit(solution)/shard_map/back/pallas_call | solution.py:353
  84.5 1.2 collective-permute-start.6
  85.8 8.4 %all-to-all-done = bf16[8,48,2048]{2,1,0:T(8,128)(2,1)S(1)} async-done(((bf16[8,48,2048]{2,1,0:T(8,128)(2,1)}), bf16[8,48,2048]{2,1,0:T(8,128)(2,1)S(1)}, u32[]{:S(2)}, u32[]{:S(2)}) %all-to-all-start) | async-done | bytes 1572896 | tf_op jit(solution)/shard_map/all_to_all | solution.py:273
  94.1 6.5 %forward.1 = (f32[384,768]{1,0:T(8,128)S(1)}, f32[384,768]{1,0:T(8,128)S(1)}, f32[384,768]{1,0:T(8,128)S(1)}, bf16[384,768]{1,0:T(8,128)(2,1)}, bf16[4,1024,768]...) custom-call(bf16[384,2048]{1,0:T(8,128)(2,1)S(1)} %bitcast.18, f32[384,768]{1,0:T(8,128)} %get-tuple-element.39.back_ref, ...), custom_call_target="tpu_custom_call" | custom-call | tf_op jit(solution)/shard_map/forward/pallas_call | solution.py:370
  100.7 4.2 %backward.1 = bf16[384,2176]{1,0:T(8,128)(2,1)} custom-call(s32[2]{0:T(128)S(1)} %pad_add_fusion.place_ref, f32[384,768]{1,0:T(8,128)S(1)} %get-tuple-element.41.act_ref, f32[384,768]{1,0:T(8,128)S(1)} %get-tuple-element.42.slope_ref, f32[384,768]{1,0:T(8,128)S(1)} %get-tuple-element.43.value_ref, bf16[4,1024,768]{2,1,0:T(8,128)(2,1)S(1)} %get-tuple-element.44.held_ref, ...), custom_call_target="tpu_custom_call" | custom-call | tf_op jit(solution)/shard_map/backward/pallas_call | solution.py:390
  104.9 6.6 %all-to-all-start.2 = ((bf16[16,24,2176]{2,1,0:T(8,128)(2,1)}), bf16[16,24,2176]{2,1,0:T(8,128)(2,1)S(1)}, u32[]{:S(2)}, u32[]{:S(2)}) async-start(bf16[16,24,2176]{2,1,0:T(8,128)(2,1)} %bitcast.23), calls=%async_computation.2 | async-start | bytes 3342336 | tf_op jit(solution)/shard_map/all_to_all | solution.py:273
  111.6 1.3 collective-permute-start.7
  112.9 13.3 %collective-permute-done.7 = bf16[384,768]{1,0:T(8,128)(2,1)S(1)} collective-permute-done((bf16[384,768]{1,0:T(8,128)(2,1)S(1)}, bf16[384,768]{1,0:T(8,128)(2,1)S(1)}, u32[]{:S(2)}, u32[]{:S(2)}) %collective-permute-start.7) | collective-permute-done | bytes 589856 | tf_op jit(solution)/shard_map/ppermute | solution.py:264
  126.2 4.5 %convolution_bitcast_fusion = f32[1,768,1024]{2,1,0:T(8,128)} fusion(bf16[768,1024]{1,0:T(8,128)(2,1)} %get-tuple-element.50, bf16[384,768]{1,0:T(8,128)(2,1)S(1)} %collective-permute-done.7, bf16[384,768]{1,0:T(8,128)(2,1)S(1)} %copy-done.3), kind=kOutput, calls=%fused_computation.1 | convolution fusion | flops 1210318848 | bytes 5898240 | tf_op jit(solution)/shard_map/dot_general | solution.py:22
  130.7 19.1 %all-to-all-done.2 = bf16[16,24,2176]{2,1,0:T(8,128)(2,1)S(1)} async-done(((bf16[16,24,2176]{2,1,0:T(8,128)(2,1)}), bf16[16,24,2176]{2,1,0:T(8,128)(2,1)S(1)}, u32[]{:S(2)}, u32[]{:S(2)}) %all-to-all-start.2) | async-done | bytes 1671200 | tf_op jit(solution)/shard_map/all_to_all | solution.py:273
  149.8 1.8 %combine.1 = (bf16[128,2048]{1,0:T(8,128)(2,1)}, f32[2,128]{1,0:T(2,128)}) custom-call(s32[2]{0:T(128)S(1)} %pad_add_fusion.place_ref, s32[2,128]{1,0:T(2,128)S(1)} %get-tuple-element.34.pos_ref, f32[2,128]{1,0:T(2,128)S(1)} %bitcast.22, bf16[384,2176]{1,0:T(8,128)(2,1)S(1)} %bitcast.17), custom_call_target="tpu_custom_call" | custom-call | tf_op jit(solution)/shard_map/combine/pallas_call | solution.py:409
  (8 shorter events, 0.0 us)
Async XLA Ops:
  0.6 9.9 %collective-permute-start.1 = (s32[2,128]{1,0:T(2,128)}, s32[2,128]{1,0:T(2,128)S(1)}, u32[]{:S(2)}, u32[]{:S(2)}) collective-permute-start(s32[2,128]{1,0:T(2,128)} %bitcast.30), channel_id=1, source_target_pairs={{0,16},{16,0},{1,17},{17,1},{2,18},{18,2},{3,19},{19,3},{4,20},{20... | collective-permute-start | bytes 3080 | tf_op jit(solution)/shard_map/ppermute | solution.py:264
  1.9 8.6 %collective-permute-start.2 = (f32[2,128]{1,0:T(2,128)}, f32[2,128]{1,0:T(2,128)S(1)}, u32[]{:S(2)}, u32[]{:S(2)}) collective-permute-start(f32[2,128]{1,0:T(2,128)} %bitcast.20), channel_id=1, source_target_pairs={{0,16},{16,0},{1,17},{17,1},{2,18},{18,2},{3,19},{19,3},{4,20},{20... | collective-permute-start | bytes 3080 | tf_op jit(solution)/shard_map/ppermute | solution.py:264
  2.2 25.4 %collective-permute-start.3 = (bf16[128,2048]{1,0:T(8,128)(2,1)}, bf16[128,2048]{1,0:T(8,128)(2,1)S(1)}, u32[]{:S(2)}, u32[]{:S(2)}) collective-permute-start(bf16[128,2048]{1,0:T(8,128)(2,1)} %refs_2_.1), channel_id=1, source_target_pairs={{0,8},{1,9},{2,10},{3,11},{4,12},{5,13},{6,14},{7,15},{8,0},{9,1},... | collective-permute-start | bytes 1572872 | tf_op jit(solution)/shard_map/ppermute | solution.py:268
  5.4 6.3 %collective-permute-start = (bf16[128,1024]{1,0:T(8,128)(2,1)S(1)}, bf16[128,1024]{1,0:T(8,128)(2,1)S(1)}, u32[]{:S(2)}, u32[]{:S(2)}) collective-permute-start(bf16[128,1024]{1,0:T(8,128)(2,1)S(1)} %constant_dynamic-slice_fusion), channel_id=1, source_target_pairs={{0,16},{16,0},{1,17},{17,1},{2,18},{18,2},{3,19},{19,3},{4,20},{20... | collective-permute-start | bytes 786440 | tf_op jit(solution)/shard_map/ppermute | solution.py:264
  6.7 6.3 %copy-start.2 = (s32[128,2]{0,1:T(2,128)S(1)}, s32[128,2]{0,1:T(2,128)}, u32[]{:S(2)}) copy-start(s32[128,2]{0,1:T(2,128)} %param.8) | copy-start | bytes 3076
  11.8 67.5 %collective-permute-start.5 = (bf16[2048,768]{1,0:T(8,128)(2,1)}, bf16[2048,768]{1,0:T(8,128)(2,1)}, u32[]{:S(2)}, u32[]{:S(2)}) collective-permute-start(bf16[2048,768]{1,0:T(8,128)(2,1)} %pad_maximum_fusion), channel_id=1, source_target_pairs={{0,16},{16,0},{1,17},{17,1},{2,18},{18,2},{3,19},{19,3},{4,20},{20... | collective-permute-start | bytes 9437192 | tf_op jit(solution)/shard_map/ppermute | solution.py:264
  13.0 14.5 %collective-permute-start.4 = (s32[2,128]{1,0:T(2,128)S(1)}, s32[2,128]{1,0:T(2,128)S(1)}, u32[]{:S(2)}, u32[]{:S(2)}) collective-permute-start(s32[2,128]{1,0:T(2,128)S(1)} %bitcast.33), channel_id=1, source_target_pairs={{0,8},{1,9},{2,10},{3,11},{4,12},{5,13},{6,14},{7,15},{8,0},{9,1},... | collective-permute-start | bytes 3080 | tf_op jit(solution)/shard_map/ppermute | solution.py:268
  27.6 0.8 copy-start.1
  28.4 43.7 %all-to-all-start.1 = ((bf16[16,48,1024]{2,1,0:T(8,128)(2,1)}), bf16[16,48,1024]{2,1,0:T(8,128)(2,1)S(1)}, u32[]{:S(2)}, u32[]{:S(2)}) async-start(bf16[16,48,1024]{2,1,0:T(8,128)(2,1)} %bitcast.24), calls=%async_computation.1 | async-start | bytes 3145728 | tf_op jit(solution)/shard_map/all_to_all | solution.py:273
  72.1 22.1 %all-to-all-start = ((bf16[8,48,2048]{2,1,0:T(8,128)(2,1)}), bf16[8,48,2048]{2,1,0:T(8,128)(2,1)S(1)}, u32[]{:S(2)}, u32[]{:S(2)}) async-start(bf16[8,48,2048]{2,1,0:T(8,128)(2,1)} %bitcast.29), calls=%async_computation | async-start | bytes 3145728 | tf_op jit(solution)/shard_map/all_to_all | solution.py:273
  84.5 16.2 %collective-permute-start.6 = (bf16[384,768]{1,0:T(8,128)(2,1)}, bf16[384,768]{1,0:T(8,128)(2,1)S(1)}, u32[]{:S(2)}, u32[]{:S(2)}) collective-permute-start(bf16[384,768]{1,0:T(8,128)(2,1)} %get-tuple-element.46), channel_id=1, source_target_pairs={{0,16},{16,0},{1,17},{17,1},{2,18},{18,2},{3,19},{19,3},{4,20},{20... | collective-permute-start | bytes 1769480 | tf_op jit(solution)/shard_map/ppermute | solution.py:264
  104.9 6.6 %copy-start.3 = (bf16[384,768]{1,0:T(8,128)(2,1)S(1)}, bf16[384,768]{1,0:T(8,128)(2,1)}, u32[]{:S(2)}) copy-start(bf16[384,768]{1,0:T(8,128)(2,1)} %get-tuple-element.49) | copy-start | bytes 1769476
  104.9 44.9 %all-to-all-start.2 = ((bf16[16,24,2176]{2,1,0:T(8,128)(2,1)}), bf16[16,24,2176]{2,1,0:T(8,128)(2,1)S(1)}, u32[]{:S(2)}, u32[]{:S(2)}) async-start(bf16[16,24,2176]{2,1,0:T(8,128)(2,1)} %bitcast.23), calls=%async_computation.2 | async-start | bytes 3342336 | tf_op jit(solution)/shard_map/all_to_all | solution.py:273
  111.6 14.6 %collective-permute-start.7 = (bf16[384,768]{1,0:T(8,128)(2,1)S(1)}, bf16[384,768]{1,0:T(8,128)(2,1)S(1)}, u32[]{:S(2)}, u32[]{:S(2)}) collective-permute-start(bf16[384,768]{1,0:T(8,128)(2,1)S(1)} %copy-done.3), channel_id=1, source_target_pairs={{0,16},{16,0},{1,17},{17,1},{2,18},{18,2},{3,19},{19,3},{4,20},{20... | collective-permute-start | bytes 1769480 | tf_op jit(solution)/shard_map/ppermute | solution.py:264
  126.2 23.7 %copy-start = (f32[128,2]{0,1:T(2,128)S(1)}, f32[128,2]{0,1:T(2,128)}, u32[]{:S(2)}) copy-start(f32[128,2]{0,1:T(2,128)} %param.9) | copy-start | bytes 3076

commit v6 on v5

--- a/solution.py
+++ b/solution.py
@@ -9,7 +9,9 @@
 
 LANES = 128
 VMEM_BYTES = 24 * 1024 * 1024
+TAIL = 16
 BACK_COST_US = 30
+TOKENS_COST_US = 30
 
 
 def contract_last(left, right):
@@ -64,12 +66,14 @@
 def dispatch_tokens(experts, cap, place_ref, *refs):
     routes_refs, tokens_refs, (out_ref, pos_ref, pick_ref) = refs[:2], refs[2:4], refs[4:]
     count = tokens_refs[0].shape[0]
+    top = pos_ref.shape[0]
 
     @pl.when(pl.program_id(0) == 0)
     def _():
         rows = lax.broadcasted_iota(jnp.int32, (pick_ref.shape[0], count), 0)
         for c, ref in enumerate(routes_refs):
-            near = ref[...] - place_ref[1] * (experts // 2)
+            routes = ref[...].astype(jnp.float32).astype(jnp.int32)[:top, :count]
+            near = routes - place_ref[1] * (experts // 2)
             pos = slot_positions(near, experts // 2, 2 * cap, c * cap)
             pick_ref[:, c * count : (c + 1) * count] = sum(
                 jnp.where(rows == p, 1.0, 0.0) for p in pos
@@ -289,7 +293,8 @@
     both, grads, routes_all, gates_all = lax.optimization_barrier(
         (both, grads, routes_all, gates_all)
     )
-    tokens_across, routes_across = across(tokens), across(routes_t)
+    tail = jnp.pad(routes_t.astype(tokens.dtype), ((0, TAIL - top), (0, width - count)))
+    tokens_across = across(jnp.concatenate([tokens, tail], axis=0))
     weights_moved = [shifted(both, k) for k in range(1, groups)]
 
     def in_hbm(value):
@@ -316,9 +321,6 @@
         compiler_params=params,
         name="dispatch_scaled",
     )(place, in_hbm(routes_t), *routes_all[1:], in_hbm(gates_own), *gates_all[1:], in_hbm(grad_out), *grads)
-    scaled, tokens_across, routes_across = lax.optimization_barrier(
-        (scaled, tokens_across, routes_across)
-    )
     scaled_rows = exchanged(scaled)
 
     sent, pos = pl.pallas_call(
@@ -330,7 +332,7 @@
         grid_spec=pltpu.PrefetchScalarGridSpec(
             num_scalar_prefetch=1,
             grid=(groups,),
-            in_specs=[small_spec] * 2
+            in_specs=[small_spec, pl.BlockSpec((TAIL, LANES), lambda k, g: (count // TAIL, 0))]
             + [
                 pl.BlockSpec(
                     (count, share), lambda k, g: (0, lax.rem(g[0] - k + groups, groups))
@@ -340,9 +342,12 @@
             out_specs=(pl.BlockSpec((slots, share), lambda k, g: (0, k)), small_spec),
             scratch_shapes=[pltpu.VMEM((slots, 2 * count), jnp.bfloat16)],
         ),
+        cost_estimate=pl.CostEstimate(
+            flops=TOKENS_COST_US * 10**9, bytes_accessed=TOKENS_COST_US * 10**6, transcendentals=0
+        ),
         compiler_params=params,
         name="dispatch_tokens",
-    )(place, in_hbm(routes_t), routes_across, in_hbm(tokens), in_hbm(tokens_across))
+    )(place, in_hbm(routes_t), tokens_across, in_hbm(tokens), in_hbm(tokens_across))
     x_rows = exchanged(sent, halves)
 
     scaled_rows, weights_moved = lax.optimization_barrier((scaled_rows, weights_moved))

time: 152 us -> 150 us (0.987)
  waiting for transfers between devices: 89 us -> 86.8 us
    all_to_all x3, waiting for transfers between devices: 60.5 us -> 36.6 us  [exchanged(): lax.all_to_all(split, 'expert', split_axis=0, concat_axis=0, axis_index_g...]
    ppermute x2 -> x1, waiting for transfers between devices: 10.7 us -> 28 us  [across(): return lax.ppermute(value, 'expert', pairs)]
    ppermute x6, waiting for transfers between devices: 17.8 us -> 22.2 us  [shifted(): lax.ppermute(value, 'dp', [(i, (i + by) % groups) for i in range(groups)])]
    ppermute x6, starting transfers between devices: 6.62 us -> 3.95 us  [shifted(): lax.ppermute(value, 'dp', [(i, (i + by) % groups) for i in range(groups)])]
    all_to_all x3, starting transfers between devices: 17.7 us -> 19.3 us  [exchanged(): lax.all_to_all(split, 'expert', split_axis=0, concat_axis=0, axis_index_g...]
  transfers between devices with their start and end apart: 11 -> 10, of which waited for: 7 -> 7; matrix products, arithmetic and copies ran while one was open for 6% -> 7% of each run, Pallas kernels for 13% -> 13%
where the time goes in v6:
time: 150 us
  waiting for transfers between devices  86.8 us (58%)
  starting transfers between devices  25.6 us (17%)
  Pallas kernels  25.2 us (17%)
  other arithmetic  5.12 us (3%)
  matrix products  4.53 us (3%)
  local copies, waits for them, and re-layouts  1.81 us (1%)
    all_to_all x3, waiting for transfers between devices, exchanged(): lax.all_to_all(split, 'expert', split_axis=0, concat_axis=0, axis_index_g...  36.6 us
    ppermute x1, waiting for transfers between devices, across(): return lax.ppermute(value, 'expert', pairs)  28 us
    ppermute x6, waiting for transfers between devices, shifted(): lax.ppermute(value, 'dp', [(i, (i + by) % groups) for i in range(groups)])  22.2 us
    all_to_all x3, starting transfers between devices, exchanged(): lax.all_to_all(split, 'expert', split_axis=0, concat_axis=0, axis_index_g...  19.3 us
    pallas_call x1, Pallas kernels, per_device(): pl.pallas_call(functools.partial(forward_kernel, groups), out_shape=[pltp...  6.6 us
    pallas_call x1, Pallas kernels, per_device(): pl.pallas_call(functools.partial(back_kernel, groups, cap), out_shape=[pl...  5.26 us
    dot_general x1, matrix products, contract_first(): lax.dot_general(left, right, (((0,), (0,)), ((), ())), preferred_element_...  4.53 us
    pallas_call x1, Pallas kernels, per_device(): pl.pallas_call(functools.partial(backward_kernel, groups, cap), out_shape...  4.15 us
  transfers between devices with their start and end apart: 10, of which 7 were waited for; matrix products, arithmetic and copies ran while one was open for 7% of the time, Pallas kernels for 13%

profile of v6, /device:TPU:11, one launch (start us, length us, event | category | flops | bytes accessed | tf_op | source)
XLA Modules:
  0.0 149.8 jit_solution(6230733624166215510)
XLA Ops:
  0.6 0.0 copy-start.1
  0.6 1.3 collective-permute-start.3
  1.9 0.2 collective-permute-start.2
  2.2 1.0 constant_dynamic-slice_fusion
  3.1 1.3 collective-permute-start.1
  4.4 0.7 bitcast_convert_fusion
  5.1 1.1 fusion.4
  6.2 2.4 %collective-permute-start = (bf16[144,2048]{1,0:T(8,128)(2,1)S(1)}, bf16[144,2048]{1,0:T(8,128)(2,1)S(1)}, u32[]{:S(2)}, u32[]{:S(2)}) collective-permute-start(bf16[144,2048]{1,0:T(8,128)(2,1)S(1)} %fusion.4), channel_id=1, source_target_pairs={{0,8},{1,9},{2,10},{3,11},{4,12},{5,13},{6,14},{7,15},{8,0},{9,1},... | collective-permute-start | bytes 1769480 | tf_op jit(solution)/shard_map/ppermute | solution.py:272
  8.6 3.3 %pad_maximum_fusion = bf16[2048,768]{1,0:T(8,128)(2,1)} fusion(bf16[1024,768]{1,0:T(8,128)(2,1)} %bitcast.28, bf16[1024,768]{1,0:T(8,128)(2,1)S(1)} %bitcast.27), kind=kLoop, calls=%fused_computation | loop fusion | flops 6291456 | bytes 6291456 | tf_op jit(solution)/shard_map/concatenate | solution.py:291
  11.9 0.0 collective-permute-done.3.refs_3_
  11.9 0.3 collective-permute-start.4
  12.2 0.1 pad_add_fusion.place_ref
  12.3 3.7 %dispatch_scaled.1 = bf16[768,1024]{1,0:T(8,128)(2,1)} custom-call(s32[2]{0:T(128)S(1)} %pad_add_fusion.place_ref, s32[2,128]{1,0:T(2,128)} %bitcast.32, s32[2,128]{1,0:T(2,128)S(1)} %collective-permute-done.2.refs_1_, f32[2,128]{1,0:T(2,128)} %bitcast.22, f32[2,128]{1,0:T(2,128)S(1)} %collective-permute-done.3.refs_3_, bf16[128,2048]{1,0:T(8,128)(2,1)} %refs_4_.1, ...), custom_call_target="tpu_custom_call" | custom-call | tf_op jit(solution)/shard_map/dispatch_scaled/pallas_call | solution.py:306
  15.9 7.1 %all-to-all-start.1 = ((bf16[16,48,1024]{2,1,0:T(8,128)(2,1)}), bf16[16,48,1024]{2,1,0:T(8,128)(2,1)S(1)}, u32[]{:S(2)}, u32[]{:S(2)}) async-start(bf16[16,48,1024]{2,1,0:T(8,128)(2,1)} %bitcast.25), calls=%async_computation.1 | async-start | bytes 3145728 | tf_op jit(solution)/shard_map/all_to_all | solution.py:277
  23.1 28.0 %collective-permute-done.refs_1_.refs_3_ = bf16[144,2048]{1,0:T(8,128)(2,1)S(1)} collective-permute-done((bf16[144,2048]{1,0:T(8,128)(2,1)S(1)}, bf16[144,2048]{1,0:T(8,128)(2,1)S(1)}, u32[]{:S(2)}, u32[]{:S(2)}) %collective-permute-start) | collective-permute-done | bytes 589856 | tf_op jit(solution)/shard_map/ppermute | solution.py:272
  51.1 0.8 copy-done.2
  51.9 3.6 %dispatch_tokens.1 = (bf16[384,2048]{1,0:T(8,128)(2,1)}, s32[2,128]{1,0:T(2,128)S(1)}) custom-call(s32[2]{0:T(128)S(1)} %pad_add_fusion.place_ref, s32[2,128]{1,0:T(2,128)} %bitcast.33, bf16[144,2048]{1,0:T(8,128)(2,1)} %copy-done.2, bf16[128,2048]{1,0:T(8,128)(2,1)} %refs_2_.1, bf16[144,2048]{1,0:T(8,128)(2,1)} %copy-done.2), custom_call_target="tpu_custom_call" | custom-call | flops 30000001024 | bytes 30000000 | tf_op jit(solution)/shard_map/dispatch_tokens/pallas_call | solution.py:326
  55.6 12.5 %all-to-all-done.1 = bf16[16,48,1024]{2,1,0:T(8,128)(2,1)S(1)} async-done(((bf16[16,48,1024]{2,1,0:T(8,128)(2,1)}), bf16[16,48,1024]{2,1,0:T(8,128)(2,1)S(1)}, u32[]{:S(2)}, u32[]{:S(2)}) %all-to-all-start.1) | async-done | bytes 1572896 | tf_op jit(solution)/shard_map/all_to_all | solution.py:277
  68.1 4.3 %all-to-all-start = ((bf16[8,48,2048]{2,1,0:T(8,128)(2,1)}), bf16[8,48,2048]{2,1,0:T(8,128)(2,1)S(1)}, u32[]{:S(2)}, u32[]{:S(2)}) async-start(bf16[8,48,2048]{2,1,0:T(8,128)(2,1)} %bitcast.30), calls=%async_computation | async-start | bytes 3145728 | tf_op jit(solution)/shard_map/all_to_all | solution.py:277
  72.4 7.7 %collective-permute-done.4.refs_2_ = bf16[2048,768]{1,0:T(8,128)(2,1)} collective-permute-done((bf16[2048,768]{1,0:T(8,128)(2,1)}, bf16[2048,768]{1,0:T(8,128)(2,1)}, u32[]{:S(2)}, u32[]{:S(2)}) %collective-permute-start.4) | collective-permute-done | bytes 3145760 | tf_op jit(solution)/shard_map/ppermute | solution.py:268
  80.1 5.3 %back.1 = (f32[384,768]{1,0:T(8,128)}, bf16[384,768]{1,0:T(8,128)(2,1)}, bf16[768,1024]{1,0:T(8,128)(2,1)}) custom-call(s32[2]{0:T(128)S(1)} %pad_add_fusion.place_ref, bf16[768,1024]{1,0:T(8,128)(2,1)S(1)} %bitcast.20, bf16[768,1024]{1,0:T(8,128)(2,1)} %bitcast.34), custom_call_target="tpu_custom_call" | custom-call | flops 30000001024 | bytes 30000000 | tf_op jit(solution)/shard_map/back/pallas_call | solution.py:358
  85.3 0.2 collective-permute-start.5
  85.6 4.9 %all-to-all-done = bf16[8,48,2048]{2,1,0:T(8,128)(2,1)S(1)} async-done(((bf16[8,48,2048]{2,1,0:T(8,128)(2,1)}), bf16[8,48,2048]{2,1,0:T(8,128)(2,1)S(1)}, u32[]{:S(2)}, u32[]{:S(2)}) %all-to-all-start) | async-done | bytes 1572896 | tf_op jit(solution)/shard_map/all_to_all | solution.py:277
  90.5 6.6 %forward.1 = (f32[384,768]{1,0:T(8,128)S(1)}, f32[384,768]{1,0:T(8,128)S(1)}, f32[384,768]{1,0:T(8,128)S(1)}, bf16[384,768]{1,0:T(8,128)(2,1)}, bf16[4,1024,768]...) custom-call(bf16[384,2048]{1,0:T(8,128)(2,1)S(1)} %bitcast.19, f32[384,768]{1,0:T(8,128)} %get-tuple-element.33.back_ref, ...), custom_call_target="tpu_custom_call" | custom-call | tf_op jit(solution)/shard_map/forward/pallas_call | solution.py:375
  97.1 0.5 collective-permute-done.5.refs_1_
  97.6 4.2 %backward.1 = bf16[384,2176]{1,0:T(8,128)(2,1)} custom-call(s32[2]{0:T(128)S(1)} %pad_add_fusion.place_ref, f32[384,768]{1,0:T(8,128)S(1)} %get-tuple-element.35.act_ref, f32[384,768]{1,0:T(8,128)S(1)} %get-tuple-element.36.slope_ref, f32[384,768]{1,0:T(8,128)S(1)} %get-tuple-element.37.value_ref, bf16[4,1024,768]{2,1,0:T(8,128)(2,1)S(1)} %get-tuple-element.38.held_ref, ...), custom_call_target="tpu_custom_call" | custom-call | tf_op jit(solution)/shard_map/backward/pallas_call | solution.py:395
  101.8 7.8 %all-to-all-start.2 = ((bf16[16,24,2176]{2,1,0:T(8,128)(2,1)}), bf16[16,24,2176]{2,1,0:T(8,128)(2,1)S(1)}, u32[]{:S(2)}, u32[]{:S(2)}) async-start(bf16[16,24,2176]{2,1,0:T(8,128)(2,1)} %bitcast.24), calls=%async_computation.2 | async-start | bytes 3342336 | tf_op jit(solution)/shard_map/all_to_all | solution.py:277
  109.6 0.6 collective-permute-start.6
  110.2 14.0 %collective-permute-done.6 = bf16[384,768]{1,0:T(8,128)(2,1)S(1)} collective-permute-done((bf16[384,768]{1,0:T(8,128)(2,1)S(1)}, bf16[384,768]{1,0:T(8,128)(2,1)S(1)}, u32[]{:S(2)}, u32[]{:S(2)}) %collective-permute-start.6) | collective-permute-done | bytes 589856 | tf_op jit(solution)/shard_map/ppermute | solution.py:268
  124.3 4.5 %convolution_bitcast_fusion = f32[1,768,1024]{2,1,0:T(8,128)} fusion(bf16[768,1024]{1,0:T(8,128)(2,1)} %get-tuple-element.44, bf16[384,768]{1,0:T(8,128)(2,1)S(1)} %collective-permute-done.6, bf16[384,768]{1,0:T(8,128)(2,1)S(1)} %copy-done.3), kind=kOutput, calls=%fused_computation.1 | convolution fusion | flops 1210318848 | bytes 5898240 | tf_op jit(solution)/shard_map/dot_general | solution.py:24
  128.8 19.1 %all-to-all-done.2 = bf16[16,24,2176]{2,1,0:T(8,128)(2,1)S(1)} async-done(((bf16[16,24,2176]{2,1,0:T(8,128)(2,1)}), bf16[16,24,2176]{2,1,0:T(8,128)(2,1)S(1)}, u32[]{:S(2)}, u32[]{:S(2)}) %all-to-all-start.2) | async-done | bytes 1671200 | tf_op jit(solution)/shard_map/all_to_all | solution.py:277
  147.9 1.8 %combine.1 = (bf16[128,2048]{1,0:T(8,128)(2,1)}, f32[2,128]{1,0:T(2,128)}) custom-call(s32[2]{0:T(128)S(1)} %pad_add_fusion.place_ref, s32[2,128]{1,0:T(2,128)S(1)} %get-tuple-element.24.pos_ref, f32[2,128]{1,0:T(2,128)S(1)} %bitcast.23, bf16[384,2176]{1,0:T(8,128)(2,1)S(1)} %bitcast.18), custom_call_target="tpu_custom_call" | custom-call | tf_op jit(solution)/shard_map/combine/pallas_call | solution.py:414
  (8 shorter events, 0.0 us)
Async XLA Ops:
  0.6 8.0 %copy-start.1 = (bf16[1,1024,768]{2,1,0:T(8,128)(2,1)S(1)}, bf16[1,1024,768]{2,1,0:T(8,128)(2,1)}, u32[]{:S(2)}) copy-start(bf16[1,1024,768]{2,1,0:T(8,128)(2,1)} %param.11) | copy-start | bytes 4718596
  0.6 11.2 %collective-permute-start.3 = (f32[2,128]{1,0:T(2,128)}, f32[2,128]{1,0:T(2,128)S(1)}, u32[]{:S(2)}, u32[]{:S(2)}) collective-permute-start(f32[2,128]{1,0:T(2,128)} %bitcast.21), channel_id=1, source_target_pairs={{0,16},{16,0},{1,17},{17,1},{2,18},{18,2},{3,19},{19,3},{4,20},{20... | collective-permute-start | bytes 3080 | tf_op jit(solution)/shard_map/ppermute | solution.py:268
  1.9 9.9 %collective-permute-start.2 = (s32[2,128]{1,0:T(2,128)}, s32[2,128]{1,0:T(2,128)S(1)}, u32[]{:S(2)}, u32[]{:S(2)}) collective-permute-start(s32[2,128]{1,0:T(2,128)} %bitcast.31), channel_id=1, source_target_pairs={{0,16},{16,0},{1,17},{17,1},{2,18},{18,2},{3,19},{19,3},{4,20},{20... | collective-permute-start | bytes 3080 | tf_op jit(solution)/shard_map/ppermute | solution.py:268
  3.1 8.7 %collective-permute-start.1 = (bf16[128,1024]{1,0:T(8,128)(2,1)S(1)}, bf16[128,1024]{1,0:T(8,128)(2,1)S(1)}, u32[]{:S(2)}, u32[]{:S(2)}) collective-permute-start(bf16[128,1024]{1,0:T(8,128)(2,1)S(1)} %constant_dynamic-slice_fusion), channel_id=1, source_target_pairs={{0,16},{16,0},{1,17},{17,1},{2,18},{18,2},{3,19},{19,3},{4,20},{20... | collective-permute-start | bytes 786440 | tf_op jit(solution)/shard_map/ppermute | solution.py:268
  6.2 44.9 %collective-permute-start = (bf16[144,2048]{1,0:T(8,128)(2,1)S(1)}, bf16[144,2048]{1,0:T(8,128)(2,1)S(1)}, u32[]{:S(2)}, u32[]{:S(2)}) collective-permute-start(bf16[144,2048]{1,0:T(8,128)(2,1)S(1)} %fusion.4), channel_id=1, source_target_pairs={{0,8},{1,9},{2,10},{3,11},{4,12},{5,13},{6,14},{7,15},{8,0},{9,1},... | collective-permute-start | bytes 1769480 | tf_op jit(solution)/shard_map/ppermute | solution.py:272
  11.9 68.2 %collective-permute-start.4 = (bf16[2048,768]{1,0:T(8,128)(2,1)}, bf16[2048,768]{1,0:T(8,128)(2,1)}, u32[]{:S(2)}, u32[]{:S(2)}) collective-permute-start(bf16[2048,768]{1,0:T(8,128)(2,1)} %pad_maximum_fusion), channel_id=1, source_target_pairs={{0,16},{16,0},{1,17},{17,1},{2,18},{18,2},{3,19},{19,3},{4,20},{20... | collective-permute-start | bytes 9437192 | tf_op jit(solution)/shard_map/ppermute | solution.py:268
  15.9 52.1 %all-to-all-start.1 = ((bf16[16,48,1024]{2,1,0:T(8,128)(2,1)}), bf16[16,48,1024]{2,1,0:T(8,128)(2,1)S(1)}, u32[]{:S(2)}, u32[]{:S(2)}) async-start(bf16[16,48,1024]{2,1,0:T(8,128)(2,1)} %bitcast.25), calls=%async_computation.1 | async-start | bytes 3145728 | tf_op jit(solution)/shard_map/all_to_all | solution.py:277
  51.1 0.8 copy-start.2
  68.1 22.4 %all-to-all-start = ((bf16[8,48,2048]{2,1,0:T(8,128)(2,1)}), bf16[8,48,2048]{2,1,0:T(8,128)(2,1)S(1)}, u32[]{:S(2)}, u32[]{:S(2)}) async-start(bf16[8,48,2048]{2,1,0:T(8,128)(2,1)} %bitcast.30), calls=%async_computation | async-start | bytes 3145728 | tf_op jit(solution)/shard_map/all_to_all | solution.py:277
  85.3 12.3 %collective-permute-start.5 = (bf16[384,768]{1,0:T(8,128)(2,1)}, bf16[384,768]{1,0:T(8,128)(2,1)S(1)}, u32[]{:S(2)}, u32[]{:S(2)}) collective-permute-start(bf16[384,768]{1,0:T(8,128)(2,1)} %get-tuple-element.40), channel_id=1, source_target_pairs={{0,16},{16,0},{1,17},{17,1},{2,18},{18,2},{3,19},{19,3},{4,20},{20... | collective-permute-start | bytes 1769480 | tf_op jit(solution)/shard_map/ppermute | solution.py:268
  101.8 7.9 %copy-start.3 = (bf16[384,768]{1,0:T(8,128)(2,1)S(1)}, bf16[384,768]{1,0:T(8,128)(2,1)}, u32[]{:S(2)}) copy-start(bf16[384,768]{1,0:T(8,128)(2,1)} %get-tuple-element.43) | copy-start | bytes 1769476
  101.8 46.1 %all-to-all-start.2 = ((bf16[16,24,2176]{2,1,0:T(8,128)(2,1)}), bf16[16,24,2176]{2,1,0:T(8,128)(2,1)S(1)}, u32[]{:S(2)}, u32[]{:S(2)}) async-start(bf16[16,24,2176]{2,1,0:T(8,128)(2,1)} %bitcast.24), calls=%async_computation.2 | async-start | bytes 3342336 | tf_op jit(solution)/shard_map/all_to_all | solution.py:277
  109.6 14.6 %collective-permute-start.6 = (bf16[384,768]{1,0:T(8,128)(2,1)S(1)}, bf16[384,768]{1,0:T(8,128)(2,1)S(1)}, u32[]{:S(2)}, u32[]{:S(2)}) collective-permute-start(bf16[384,768]{1,0:T(8,128)(2,1)S(1)} %copy-done.3), channel_id=1, source_target_pairs={{0,16},{16,0},{1,17},{17,1},{2,18},{18,2},{3,19},{19,3},{4,20},{20... | collective-permute-start | bytes 1769480 | tf_op jit(solution)/shard_map/ppermute | solution.py:268
  124.3 23.7 %copy-start = (f32[128,2]{0,1:T(2,128)S(1)}, f32[128,2]{0,1:T(2,128)}, u32[]{:S(2)}) copy-start(f32[128,2]{0,1:T(2,128)} %param.9) | copy-start | bytes 3076

commit v7 on v6

--- a/solution.py
+++ b/solution.py
@@ -10,7 +10,7 @@
 LANES = 128
 VMEM_BYTES = 24 * 1024 * 1024
 TAIL = 16
-BACK_COST_US = 30
+READY_COST_US = 30
 TOKENS_COST_US = 30
 
 
@@ -87,31 +87,34 @@
     ).astype(out_ref.dtype)
 
 
-def dispatch_scaled(experts, cap, groups, place_ref, *refs):
+def pick_scaled(experts, cap, groups, *refs):
     routes_refs, gate_refs = refs[:groups], refs[groups : 2 * groups]
-    grad_refs, (out_ref, pick_ref, scale_ref) = refs[2 * groups : 3 * groups], refs[3 * groups :]
-    count = grad_refs[0].shape[0]
-    slots = out_ref.shape[0]
-
-    @pl.when(pl.program_id(0) == 0)
-    def _():
-        rows = lax.broadcasted_iota(jnp.int32, (slots, count), 0)
-        total = jnp.zeros((slots, 1), jnp.float32)
-        for q in range(groups):
-            pos = slot_positions(routes_refs[q][...], experts, groups * cap, q * cap)
-            hit = jnp.zeros((slots, count), jnp.float32)
-            weight = jnp.zeros((slots, count), jnp.float32)
-            for k, p in enumerate(pos):
-                here = rows == p
-                hit = hit + jnp.where(here, 1.0, 0.0)
-                weight = weight + jnp.where(here, gate_refs[q][k : k + 1, :], 0.0)
-            pick_ref[:, q * count : (q + 1) * count] = hit.astype(jnp.bfloat16)
-            total = total + jnp.sum(weight, axis=1, keepdims=True)
-        scale_ref[...] = jnp.broadcast_to(total, scale_ref.shape)
-
+    pick_ref, scale_ref = refs[2 * groups :]
+    slots, count = pick_ref.shape[0], routes_refs[0].shape[1]
+    rows = lax.broadcasted_iota(jnp.int32, (slots, count), 0)
+    total = jnp.zeros((slots, 1), jnp.float32)
+    for q in range(groups):
+        pos = slot_positions(routes_refs[q][...], experts, groups * cap, q * cap)
+        hit = jnp.zeros((slots, count), jnp.float32)
+        weight = jnp.zeros((slots, count), jnp.float32)
+        for k, p in enumerate(pos):
+            here = rows == p
+            hit = hit + jnp.where(here, 1.0, 0.0)
+            weight = weight + jnp.where(here, gate_refs[q][k : k + 1, :], 0.0)
+        pick_ref[:, q * count : (q + 1) * count] = hit.astype(jnp.bfloat16)
+        total = total + jnp.sum(weight, axis=1, keepdims=True)
+    scale_ref[...] = jnp.broadcast_to(total, scale_ref.shape)
+
+
+def dispatch_scaled(place_ref, pick_ref, scale_ref, *refs):
+    grad_refs, out_ref = refs[:-1], refs[-1]
     grads = jnp.concatenate([ref[...] for ref in grad_refs], axis=0)
     rows = jnp.dot(pick_ref[...], grads, preferred_element_type=jnp.float32)
     out_ref[...] = (scale_ref[:, :1] * rows).astype(out_ref.dtype)
+
+
+def ready_kernel(*refs):
+    del refs
 
 
 def back_kernel(groups, cap, place_ref, rows_ref, down_ref, own_ref, *rest):
@@ -137,62 +140,53 @@
     act_ref, slope_ref, value_ref, hidden_ref, held_ref, kept_ref = refs[groups + 1 : groups + 7]
     gate_sum_ref, up_sum_ref, sems, back_sem = refs[groups + 7 :]
     share, hidden = held_ref.shape[1:]
-    step = tile_of(hidden, 384)
+    step = tile_of(hidden, 256)
     gates = [own_gate, *[ref.at[:share] for ref in others]]
     ups = [own_up, *[ref.at[share:] for ref in others]]
     spans = [slice(at, at + step) for at in range(0, hidden, step)]
 
-    loads = []
-    for k in range(groups):
-        for ref, i in ((gates[k], k), (ups[k], groups + k)):
-            for n, cols in enumerate(spans):
-                loads.append(
-                    pltpu.make_async_copy(
-                        ref.at[:, cols], held_ref.at[i, :, cols], sems.at[n, i]
-                    )
-                )
+    uses = [(k, cols, i) for k in range(groups) for cols in spans for i in (k, groups + k)]
+    sources = gates + ups
+    loads = [
+        pltpu.make_async_copy(
+            sources[i].at[:, cols], held_ref.at[i, :, cols], sems.at[cols.start // step, i]
+        )
+        for _, cols, i in uses
+    ]
     loads.append(pltpu.make_async_copy(back_ref, kept_ref, back_sem.at[0]))
     flying = 3
     for copy in loads[:flying]:
         copy.start()
-    place = 0
-
-    def arrived():
-        nonlocal place
-        loads[place].wait()
-        if place + flying < len(loads):
-            loads[place + flying].start()
-        place += 1
-
-    def against(k, i, cols):
-        return jnp.dot(
+
+    def finish(cols):
+        pre_gate, pre_up = gate_sum_ref[:, cols], up_sum_ref[:, cols]
+        sig = jax.nn.sigmoid(pre_gate)
+        act = pre_gate * sig
+        hidden_f = act * pre_up
+        act_ref[:, cols] = act
+        slope_ref[:, cols] = pre_up * (sig * (1.0 + pre_gate * (1.0 - sig)))
+        value_ref[:, cols] = hidden_f
+        hidden_ref[:, cols] = hidden_f.astype(hidden_ref.dtype)
+
+    complete = None
+    for n, (k, cols, i) in enumerate(uses):
+        loads[n].wait()
+        if n + flying < len(loads):
+            loads[n + flying].start()
+        part = jnp.dot(
             x_ref[:, k * share : (k + 1) * share],
             held_ref[i, :, cols],
             preferred_element_type=jnp.float32,
         )
-
-    for k in range(groups):
-        for cols in spans:
-            arrived()
-            part = against(k, k, cols)
-            gate_sum_ref[:, cols] = part if k == 0 else gate_sum_ref[:, cols] + part
-        for cols in spans:
-            arrived()
-            pre_up = against(k, groups + k, cols)
-            if k > 0:
-                pre_up += up_sum_ref[:, cols]
-            if k < groups - 1:
-                up_sum_ref[:, cols] = pre_up
-                continue
-            pre_gate = gate_sum_ref[:, cols]
-            sig = jax.nn.sigmoid(pre_gate)
-            act = pre_gate * sig
-            hidden_f = act * pre_up
-            act_ref[:, cols] = act
-            slope_ref[:, cols] = pre_up * (sig * (1.0 + pre_gate * (1.0 - sig)))
-            value_ref[:, cols] = hidden_f
-            hidden_ref[:, cols] = hidden_f.astype(hidden_ref.dtype)
-    arrived()
+        sum_ref = gate_sum_ref if i < groups else up_sum_ref
+        if complete is not None:
+            finish(complete)
+            complete = None
+        sum_ref[:, cols] = part if k == 0 else sum_ref[:, cols] + part
+        if k == groups - 1 and i >= groups:
+            complete = cols
+    finish(complete)
+    loads[-1].wait()
 
 
 def backward_kernel(groups, cap, place_ref, act_ref, slope_ref, value_ref, held_ref, *refs):
@@ -303,24 +297,29 @@
     block = tile_of(share, 512)
     steps = share // block
     small_spec = pl.BlockSpec((top, count), lambda c, g: (0, 0))
+    picks = pl.pallas_call(
+        functools.partial(pick_scaled, experts, cap, groups),
+        out_shape=(
+            pltpu.VMEM((groups * slots, groups * count), jnp.bfloat16),
+            pltpu.VMEM((groups * slots, LANES), jnp.float32),
+        ),
+        compiler_params=params,
+        name="pick_scaled",
+    )(in_hbm(routes_t), *routes_all[1:], in_hbm(gates_own), *gates_all[1:])
     scaled = pl.pallas_call(
-        functools.partial(dispatch_scaled, experts, cap, groups),
+        dispatch_scaled,
         out_shape=pltpu.HBM((groups * slots, share), jnp.bfloat16),
         grid_spec=pltpu.PrefetchScalarGridSpec(
             num_scalar_prefetch=1,
             grid=(steps,),
-            in_specs=[small_spec] * (2 * groups)
+            in_specs=[pl.BlockSpec(memory_space=pltpu.VMEM)] * 2
             + [pl.BlockSpec((count, block), lambda c, g: (0, g[0] * steps + c))]
             + [pl.BlockSpec((count, block), lambda c, g: (0, c))] * (groups - 1),
             out_specs=pl.BlockSpec((groups * slots, block), lambda c, g: (0, c)),
-            scratch_shapes=[
-                pltpu.VMEM((groups * slots, groups * count), jnp.bfloat16),
-                pltpu.VMEM((groups * slots, LANES), jnp.float32),
-            ],
         ),
         compiler_params=params,
         name="dispatch_scaled",
-    )(place, in_hbm(routes_t), *routes_all[1:], in_hbm(gates_own), *gates_all[1:], in_hbm(grad_out), *grads)
+    )(place, *picks, in_hbm(grad_out), *grads)
     scaled_rows = exchanged(scaled)
 
     sent, pos = pl.pallas_call(
@@ -350,7 +349,18 @@
     )(place, in_hbm(routes_t), tokens_across, in_hbm(tokens), in_hbm(tokens_across))
     x_rows = exchanged(sent, halves)
 
-    scaled_rows, weights_moved = lax.optimization_barrier((scaled_rows, weights_moved))
+    weights_moved = pl.pallas_call(
+        ready_kernel,
+        out_shape=[pltpu.HBM(value.shape, value.dtype) for value in weights_moved],
+        in_specs=[pl.BlockSpec(memory_space=pl.ANY)] * (groups - 1),
+        out_specs=[pl.BlockSpec(memory_space=pl.ANY)] * (groups - 1),
+        input_output_aliases={k: k for k in range(groups - 1)},
+        cost_estimate=pl.CostEstimate(
+            flops=READY_COST_US * 10**9, bytes_accessed=READY_COST_US * 10**6, transcendentals=0
+        ),
+        compiler_params=params,
+        name="ready",
+    )(*[in_hbm(value) for value in weights_moved])
     weights = [w_gate[0], w_up[0], *weights_moved]
 
     place_spec = pl.BlockSpec(memory_space=pltpu.SMEM)
@@ -361,9 +371,6 @@
         + [pltpu.HBM((slots, hidden), jnp.bfloat16)] * (groups - 1)
         + [pltpu.HBM((groups * slots, share), jnp.bfloat16)],
         in_specs=[place_spec, pl.BlockSpec(), pl.BlockSpec()],
-        cost_estimate=pl.CostEstimate(
-            flops=BACK_COST_US * 10**9, bytes_accessed=BACK_COST_US * 10**6, transcendentals=0
-        ),
         compiler_params=params,
         name="back",
     )(place, scaled_rows, in_hbm(w_down[0]))
@@ -384,7 +391,7 @@
         scratch_shapes=[
             pltpu.VMEM((slots, hidden), jnp.float32),
             pltpu.VMEM((slots, hidden), jnp.float32),
-            pltpu.SemaphoreType.DMA((hidden // tile_of(hidden, 384), 2 * groups)),
+            pltpu.SemaphoreType.DMA((hidden // tile_of(hidden, 256), 2 * groups)),
             pltpu.SemaphoreType.DMA((1,)),
         ],
         compiler_params=params,

time: 150 us -> 152 us (1.013)
  Pallas kernels: 25.2 us -> 27.8 us
    all_to_all x3, waiting for transfers between devices: 36.6 us -> 42.3 us  [exchanged(): lax.all_to_all(split, 'expert', split_axis=0, concat_axis=0, axis_index_g...]
    ppermute x6, waiting for transfers between devices: 22.2 us -> 16.8 us  [shifted(): lax.ppermute(value, 'dp', [(i, (i + by) % groups) for i in range(groups)])]
    pallas_call x1, Pallas kernels: 6.6 us -> 8.58 us  [per_device(): pl.pallas_call(functools.partial(forward_kernel, groups), out_shape=[pltp...]
    pallas_call x1 -> x3, Pallas kernels: 3.69 us -> 4.36 us  [the longest x1 3.15 us: per_device(): pl.pallas_call(dispatch_scaled, out_shape=pltpu.HBM((groups * slots, shar...]
  transfers between devices with their start and end apart: 10 -> 10, of which waited for: 7 -> 6; matrix products, arithmetic and copies ran while one was open for 7% -> 7% of each run, Pallas kernels for 13% -> 14%
where the time goes in v7:
time: 152 us
  waiting for transfers between devices  86.4 us (57%)
  Pallas kernels  27.8 us (18%)
  starting transfers between devices  25.8 us (17%)
  other arithmetic  5.12 us (3%)
  matrix products  4.18 us (3%)
  local copies, waits for them, and re-layouts  1.81 us (1%)
    all_to_all x3, waiting for transfers between devices, exchanged(): lax.all_to_all(split, 'expert', split_axis=0, concat_axis=0, axis_index_g...  42.3 us
    ppermute x1, waiting for transfers between devices, across(): return lax.ppermute(value, 'expert', pairs)  27.3 us
    all_to_all x3, starting transfers between devices, exchanged(): lax.all_to_all(split, 'expert', split_axis=0, concat_axis=0, axis_index_g...  19.8 us
    ppermute x6, waiting for transfers between devices, shifted(): lax.ppermute(value, 'dp', [(i, (i + by) % groups) for i in range(groups)])  16.8 us
    pallas_call x1, Pallas kernels, per_device(): pl.pallas_call(functools.partial(forward_kernel, groups), out_shape=[pltp...  8.58 us
    pallas_call x1, Pallas kernels, per_device(): pl.pallas_call(functools.partial(back_kernel, groups, cap), out_shape=[pl...  5.22 us
    dot_general x1, matrix products, contract_first(): lax.dot_general(left, right, (((0,), (0,)), ((), ())), preferred_element_...  4.18 us
    pallas_call x1, Pallas kernels, per_device(): pl.pallas_call(functools.partial(backward_kernel, groups, cap), out_shape...  4.16 us
  transfers between devices with their start and end apart: 10, of which 6 were waited for; matrix products, arithmetic and copies ran while one was open for 7% of the time, Pallas kernels for 14%

profile of v7, /device:TPU:11, one launch (start us, length us, event | category | flops | bytes accessed | tf_op | source)
XLA Modules:
  0.0 151.8 jit_solution(6163317356635905069)
XLA Ops:
  0.6 0.0 copy-start.1
  0.6 1.3 collective-permute-start.3
  1.9 0.2 collective-permute-start.2
  2.2 1.0 constant_dynamic-slice_fusion
  3.1 1.3 collective-permute-start.1
  4.4 0.7 bitcast_convert_fusion
  5.1 1.1 fusion.4
  6.2 2.4 %collective-permute-start = (bf16[144,2048]{1,0:T(8,128)(2,1)S(1)}, bf16[144,2048]{1,0:T(8,128)(2,1)S(1)}, u32[]{:S(2)}, u32[]{:S(2)}) collective-permute-start(bf16[144,2048]{1,0:T(8,128)(2,1)S(1)} %fusion.4), channel_id=1, source_target_pairs={{0,8},{1,9},{2,10},{3,11},{4,12},{5,13},{6,14},{7,15},{8,0},{9,1},... | collective-permute-start | bytes 1769480 | tf_op jit(solution)/shard_map/ppermute | solution.py:266
  8.6 3.3 %pad_maximum_fusion = bf16[2048,768]{1,0:T(8,128)(2,1)} fusion(bf16[1024,768]{1,0:T(8,128)(2,1)} %bitcast.28, bf16[1024,768]{1,0:T(8,128)(2,1)S(1)} %bitcast.27), kind=kLoop, calls=%fused_computation | loop fusion | flops 6291456 | bytes 6291456 | tf_op jit(solution)/shard_map/concatenate | solution.py:285
  11.9 0.0 collective-permute-done.2.refs_1_
  11.9 0.3 collective-permute-start.4
  12.2 0.1 pad_add_fusion.place_ref
  12.3 1.2 pick_scaled.1
  13.5 3.1 %dispatch_scaled.1 = bf16[768,1024]{1,0:T(8,128)(2,1)} custom-call(s32[2]{0:T(128)S(1)} %pad_add_fusion.place_ref, bf16[768,256]{1,0:T(8,128)(2,1)S(1)} %get-tuple-element.30.pick_ref, f32[768,128]{1,0:T(8,128)S(1)} %get-tuple-element.31.scale_ref, bf16[128,2048]{1,0:T(8,128)(2,1)} %refs_0_.1, bf16[128,1024]{1,0:T(8,128)(2,1)S(1)} %collective-permute-done.1.refs_1_), custom_call_target="tpu_custom_call" | custom-call | tf_op jit(solution)/shard_map/dispatch_scaled/pallas_call | solution.py:309
  16.6 7.1 %all-to-all-start.1 = ((bf16[16,48,1024]{2,1,0:T(8,128)(2,1)}), bf16[16,48,1024]{2,1,0:T(8,128)(2,1)S(1)}, u32[]{:S(2)}, u32[]{:S(2)}) async-start(bf16[16,48,1024]{2,1,0:T(8,128)(2,1)} %bitcast.25), calls=%async_computation.1 | async-start | bytes 3145728 | tf_op jit(solution)/shard_map/all_to_all | solution.py:271
  23.8 27.3 %collective-permute-done.refs_1_.refs_3_ = bf16[144,2048]{1,0:T(8,128)(2,1)S(1)} collective-permute-done((bf16[144,2048]{1,0:T(8,128)(2,1)S(1)}, bf16[144,2048]{1,0:T(8,128)(2,1)S(1)}, u32[]{:S(2)}, u32[]{:S(2)}) %collective-permute-start) | collective-permute-done | bytes 589856 | tf_op jit(solution)/shard_map/ppermute | solution.py:266
  51.1 0.8 copy-done.3
  51.9 3.6 %dispatch_tokens.1 = (bf16[384,2048]{1,0:T(8,128)(2,1)}, s32[2,128]{1,0:T(2,128)S(1)}) custom-call(s32[2]{0:T(128)S(1)} %pad_add_fusion.place_ref, s32[2,128]{1,0:T(2,128)} %bitcast.34, bf16[144,2048]{1,0:T(8,128)(2,1)} %copy-done.3, bf16[128,2048]{1,0:T(8,128)(2,1)} %refs_2_.1, bf16[144,2048]{1,0:T(8,128)(2,1)} %copy-done.3), custom_call_target="tpu_custom_call" | custom-call | flops 30000001024 | bytes 30000000 | tf_op jit(solution)/shard_map/dispatch_tokens/pallas_call | solution.py:325
  55.5 12.5 %all-to-all-done.1 = bf16[16,48,1024]{2,1,0:T(8,128)(2,1)S(1)} async-done(((bf16[16,48,1024]{2,1,0:T(8,128)(2,1)}), bf16[16,48,1024]{2,1,0:T(8,128)(2,1)S(1)}, u32[]{:S(2)}, u32[]{:S(2)}) %all-to-all-start.1) | async-done | bytes 1572896 | tf_op jit(solution)/shard_map/all_to_all | solution.py:271
  68.1 4.3 %all-to-all-start = ((bf16[8,48,2048]{2,1,0:T(8,128)(2,1)}), bf16[8,48,2048]{2,1,0:T(8,128)(2,1)S(1)}, u32[]{:S(2)}, u32[]{:S(2)}) async-start(bf16[8,48,2048]{2,1,0:T(8,128)(2,1)} %bitcast.30), calls=%async_computation | async-start | bytes 3145728 | tf_op jit(solution)/shard_map/all_to_all | solution.py:271
  72.4 5.2 %back.1 = (f32[384,768]{1,0:T(8,128)}, bf16[384,768]{1,0:T(8,128)(2,1)}, bf16[768,1024]{1,0:T(8,128)(2,1)}) custom-call(s32[2]{0:T(128)S(1)} %pad_add_fusion.place_ref, bf16[768,1024]{1,0:T(8,128)(2,1)S(1)} %bitcast.19, bf16[768,1024]{1,0:T(8,128)(2,1)} %bitcast.31), custom_call_target="tpu_custom_call" | custom-call | tf_op jit(solution)/shard_map/back/pallas_call | solution.py:368
  77.6 0.2 collective-permute-start.5
  77.8 2.2 %collective-permute-done.4.refs_0_ = bf16[2048,768]{1,0:T(8,128)(2,1)} collective-permute-done((bf16[2048,768]{1,0:T(8,128)(2,1)}, bf16[2048,768]{1,0:T(8,128)(2,1)}, u32[]{:S(2)}, u32[]{:S(2)}) %collective-permute-start.4) | collective-permute-done | bytes 3145760 | tf_op jit(solution)/shard_map/ppermute | solution.py:262
  80.1 10.4 %all-to-all-done = bf16[8,48,2048]{2,1,0:T(8,128)(2,1)S(1)} async-done(((bf16[8,48,2048]{2,1,0:T(8,128)(2,1)}), bf16[8,48,2048]{2,1,0:T(8,128)(2,1)S(1)}, u32[]{:S(2)}, u32[]{:S(2)}) %all-to-all-start) | async-done | bytes 1572896 | tf_op jit(solution)/shard_map/all_to_all | solution.py:271
  90.5 8.6 %forward.1 = (f32[384,768]{1,0:T(8,128)S(1)}, f32[384,768]{1,0:T(8,128)S(1)}, f32[384,768]{1,0:T(8,128)S(1)}, bf16[384,768]{1,0:T(8,128)(2,1)}, bf16[4,1024,768]...) custom-call(bf16[384,2048]{1,0:T(8,128)(2,1)S(1)} %bitcast.20, f32[384,768]{1,0:T(8,128)} %get-tuple-element.33.back_ref, ...), custom_call_target="tpu_custom_call" | custom-call | tf_op jit(solution)/shard_map/forward/pallas_call | solution.py:382
  99.1 4.2 %backward.1 = bf16[384,2176]{1,0:T(8,128)(2,1)} custom-call(s32[2]{0:T(128)S(1)} %pad_add_fusion.place_ref, f32[384,768]{1,0:T(8,128)S(1)} %get-tuple-element.35.act_ref, f32[384,768]{1,0:T(8,128)S(1)} %get-tuple-element.36.slope_ref, f32[384,768]{1,0:T(8,128)S(1)} %get-tuple-element.37.value_ref, bf16[4,1024,768]{2,1,0:T(8,128)(2,1)S(1)} %get-tuple-element.38.held_ref, ...), custom_call_target="tpu_custom_call" | custom-call | tf_op jit(solution)/shard_map/backward/pallas_call | solution.py:402
  103.3 8.4 %all-to-all-start.2 = ((bf16[16,24,2176]{2,1,0:T(8,128)(2,1)}), bf16[16,24,2176]{2,1,0:T(8,128)(2,1)S(1)}, u32[]{:S(2)}, u32[]{:S(2)}) async-start(bf16[16,24,2176]{2,1,0:T(8,128)(2,1)} %bitcast.24), calls=%async_computation.2 | async-start | bytes 3342336 | tf_op jit(solution)/shard_map/all_to_all | solution.py:271
  111.6 0.2 collective-permute-start.6
  111.9 14.5 %collective-permute-done.6 = bf16[384,768]{1,0:T(8,128)(2,1)S(1)} collective-permute-done((bf16[384,768]{1,0:T(8,128)(2,1)}, bf16[384,768]{1,0:T(8,128)(2,1)S(1)}, u32[]{:S(2)}, u32[]{:S(2)}) %collective-permute-start.6) | collective-permute-done | bytes 589856 | tf_op jit(solution)/shard_map/ppermute | solution.py:262
  126.4 4.2 %convolution_bitcast_fusion = f32[1,768,1024]{2,1,0:T(8,128)} fusion(bf16[768,1024]{1,0:T(8,128)(2,1)S(1)} %copy-done.2, bf16[384,768]{1,0:T(8,128)(2,1)S(1)} %collective-permute-done.6, bf16[384,768]{1,0:T(8,128)(2,1)} %get-tuple-element.43), kind=kOutput, calls=%fused_computation.1 | convolution fusion | flops 1210318848 | bytes 5898240 | tf_op jit(solution)/shard_map/dot_general | solution.py:24
  130.6 19.3 %all-to-all-done.2 = bf16[16,24,2176]{2,1,0:T(8,128)(2,1)S(1)} async-done(((bf16[16,24,2176]{2,1,0:T(8,128)(2,1)}), bf16[16,24,2176]{2,1,0:T(8,128)(2,1)S(1)}, u32[]{:S(2)}, u32[]{:S(2)}) %all-to-all-start.2) | async-done | bytes 1671200 | tf_op jit(solution)/shard_map/all_to_all | solution.py:271
  149.9 1.8 %combine.1 = (bf16[128,2048]{1,0:T(8,128)(2,1)}, f32[2,128]{1,0:T(2,128)}) custom-call(s32[2]{0:T(128)S(1)} %pad_add_fusion.place_ref, s32[2,128]{1,0:T(2,128)S(1)} %get-tuple-element.24.pos_ref, f32[2,128]{1,0:T(2,128)S(1)} %bitcast.23, bf16[384,2176]{1,0:T(8,128)(2,1)S(1)} %bitcast.18), custom_call_target="tpu_custom_call" | custom-call | tf_op jit(solution)/shard_map/combine/pallas_call | solution.py:421
  (10 shorter events, 0.0 us)
Async XLA Ops:
  0.6 8.0 %copy-start.1 = (bf16[1,1024,768]{2,1,0:T(8,128)(2,1)S(1)}, bf16[1,1024,768]{2,1,0:T(8,128)(2,1)}, u32[]{:S(2)}) copy-start(bf16[1,1024,768]{2,1,0:T(8,128)(2,1)} %param.11) | copy-start | bytes 4718596
  0.6 11.2 %collective-permute-start.3 = (f32[2,128]{1,0:T(2,128)}, f32[2,128]{1,0:T(2,128)S(1)}, u32[]{:S(2)}, u32[]{:S(2)}) collective-permute-start(f32[2,128]{1,0:T(2,128)} %bitcast.21), channel_id=1, source_target_pairs={{0,16},{16,0},{1,17},{17,1},{2,18},{18,2},{3,19},{19,3},{4,20},{20... | collective-permute-start | bytes 3080 | tf_op jit(solution)/shard_map/ppermute | solution.py:262
  1.9 9.9 %collective-permute-start.2 = (s32[2,128]{1,0:T(2,128)}, s32[2,128]{1,0:T(2,128)S(1)}, u32[]{:S(2)}, u32[]{:S(2)}) collective-permute-start(s32[2,128]{1,0:T(2,128)} %bitcast.32), channel_id=1, source_target_pairs={{0,16},{16,0},{1,17},{17,1},{2,18},{18,2},{3,19},{19,3},{4,20},{20... | collective-permute-start | bytes 3080 | tf_op jit(solution)/shard_map/ppermute | solution.py:262
  3.1 8.7 %collective-permute-start.1 = (bf16[128,1024]{1,0:T(8,128)(2,1)S(1)}, bf16[128,1024]{1,0:T(8,128)(2,1)S(1)}, u32[]{:S(2)}, u32[]{:S(2)}) collective-permute-start(bf16[128,1024]{1,0:T(8,128)(2,1)S(1)} %constant_dynamic-slice_fusion), channel_id=1, source_target_pairs={{0,16},{16,0},{1,17},{17,1},{2,18},{18,2},{3,19},{19,3},{4,20},{20... | collective-permute-start | bytes 786440 | tf_op jit(solution)/shard_map/ppermute | solution.py:262
  6.2 44.9 %collective-permute-start = (bf16[144,2048]{1,0:T(8,128)(2,1)S(1)}, bf16[144,2048]{1,0:T(8,128)(2,1)S(1)}, u32[]{:S(2)}, u32[]{:S(2)}) collective-permute-start(bf16[144,2048]{1,0:T(8,128)(2,1)S(1)} %fusion.4), channel_id=1, source_target_pairs={{0,8},{1,9},{2,10},{3,11},{4,12},{5,13},{6,14},{7,15},{8,0},{9,1},... | collective-permute-start | bytes 1769480 | tf_op jit(solution)/shard_map/ppermute | solution.py:266
  11.9 68.2 %collective-permute-start.4 = (bf16[2048,768]{1,0:T(8,128)(2,1)}, bf16[2048,768]{1,0:T(8,128)(2,1)}, u32[]{:S(2)}, u32[]{:S(2)}) collective-permute-start(bf16[2048,768]{1,0:T(8,128)(2,1)} %pad_maximum_fusion), channel_id=1, source_target_pairs={{0,16},{16,0},{1,17},{17,1},{2,18},{18,2},{3,19},{19,3},{4,20},{20... | collective-permute-start | bytes 9437192 | tf_op jit(solution)/shard_map/ppermute | solution.py:262
  16.6 51.4 %all-to-all-start.1 = ((bf16[16,48,1024]{2,1,0:T(8,128)(2,1)}), bf16[16,48,1024]{2,1,0:T(8,128)(2,1)S(1)}, u32[]{:S(2)}, u32[]{:S(2)}) async-start(bf16[16,48,1024]{2,1,0:T(8,128)(2,1)} %bitcast.25), calls=%async_computation.1 | async-start | bytes 3145728 | tf_op jit(solution)/shard_map/all_to_all | solution.py:271
  51.1 0.8 copy-start.3
  68.1 22.4 %all-to-all-start = ((bf16[8,48,2048]{2,1,0:T(8,128)(2,1)}), bf16[8,48,2048]{2,1,0:T(8,128)(2,1)S(1)}, u32[]{:S(2)}, u32[]{:S(2)}) async-start(bf16[8,48,2048]{2,1,0:T(8,128)(2,1)} %bitcast.30), calls=%async_computation | async-start | bytes 3145728 | tf_op jit(solution)/shard_map/all_to_all | solution.py:271
  77.6 21.5 %collective-permute-start.5 = (bf16[384,768]{1,0:T(8,128)(2,1)}, bf16[384,768]{1,0:T(8,128)(2,1)S(1)}, u32[]{:S(2)}, u32[]{:S(2)}) collective-permute-start(bf16[384,768]{1,0:T(8,128)(2,1)} %get-tuple-element.40), channel_id=1, source_target_pairs={{0,16},{16,0},{1,17},{17,1},{2,18},{18,2},{3,19},{19,3},{4,20},{20... | collective-permute-start | bytes 1769480 | tf_op jit(solution)/shard_map/ppermute | solution.py:262
  103.3 23.1 %copy-start.2 = (bf16[768,1024]{1,0:T(8,128)(2,1)S(1)}, bf16[768,1024]{1,0:T(8,128)(2,1)}, u32[]{:S(2)}) copy-start(bf16[768,1024]{1,0:T(8,128)(2,1)} %get-tuple-element.44) | copy-start | bytes 4718596
  103.3 46.7 %all-to-all-start.2 = ((bf16[16,24,2176]{2,1,0:T(8,128)(2,1)}), bf16[16,24,2176]{2,1,0:T(8,128)(2,1)S(1)}, u32[]{:S(2)}, u32[]{:S(2)}) async-start(bf16[16,24,2176]{2,1,0:T(8,128)(2,1)} %bitcast.24), calls=%async_computation.2 | async-start | bytes 3342336 | tf_op jit(solution)/shard_map/all_to_all | solution.py:271
  111.6 14.8 %collective-permute-start.6 = (bf16[384,768]{1,0:T(8,128)(2,1)}, bf16[384,768]{1,0:T(8,128)(2,1)S(1)}, u32[]{:S(2)}, u32[]{:S(2)}) collective-permute-start(bf16[384,768]{1,0:T(8,128)(2,1)} %get-tuple-element.43), channel_id=1, source_target_pairs={{0,16},{16,0},{1,17},{17,1},{2,18},{18,2},{3,19},{19,3},{4,20},{20... | collective-permute-start | bytes 1769480 | tf_op jit(solution)/shard_map/ppermute | solution.py:262
  126.4 23.5 %copy-start = (f32[128,2]{0,1:T(2,128)S(1)}, f32[128,2]{0,1:T(2,128)}, u32[]{:S(2)}) copy-start(f32[128,2]{0,1:T(2,128)} %param.9) | copy-start | bytes 3076

commit v8 on v7

--- a/solution.py
+++ b/solution.py
@@ -87,27 +87,28 @@
     ).astype(out_ref.dtype)
 
 
-def pick_scaled(experts, cap, groups, *refs):
+def dispatch_scaled(experts, cap, groups, place_ref, *refs):
     routes_refs, gate_refs = refs[:groups], refs[groups : 2 * groups]
-    pick_ref, scale_ref = refs[2 * groups :]
-    slots, count = pick_ref.shape[0], routes_refs[0].shape[1]
-    rows = lax.broadcasted_iota(jnp.int32, (slots, count), 0)
-    total = jnp.zeros((slots, 1), jnp.float32)
-    for q in range(groups):
-        pos = slot_positions(routes_refs[q][...], experts, groups * cap, q * cap)
-        hit = jnp.zeros((slots, count), jnp.float32)
-        weight = jnp.zeros((slots, count), jnp.float32)
-        for k, p in enumerate(pos):
-            here = rows == p
-            hit = hit + jnp.where(here, 1.0, 0.0)
-            weight = weight + jnp.where(here, gate_refs[q][k : k + 1, :], 0.0)
-        pick_ref[:, q * count : (q + 1) * count] = hit.astype(jnp.bfloat16)
-        total = total + jnp.sum(weight, axis=1, keepdims=True)
-    scale_ref[...] = jnp.broadcast_to(total, scale_ref.shape)
-
-
-def dispatch_scaled(place_ref, pick_ref, scale_ref, *refs):
-    grad_refs, out_ref = refs[:-1], refs[-1]
+    grad_refs, (out_ref, pick_ref, scale_ref) = refs[2 * groups : 3 * groups], refs[3 * groups :]
+    count = grad_refs[0].shape[0]
+    slots = out_ref.shape[0]
+
+    @pl.when(pl.program_id(0) == 0)
+    def _():
+        rows = lax.broadcasted_iota(jnp.int32, (slots, count), 0)
+        total = jnp.zeros((slots, 1), jnp.float32)
+        for q in range(groups):
+            pos = slot_positions(routes_refs[q][...], experts, groups * cap, q * cap)
+            hit = jnp.zeros((slots, count), jnp.float32)
+            weight = jnp.zeros((slots, count), jnp.float32)
+            for k, p in enumerate(pos):
+                here = rows == p
+                hit = hit + jnp.where(here, 1.0, 0.0)
+                weight = weight + jnp.where(here, gate_refs[q][k : k + 1, :], 0.0)
+            pick_ref[:, q * count : (q + 1) * count] = hit.astype(jnp.bfloat16)
+            total = total + jnp.sum(weight, axis=1, keepdims=True)
+        scale_ref[...] = jnp.broadcast_to(total, scale_ref.shape)
+
     grads = jnp.concatenate([ref[...] for ref in grad_refs], axis=0)
     rows = jnp.dot(pick_ref[...], grads, preferred_element_type=jnp.float32)
     out_ref[...] = (scale_ref[:, :1] * rows).astype(out_ref.dtype)
@@ -145,16 +146,19 @@
     ups = [own_up, *[ref.at[share:] for ref in others]]
     spans = [slice(at, at + step) for at in range(0, hidden, step)]
 
-    uses = [(k, cols, i) for k in range(groups) for cols in spans for i in (k, groups + k)]
-    sources = gates + ups
+    order = [i for k in range(groups) for i in (k, groups + k)]
+    sources, part_rows = gates + ups, share // 2
     loads = [
         pltpu.make_async_copy(
-            sources[i].at[:, cols], held_ref.at[i, :, cols], sems.at[cols.start // step, i]
+            sources[i].at[n * part_rows : (n + 1) * part_rows],
+            held_ref.at[i, n * part_rows : (n + 1) * part_rows],
+            sems.at[n, i],
         )
-        for _, cols, i in uses
+        for i in order
+        for n in range(2)
     ]
     loads.append(pltpu.make_async_copy(back_ref, kept_ref, back_sem.at[0]))
-    flying = 3
+    flying = 2
     for copy in loads[:flying]:
         copy.start()
 
@@ -169,22 +173,23 @@
         hidden_ref[:, cols] = hidden_f.astype(hidden_ref.dtype)
 
     complete = None
-    for n, (k, cols, i) in enumerate(uses):
-        loads[n].wait()
-        if n + flying < len(loads):
-            loads[n + flying].start()
-        part = jnp.dot(
-            x_ref[:, k * share : (k + 1) * share],
-            held_ref[i, :, cols],
-            preferred_element_type=jnp.float32,
-        )
+    for at, i in enumerate(order):
+        k = i % groups
+        for n in (2 * at, 2 * at + 1):
+            loads[n].wait()
+            if n + flying < len(loads):
+                loads[n + flying].start()
         sum_ref = gate_sum_ref if i < groups else up_sum_ref
-        if complete is not None:
-            finish(complete)
-            complete = None
-        sum_ref[:, cols] = part if k == 0 else sum_ref[:, cols] + part
-        if k == groups - 1 and i >= groups:
-            complete = cols
+        for cols in spans:
+            part = jnp.dot(
+                x_ref[:, k * share : (k + 1) * share],
+                held_ref[i, :, cols],
+                preferred_element_type=jnp.float32,
+            )
+            if complete is not None:
+                finish(complete)
+            sum_ref[:, cols] = part if k == 0 else sum_ref[:, cols] + part
+            complete = cols if i == order[-1] else None
     finish(complete)
     loads[-1].wait()
 
@@ -297,29 +302,24 @@
     block = tile_of(share, 512)
     steps = share // block
     small_spec = pl.BlockSpec((top, count), lambda c, g: (0, 0))
-    picks = pl.pallas_call(
-        functools.partial(pick_scaled, experts, cap, groups),
-        out_shape=(
-            pltpu.VMEM((groups * slots, groups * count), jnp.bfloat16),
-            pltpu.VMEM((groups * slots, LANES), jnp.float32),
-        ),
-        compiler_params=params,
-        name="pick_scaled",
-    )(in_hbm(routes_t), *routes_all[1:], in_hbm(gates_own), *gates_all[1:])
     scaled = pl.pallas_call(
-        dispatch_scaled,
+        functools.partial(dispatch_scaled, experts, cap, groups),
         out_shape=pltpu.HBM((groups * slots, share), jnp.bfloat16),
         grid_spec=pltpu.PrefetchScalarGridSpec(
             num_scalar_prefetch=1,
             grid=(steps,),
-            in_specs=[pl.BlockSpec(memory_space=pltpu.VMEM)] * 2
+            in_specs=[small_spec] * (2 * groups)
             + [pl.BlockSpec((count, block), lambda c, g: (0, g[0] * steps + c))]
             + [pl.BlockSpec((count, block), lambda c, g: (0, c))] * (groups - 1),
             out_specs=pl.BlockSpec((groups * slots, block), lambda c, g: (0, c)),
+            scratch_shapes=[
+                pltpu.VMEM((groups * slots, groups * count), jnp.bfloat16),
+                pltpu.VMEM((groups * slots, LANES), jnp.float32),
+            ],
         ),
         compiler_params=params,
         name="dispatch_scaled",
-    )(place, *picks, in_hbm(grad_out), *grads)
+    )(place, in_hbm(routes_t), *routes_all[1:], in_hbm(gates_own), *gates_all[1:], in_hbm(grad_out), *grads)
     scaled_rows = exchanged(scaled)
 
     sent, pos = pl.pallas_call(
@@ -391,7 +391,7 @@
         scratch_shapes=[
             pltpu.VMEM((slots, hidden), jnp.float32),
             pltpu.VMEM((slots, hidden), jnp.float32),
-            pltpu.SemaphoreType.DMA((hidden // tile_of(hidden, 256), 2 * groups)),
+            pltpu.SemaphoreType.DMA((2, 2 * groups)),
             pltpu.SemaphoreType.DMA((1,)),
         ],
         compiler_params=params,

time: 152 us -> 151 us (level)
  Pallas kernels: 27.8 us -> 25.5 us
    pallas_call x1, Pallas kernels: 8.58 us -> 6.97 us  [per_device(): pl.pallas_call(functools.partial(forward_kernel, groups), out_shape=[pltp...]
    pallas_call x2 -> x1, Pallas kernels: 4.36 us -> 3.69 us  [per_device(): pl.pallas_call(functools.partial(dispatch_scaled, experts, cap, groups),...]
  transfers between devices with their start and end apart: 10 -> 10, of which waited for: 6 -> 6; matrix products, arithmetic and copies ran while one was open for 7% -> 7% of each run, Pallas kernels for 14% -> 13%
where the time goes in v8:
time: 151 us; the launch traced here: 150 us
  waiting for transfers between devices  87.1 us (58%)
  starting transfers between devices  25.8 us (17%)
  Pallas kernels  25.5 us (17%)
  other arithmetic  5.12 us (3%)
  matrix products  4.19 us (3%)
  local copies, waits for them, and re-layouts  1.81 us (1%)
    all_to_all x3, waiting for transfers between devices, exchanged(): lax.all_to_all(split, 'expert', split_axis=0, concat_axis=0, axis_index_g...  42.3 us
    ppermute x1, waiting for transfers between devices, across(): return lax.ppermute(value, 'expert', pairs)  28 us
    all_to_all x3, starting transfers between devices, exchanged(): lax.all_to_all(split, 'expert', split_axis=0, concat_axis=0, axis_index_g...  19.8 us
    ppermute x6, waiting for transfers between devices, shifted(): lax.ppermute(value, 'dp', [(i, (i + by) % groups) for i in range(groups)])  16.8 us
    pallas_call x1, Pallas kernels, per_device(): pl.pallas_call(functools.partial(forward_kernel, groups), out_shape=[pltp...  6.97 us
    pallas_call x1, Pallas kernels, per_device(): pl.pallas_call(functools.partial(back_kernel, groups, cap), out_shape=[pl...  5.21 us
    dot_general x1, matrix products, contract_first(): lax.dot_general(left, right, (((0,), (0,)), ((), ())), preferred_element_...  4.19 us
    pallas_call x1, Pallas kernels, per_device(): pl.pallas_call(functools.partial(backward_kernel, groups, cap), out_shape...  4.17 us
  transfers between devices with their start and end apart: 10, of which 6 were waited for; matrix products, arithmetic and copies ran while one was open for 7% of the time, Pallas kernels for 13%

profile of v8, /device:TPU:11, one launch (start us, length us, event | category | flops | bytes accessed | tf_op | source)
XLA Modules:
  0.0 150.1 jit_solution(15891824512076971780)
XLA Ops:
  0.6 0.0 copy-start.1
  0.6 1.3 collective-permute-start.3
  1.9 0.2 collective-permute-start.2
  2.2 1.0 constant_dynamic-slice_fusion
  3.1 1.3 collective-permute-start.1
  4.4 0.7 bitcast_convert_fusion
  5.1 1.1 fusion.4
  6.2 2.4 %collective-permute-start = (bf16[144,2048]{1,0:T(8,128)(2,1)S(1)}, bf16[144,2048]{1,0:T(8,128)(2,1)S(1)}, u32[]{:S(2)}, u32[]{:S(2)}) collective-permute-start(bf16[144,2048]{1,0:T(8,128)(2,1)S(1)} %fusion.4), channel_id=1, source_target_pairs={{0,8},{1,9},{2,10},{3,11},{4,12},{5,13},{6,14},{7,15},{8,0},{9,1},... | collective-permute-start | bytes 1769480 | tf_op jit(solution)/shard_map/ppermute | solution.py:271
  8.6 3.3 %pad_maximum_fusion = bf16[2048,768]{1,0:T(8,128)(2,1)} fusion(bf16[1024,768]{1,0:T(8,128)(2,1)} %bitcast.28, bf16[1024,768]{1,0:T(8,128)(2,1)S(1)} %bitcast.27), kind=kLoop, calls=%fused_computation | loop fusion | flops 6291456 | bytes 6291456 | tf_op jit(solution)/shard_map/concatenate | solution.py:290
  11.9 0.0 collective-permute-done.3.refs_3_
  11.9 0.3 collective-permute-start.4
  12.2 0.1 pad_add_fusion.place_ref
  12.3 3.7 %dispatch_scaled.1 = bf16[768,1024]{1,0:T(8,128)(2,1)} custom-call(s32[2]{0:T(128)S(1)} %pad_add_fusion.place_ref, s32[2,128]{1,0:T(2,128)} %bitcast.33, s32[2,128]{1,0:T(2,128)S(1)} %collective-permute-done.2.refs_1_, f32[2,128]{1,0:T(2,128)} %bitcast.22, f32[2,128]{1,0:T(2,128)S(1)} %collective-permute-done.3.refs_3_, bf16[128,2048]{1,0:T(8,128)(2,1)} %refs_4_.1, ...), custom_call_target="tpu_custom_call" | custom-call | tf_op jit(solution)/shard_map/dispatch_scaled/pallas_call | solution.py:305
  15.9 7.1 %all-to-all-start.1 = ((bf16[16,48,1024]{2,1,0:T(8,128)(2,1)}), bf16[16,48,1024]{2,1,0:T(8,128)(2,1)S(1)}, u32[]{:S(2)}, u32[]{:S(2)}) async-start(bf16[16,48,1024]{2,1,0:T(8,128)(2,1)} %bitcast.25), calls=%async_computation.1 | async-start | bytes 3145728 | tf_op jit(solution)/shard_map/all_to_all | solution.py:276
  23.1 28.0 %collective-permute-done.refs_1_.refs_3_ = bf16[144,2048]{1,0:T(8,128)(2,1)S(1)} collective-permute-done((bf16[144,2048]{1,0:T(8,128)(2,1)S(1)}, bf16[144,2048]{1,0:T(8,128)(2,1)S(1)}, u32[]{:S(2)}, u32[]{:S(2)}) %collective-permute-start) | collective-permute-done | bytes 589856 | tf_op jit(solution)/shard_map/ppermute | solution.py:271
  51.1 0.8 copy-done.3
  51.9 3.6 %dispatch_tokens.1 = (bf16[384,2048]{1,0:T(8,128)(2,1)}, s32[2,128]{1,0:T(2,128)S(1)}) custom-call(s32[2]{0:T(128)S(1)} %pad_add_fusion.place_ref, s32[2,128]{1,0:T(2,128)} %bitcast.34, bf16[144,2048]{1,0:T(8,128)(2,1)} %copy-done.3, bf16[128,2048]{1,0:T(8,128)(2,1)} %refs_2_.1, bf16[144,2048]{1,0:T(8,128)(2,1)} %copy-done.3), custom_call_target="tpu_custom_call" | custom-call | flops 30000001024 | bytes 30000000 | tf_op jit(solution)/shard_map/dispatch_tokens/pallas_call | solution.py:325
  55.6 12.5 %all-to-all-done.1 = bf16[16,48,1024]{2,1,0:T(8,128)(2,1)S(1)} async-done(((bf16[16,48,1024]{2,1,0:T(8,128)(2,1)}), bf16[16,48,1024]{2,1,0:T(8,128)(2,1)S(1)}, u32[]{:S(2)}, u32[]{:S(2)}) %all-to-all-start.1) | async-done | bytes 1572896 | tf_op jit(solution)/shard_map/all_to_all | solution.py:276
  68.1 4.3 %all-to-all-start = ((bf16[8,48,2048]{2,1,0:T(8,128)(2,1)}), bf16[8,48,2048]{2,1,0:T(8,128)(2,1)S(1)}, u32[]{:S(2)}, u32[]{:S(2)}) async-start(bf16[8,48,2048]{2,1,0:T(8,128)(2,1)} %bitcast.30), calls=%async_computation | async-start | bytes 3145728 | tf_op jit(solution)/shard_map/all_to_all | solution.py:276
  72.4 5.2 %back.1 = (f32[384,768]{1,0:T(8,128)}, bf16[384,768]{1,0:T(8,128)(2,1)}, bf16[768,1024]{1,0:T(8,128)(2,1)}) custom-call(s32[2]{0:T(128)S(1)} %pad_add_fusion.place_ref, bf16[768,1024]{1,0:T(8,128)(2,1)S(1)} %bitcast.19, bf16[768,1024]{1,0:T(8,128)(2,1)} %bitcast.31), custom_call_target="tpu_custom_call" | custom-call | tf_op jit(solution)/shard_map/back/pallas_call | solution.py:368
  77.6 0.2 collective-permute-start.5
  77.8 2.3 %collective-permute-done.4.refs_0_ = bf16[2048,768]{1,0:T(8,128)(2,1)} collective-permute-done((bf16[2048,768]{1,0:T(8,128)(2,1)}, bf16[2048,768]{1,0:T(8,128)(2,1)}, u32[]{:S(2)}, u32[]{:S(2)}) %collective-permute-start.4) | collective-permute-done | bytes 3145760 | tf_op jit(solution)/shard_map/ppermute | solution.py:267
  80.1 10.4 %all-to-all-done = bf16[8,48,2048]{2,1,0:T(8,128)(2,1)S(1)} async-done(((bf16[8,48,2048]{2,1,0:T(8,128)(2,1)}), bf16[8,48,2048]{2,1,0:T(8,128)(2,1)S(1)}, u32[]{:S(2)}, u32[]{:S(2)}) %all-to-all-start) | async-done | bytes 1572896 | tf_op jit(solution)/shard_map/all_to_all | solution.py:276
  90.5 7.0 %forward.1 = (f32[384,768]{1,0:T(8,128)S(1)}, f32[384,768]{1,0:T(8,128)S(1)}, f32[384,768]{1,0:T(8,128)S(1)}, bf16[384,768]{1,0:T(8,128)(2,1)}, bf16[4,1024,768]...) custom-call(bf16[384,2048]{1,0:T(8,128)(2,1)S(1)} %bitcast.20, f32[384,768]{1,0:T(8,128)} %get-tuple-element.29.back_ref, ...), custom_call_target="tpu_custom_call" | custom-call | tf_op jit(solution)/shard_map/forward/pallas_call | solution.py:382
  97.5 0.0 collective-permute-done.5.refs_1_
  97.5 4.2 %backward.1 = bf16[384,2176]{1,0:T(8,128)(2,1)} custom-call(s32[2]{0:T(128)S(1)} %pad_add_fusion.place_ref, f32[384,768]{1,0:T(8,128)S(1)} %get-tuple-element.31.act_ref, f32[384,768]{1,0:T(8,128)S(1)} %get-tuple-element.32.slope_ref, f32[384,768]{1,0:T(8,128)S(1)} %get-tuple-element.33.value_ref, bf16[4,1024,768]{2,1,0:T(8,128)(2,1)S(1)} %get-tuple-element.34.held_ref, ...), custom_call_target="tpu_custom_call" | custom-call | tf_op jit(solution)/shard_map/backward/pallas_call | solution.py:402
  101.7 8.4 %all-to-all-start.2 = ((bf16[16,24,2176]{2,1,0:T(8,128)(2,1)}), bf16[16,24,2176]{2,1,0:T(8,128)(2,1)S(1)}, u32[]{:S(2)}, u32[]{:S(2)}) async-start(bf16[16,24,2176]{2,1,0:T(8,128)(2,1)} %bitcast.24), calls=%async_computation.2 | async-start | bytes 3342336 | tf_op jit(solution)/shard_map/all_to_all | solution.py:276
  110.0 0.2 collective-permute-start.6
  110.2 14.5 %collective-permute-done.6 = bf16[384,768]{1,0:T(8,128)(2,1)S(1)} collective-permute-done((bf16[384,768]{1,0:T(8,128)(2,1)}, bf16[384,768]{1,0:T(8,128)(2,1)S(1)}, u32[]{:S(2)}, u32[]{:S(2)}) %collective-permute-start.6) | collective-permute-done | bytes 589856 | tf_op jit(solution)/shard_map/ppermute | solution.py:267
  124.8 4.2 %convolution_bitcast_fusion = f32[1,768,1024]{2,1,0:T(8,128)} fusion(bf16[768,1024]{1,0:T(8,128)(2,1)S(1)} %copy-done.2, bf16[384,768]{1,0:T(8,128)(2,1)S(1)} %collective-permute-done.6, bf16[384,768]{1,0:T(8,128)(2,1)} %get-tuple-element.39), kind=kOutput, calls=%fused_computation.1 | convolution fusion | flops 1210318848 | bytes 5898240 | tf_op jit(solution)/shard_map/dot_general | solution.py:24
  129.0 19.3 %all-to-all-done.2 = bf16[16,24,2176]{2,1,0:T(8,128)(2,1)S(1)} async-done(((bf16[16,24,2176]{2,1,0:T(8,128)(2,1)}), bf16[16,24,2176]{2,1,0:T(8,128)(2,1)S(1)}, u32[]{:S(2)}, u32[]{:S(2)}) %all-to-all-start.2) | async-done | bytes 1671200 | tf_op jit(solution)/shard_map/all_to_all | solution.py:276
  148.3 1.8 %combine.1 = (bf16[128,2048]{1,0:T(8,128)(2,1)}, f32[2,128]{1,0:T(2,128)}) custom-call(s32[2]{0:T(128)S(1)} %pad_add_fusion.place_ref, s32[2,128]{1,0:T(2,128)S(1)} %get-tuple-element.22.pos_ref, f32[2,128]{1,0:T(2,128)S(1)} %bitcast.23, bf16[384,2176]{1,0:T(8,128)(2,1)S(1)} %bitcast.18), custom_call_target="tpu_custom_call" | custom-call | tf_op jit(solution)/shard_map/combine/pallas_call | solution.py:421
  (9 shorter events, 0.0 us)
Async XLA Ops:
  0.6 8.0 %copy-start.1 = (bf16[1,1024,768]{2,1,0:T(8,128)(2,1)S(1)}, bf16[1,1024,768]{2,1,0:T(8,128)(2,1)}, u32[]{:S(2)}) copy-start(bf16[1,1024,768]{2,1,0:T(8,128)(2,1)} %param.11) | copy-start | bytes 4718596
  0.6 11.2 %collective-permute-start.3 = (f32[2,128]{1,0:T(2,128)}, f32[2,128]{1,0:T(2,128)S(1)}, u32[]{:S(2)}, u32[]{:S(2)}) collective-permute-start(f32[2,128]{1,0:T(2,128)} %bitcast.21), channel_id=1, source_target_pairs={{0,16},{16,0},{1,17},{17,1},{2,18},{18,2},{3,19},{19,3},{4,20},{20... | collective-permute-start | bytes 3080 | tf_op jit(solution)/shard_map/ppermute | solution.py:267
  1.9 9.9 %collective-permute-start.2 = (s32[2,128]{1,0:T(2,128)}, s32[2,128]{1,0:T(2,128)S(1)}, u32[]{:S(2)}, u32[]{:S(2)}) collective-permute-start(s32[2,128]{1,0:T(2,128)} %bitcast.32), channel_id=1, source_target_pairs={{0,16},{16,0},{1,17},{17,1},{2,18},{18,2},{3,19},{19,3},{4,20},{20... | collective-permute-start | bytes 3080 | tf_op jit(solution)/shard_map/ppermute | solution.py:267
  3.1 8.7 %collective-permute-start.1 = (bf16[128,1024]{1,0:T(8,128)(2,1)S(1)}, bf16[128,1024]{1,0:T(8,128)(2,1)S(1)}, u32[]{:S(2)}, u32[]{:S(2)}) collective-permute-start(bf16[128,1024]{1,0:T(8,128)(2,1)S(1)} %constant_dynamic-slice_fusion), channel_id=1, source_target_pairs={{0,16},{16,0},{1,17},{17,1},{2,18},{18,2},{3,19},{19,3},{4,20},{20... | collective-permute-start | bytes 786440 | tf_op jit(solution)/shard_map/ppermute | solution.py:267
  6.2 44.9 %collective-permute-start = (bf16[144,2048]{1,0:T(8,128)(2,1)S(1)}, bf16[144,2048]{1,0:T(8,128)(2,1)S(1)}, u32[]{:S(2)}, u32[]{:S(2)}) collective-permute-start(bf16[144,2048]{1,0:T(8,128)(2,1)S(1)} %fusion.4), channel_id=1, source_target_pairs={{0,8},{1,9},{2,10},{3,11},{4,12},{5,13},{6,14},{7,15},{8,0},{9,1},... | collective-permute-start | bytes 1769480 | tf_op jit(solution)/shard_map/ppermute | solution.py:271
  11.9 68.2 %collective-permute-start.4 = (bf16[2048,768]{1,0:T(8,128)(2,1)}, bf16[2048,768]{1,0:T(8,128)(2,1)}, u32[]{:S(2)}, u32[]{:S(2)}) collective-permute-start(bf16[2048,768]{1,0:T(8,128)(2,1)} %pad_maximum_fusion), channel_id=1, source_target_pairs={{0,16},{16,0},{1,17},{17,1},{2,18},{18,2},{3,19},{19,3},{4,20},{20... | collective-permute-start | bytes 9437192 | tf_op jit(solution)/shard_map/ppermute | solution.py:267
  15.9 52.1 %all-to-all-start.1 = ((bf16[16,48,1024]{2,1,0:T(8,128)(2,1)}), bf16[16,48,1024]{2,1,0:T(8,128)(2,1)S(1)}, u32[]{:S(2)}, u32[]{:S(2)}) async-start(bf16[16,48,1024]{2,1,0:T(8,128)(2,1)} %bitcast.25), calls=%async_computation.1 | async-start | bytes 3145728 | tf_op jit(solution)/shard_map/all_to_all | solution.py:276
  51.1 0.8 copy-start.3
  68.1 22.4 %all-to-all-start = ((bf16[8,48,2048]{2,1,0:T(8,128)(2,1)}), bf16[8,48,2048]{2,1,0:T(8,128)(2,1)S(1)}, u32[]{:S(2)}, u32[]{:S(2)}) async-start(bf16[8,48,2048]{2,1,0:T(8,128)(2,1)} %bitcast.30), calls=%async_computation | async-start | bytes 3145728 | tf_op jit(solution)/shard_map/all_to_all | solution.py:276
  77.6 19.9 %collective-permute-start.5 = (bf16[384,768]{1,0:T(8,128)(2,1)}, bf16[384,768]{1,0:T(8,128)(2,1)S(1)}, u32[]{:S(2)}, u32[]{:S(2)}) collective-permute-start(bf16[384,768]{1,0:T(8,128)(2,1)} %get-tuple-element.36), channel_id=1, source_target_pairs={{0,16},{16,0},{1,17},{17,1},{2,18},{18,2},{3,19},{19,3},{4,20},{20... | collective-permute-start | bytes 1769480 | tf_op jit(solution)/shard_map/ppermute | solution.py:267
  101.7 23.1 %copy-start.2 = (bf16[768,1024]{1,0:T(8,128)(2,1)S(1)}, bf16[768,1024]{1,0:T(8,128)(2,1)}, u32[]{:S(2)}) copy-start(bf16[768,1024]{1,0:T(8,128)(2,1)} %get-tuple-element.40) | copy-start | bytes 4718596
  101.7 46.7 %all-to-all-start.2 = ((bf16[16,24,2176]{2,1,0:T(8,128)(2,1)}), bf16[16,24,2176]{2,1,0:T(8,128)(2,1)S(1)}, u32[]{:S(2)}, u32[]{:S(2)}) async-start(bf16[16,24,2176]{2,1,0:T(8,128)(2,1)} %bitcast.24), calls=%async_computation.2 | async-start | bytes 3342336 | tf_op jit(solution)/shard_map/all_to_all | solution.py:276
  110.0 14.8 %collective-permute-start.6 = (bf16[384,768]{1,0:T(8,128)(2,1)}, bf16[384,768]{1,0:T(8,128)(2,1)S(1)}, u32[]{:S(2)}, u32[]{:S(2)}) collective-permute-start(bf16[384,768]{1,0:T(8,128)(2,1)} %get-tuple-element.39), channel_id=1, source_target_pairs={{0,16},{16,0},{1,17},{17,1},{2,18},{18,2},{3,19},{19,3},{4,20},{20... | collective-permute-start | bytes 1769480 | tf_op jit(solution)/shard_map/ppermute | solution.py:267
  124.8 23.5 %copy-start = (f32[128,2]{0,1:T(2,128)S(1)}, f32[128,2]{0,1:T(2,128)}, u32[]{:S(2)}) copy-start(f32[128,2]{0,1:T(2,128)} %param.9) | copy-start | bytes 3076

commit v9 on v8

--- a/solution.py
+++ b/solution.py
@@ -9,7 +9,6 @@
 
 LANES = 128
 VMEM_BYTES = 24 * 1024 * 1024
-TAIL = 16
 READY_COST_US = 30
 TOKENS_COST_US = 30
 
@@ -66,14 +65,12 @@
 def dispatch_tokens(experts, cap, place_ref, *refs):
     routes_refs, tokens_refs, (out_ref, pos_ref, pick_ref) = refs[:2], refs[2:4], refs[4:]
     count = tokens_refs[0].shape[0]
-    top = pos_ref.shape[0]
 
     @pl.when(pl.program_id(0) == 0)
     def _():
         rows = lax.broadcasted_iota(jnp.int32, (pick_ref.shape[0], count), 0)
         for c, ref in enumerate(routes_refs):
-            routes = ref[...].astype(jnp.float32).astype(jnp.int32)[:top, :count]
-            near = routes - place_ref[1] * (experts // 2)
+            near = ref[...] - place_ref[1] * (experts // 2)
             pos = slot_positions(near, experts // 2, 2 * cap, c * cap)
             pick_ref[:, c * count : (c + 1) * count] = sum(
                 jnp.where(rows == p, 1.0, 0.0) for p in pos
@@ -114,8 +111,21 @@
     out_ref[...] = (scale_ref[:, :1] * rows).astype(out_ref.dtype)
 
 
-def ready_kernel(*refs):
-    del refs
+def ready_kernel(gate_ref, *refs):
+    held_ref, sems = refs[-2:]
+    half = gate_ref.shape[0] // 2
+    copies = [
+        pltpu.make_async_copy(
+            gate_ref.at[n * half : (n + 1) * half],
+            held_ref.at[n * half : (n + 1) * half],
+            sems.at[n],
+        )
+        for n in range(2)
+    ]
+    for copy in copies:
+        copy.start()
+    for copy in copies:
+        copy.wait()
 
 
 def back_kernel(groups, cap, place_ref, rows_ref, down_ref, own_ref, *rest):
@@ -136,31 +146,30 @@
             ref[:, cols] = part.astype(ref.dtype)
 
 
-def forward_kernel(groups, x_ref, back_ref, *refs):
-    (own_gate, own_up), others = refs[:2], refs[2 : groups + 1]
-    act_ref, slope_ref, value_ref, hidden_ref, held_ref, kept_ref = refs[groups + 1 : groups + 7]
-    gate_sum_ref, up_sum_ref, sems, back_sem = refs[groups + 7 :]
-    share, hidden = held_ref.shape[1:]
+def forward_kernel(groups, x_ref, gate_ref, back_ref, own_up_ref, *refs):
+    others = refs[: groups - 1]
+    act_ref, slope_ref, value_ref, hidden_ref, held_ref, kept_ref = refs[groups - 1 : groups + 5]
+    gate_sum_ref, up_sum_ref, sems, back_sem = refs[groups + 5 :]
+    share, hidden = gate_ref.shape
     step = tile_of(hidden, 256)
-    gates = [own_gate, *[ref.at[:share] for ref in others]]
-    ups = [own_up, *[ref.at[share:] for ref in others]]
+    sources = [gate_ref, *[ref.at[:share] for ref in others]]
+    sources += [own_up_ref, *[ref.at[share:] for ref in others]]
     spans = [slice(at, at + step) for at in range(0, hidden, step)]
 
     order = [i for k in range(groups) for i in (k, groups + k)]
-    sources, part_rows = gates + ups, share // 2
-    loads = [
-        pltpu.make_async_copy(
-            sources[i].at[n * part_rows : (n + 1) * part_rows],
-            held_ref.at[i, n * part_rows : (n + 1) * part_rows],
-            sems.at[n, i],
-        )
-        for i in order
-        for n in range(2)
+    part_rows = share // 2
+    stages = [
+        [
+            pltpu.make_async_copy(
+                sources[i].at[n * part_rows : (n + 1) * part_rows],
+                held_ref.at[i - 1, n * part_rows : (n + 1) * part_rows],
+                sems.at[n, i - 1],
+            )
+            for n in range(2)
+        ]
+        for i in order[1:]
     ]
-    loads.append(pltpu.make_async_copy(back_ref, kept_ref, back_sem.at[0]))
-    flying = 2
-    for copy in loads[:flying]:
-        copy.start()
+    stages[-1].append(pltpu.make_async_copy(back_ref, kept_ref, back_sem.at[0]))
 
     def finish(cols):
         pre_gate, pre_up = gate_sum_ref[:, cols], up_sum_ref[:, cols]
@@ -175,15 +184,17 @@
     complete = None
     for at, i in enumerate(order):
         k = i % groups
-        for n in (2 * at, 2 * at + 1):
-            loads[n].wait()
-            if n + flying < len(loads):
-                loads[n + flying].start()
+        if at > 0:
+            for copy in stages[at - 1]:
+                copy.wait()
+        if at < len(stages):
+            for copy in stages[at]:
+                copy.start()
         sum_ref = gate_sum_ref if i < groups else up_sum_ref
         for cols in spans:
             part = jnp.dot(
                 x_ref[:, k * share : (k + 1) * share],
-                held_ref[i, :, cols],
+                gate_ref[:, cols] if i == 0 else held_ref[i - 1, :, cols],
                 preferred_element_type=jnp.float32,
             )
             if complete is not None:
@@ -191,15 +202,16 @@
             sum_ref[:, cols] = part if k == 0 else sum_ref[:, cols] + part
             complete = cols if i == order[-1] else None
     finish(complete)
-    loads[-1].wait()
-
-
-def backward_kernel(groups, cap, place_ref, act_ref, slope_ref, value_ref, held_ref, *refs):
+
+
+def backward_kernel(
+    groups, cap, half_ref, act_ref, slope_ref, value_ref, gate_ref, held_ref, *refs
+):
     parts, (out_ref, d_gate_ref, d_up_ref, rows_ref, out_sems) = refs[:groups], refs[groups:]
     share = held_ref.shape[1]
     width = groups * share
     block = tile_of(share, 512)
-    half = place_ref[1]
+    half = half_ref[0]
     back = sum(part[...].astype(jnp.float32) for part in parts)
     score = jnp.sum(back * value_ref[...], axis=1, keepdims=True)
     d_gate_ref[...] = by_half(back * slope_ref[...], cap, half, True).astype(jnp.bfloat16)
@@ -219,8 +231,9 @@
     for k in range(groups):
         for at in range(0, share, block):
             cols = slice(k * share + at, k * share + at + block)
-            grad = contract_last(d_gate_ref[...], held_ref[k, at : at + block])
-            grad += contract_last(d_up_ref[...], held_ref[groups + k, at : at + block])
+            gate = gate_ref[at : at + block] if k == 0 else held_ref[k - 1, at : at + block]
+            grad = contract_last(d_gate_ref[...], gate)
+            grad += contract_last(d_up_ref[...], held_ref[groups - 1 + k, at : at + block])
             rows_ref[:, cols] = grad.astype(rows_ref.dtype)
             send(cols)
     for copy in outs:
@@ -261,6 +274,7 @@
     params = pltpu.CompilerParams(vmem_limit_bytes=VMEM_BYTES)
     half = lax.div(lax.axis_index("expert"), experts // 2)
     place = jnp.stack([group, half]).astype(jnp.int32)
+    place_group, place_half = group.reshape(1), half.reshape(1)
     halves = [list(range(experts // 2)), list(range(experts // 2, experts))]
 
     def shifted(value, by):
@@ -292,8 +306,9 @@
     both, grads, routes_all, gates_all = lax.optimization_barrier(
         (both, grads, routes_all, gates_all)
     )
-    tail = jnp.pad(routes_t.astype(tokens.dtype), ((0, TAIL - top), (0, width - count)))
-    tokens_across = across(jnp.concatenate([tokens, tail], axis=0))
+    routes_across = across(routes_t)
+    tokens_sent, routes_across = lax.optimization_barrier((tokens, routes_across))
+    tokens_across = across(tokens_sent)
     weights_moved = [shifted(both, k) for k in range(1, groups)]
 
     def in_hbm(value):
@@ -319,7 +334,15 @@
         ),
         compiler_params=params,
         name="dispatch_scaled",
-    )(place, in_hbm(routes_t), *routes_all[1:], in_hbm(gates_own), *gates_all[1:], in_hbm(grad_out), *grads)
+    )(
+        place_group,
+        in_hbm(routes_t),
+        *routes_all[1:],
+        in_hbm(gates_own),
+        *gates_all[1:],
+        in_hbm(grad_out),
+        *grads,
+    )
     scaled_rows = exchanged(scaled)
 
     sent, pos = pl.pallas_call(
@@ -331,7 +354,7 @@
         grid_spec=pltpu.PrefetchScalarGridSpec(
             num_scalar_prefetch=1,
             grid=(groups,),
-            in_specs=[small_spec, pl.BlockSpec((TAIL, LANES), lambda k, g: (count // TAIL, 0))]
+            in_specs=[small_spec] * 2
             + [
                 pl.BlockSpec(
                     (count, share), lambda k, g: (0, lax.rem(g[0] - k + groups, groups))
@@ -346,22 +369,25 @@
         ),
         compiler_params=params,
         name="dispatch_tokens",
-    )(place, in_hbm(routes_t), tokens_across, in_hbm(tokens), in_hbm(tokens_across))
+    )(place, in_hbm(routes_t), routes_across, in_hbm(tokens), in_hbm(tokens_across))
     x_rows = exchanged(sent, halves)
 
-    weights_moved = pl.pallas_call(
+    any_spec = pl.BlockSpec(memory_space=pl.ANY)
+    whole_spec = pl.BlockSpec(memory_space=pltpu.VMEM)
+    *weights_moved, gate_held = pl.pallas_call(
         ready_kernel,
-        out_shape=[pltpu.HBM(value.shape, value.dtype) for value in weights_moved],
-        in_specs=[pl.BlockSpec(memory_space=pl.ANY)] * (groups - 1),
-        out_specs=[pl.BlockSpec(memory_space=pl.ANY)] * (groups - 1),
-        input_output_aliases={k: k for k in range(groups - 1)},
+        out_shape=[pltpu.HBM(value.shape, value.dtype) for value in weights_moved]
+        + [pltpu.VMEM((share, hidden), jnp.bfloat16)],
+        in_specs=[any_spec] * groups,
+        out_specs=[any_spec] * (groups - 1) + [whole_spec],
+        input_output_aliases={k + 1: k for k in range(groups - 1)},
+        scratch_shapes=[pltpu.SemaphoreType.DMA((2,))],
         cost_estimate=pl.CostEstimate(
             flops=READY_COST_US * 10**9, bytes_accessed=READY_COST_US * 10**6, transcendentals=0
         ),
         compiler_params=params,
         name="ready",
-    )(*[in_hbm(value) for value in weights_moved])
-    weights = [w_gate[0], w_up[0], *weights_moved]
+    )(in_hbm(w_gate[0]), *[in_hbm(value) for value in weights_moved])
 
     place_spec = pl.BlockSpec(memory_space=pltpu.SMEM)
 
@@ -377,32 +403,30 @@
     scaled_all = rest[-1]
     back_parts = [shifted(rest[k - 1], -k) for k in range(1, groups)]
 
-    whole_spec = pl.BlockSpec(memory_space=pltpu.VMEM)
-    any_spec = pl.BlockSpec(memory_space=pl.ANY)
     *factors, hidden_own, held, back_kept = pl.pallas_call(
         functools.partial(forward_kernel, groups),
         out_shape=[pltpu.VMEM((slots, hidden), jnp.float32)] * 3
         + [
             pltpu.HBM((slots, hidden), jnp.bfloat16),
-            pltpu.VMEM((2 * groups, share, hidden), jnp.bfloat16),
+            pltpu.VMEM((2 * groups - 1, share, hidden), jnp.bfloat16),
             pltpu.VMEM((slots, hidden), jnp.float32),
         ],
-        in_specs=[whole_spec] + [any_spec] * (groups + 2),
+        in_specs=[whole_spec] * 2 + [any_spec] * (groups + 1),
         scratch_shapes=[
             pltpu.VMEM((slots, hidden), jnp.float32),
             pltpu.VMEM((slots, hidden), jnp.float32),
-            pltpu.SemaphoreType.DMA((2, 2 * groups)),
+            pltpu.SemaphoreType.DMA((2, 2 * groups - 1)),
             pltpu.SemaphoreType.DMA((1,)),
         ],
         compiler_params=params,
         name="forward",
-    )(x_rows, in_hbm(back_own), *[in_hbm(value) for value in weights])
+    )(x_rows, gate_held, in_hbm(back_own), in_hbm(w_up[0]), *[in_hbm(w) for w in weights_moved])
 
     pieces = groups * (share // tile_of(share, 512))
     returning = pl.pallas_call(
         functools.partial(backward_kernel, groups, cap),
         out_shape=pltpu.HBM((slots, width + LANES), jnp.bfloat16),
-        in_specs=[place_spec] + [whole_spec] * (4 + groups),
+        in_specs=[place_spec] + [whole_spec] * (5 + groups),
         out_specs=any_spec,
         scratch_shapes=[
             pltpu.VMEM((slots, hidden), jnp.bfloat16),
@@ -412,7 +436,7 @@
         ],
         compiler_params=params,
         name="backward",
-    )(place, *factors, held, back_kept, *back_parts)
+    )(place_half, *factors, gate_held, held, back_kept, *back_parts)
     returned = exchanged(returning)
 
     hiddens = [hidden_own] + [shifted(hidden_own, k) for k in range(1, groups)]
@@ -427,7 +451,7 @@
         in_specs=[pl.BlockSpec(memory_space=pltpu.SMEM)] + [whole_spec] * 3,
         compiler_params=params,
         name="combine",
-    )(place, pos, gates_t, returned)
+    )(place_group, pos, gates_t, returned)
     return (grad_tokens, jnp.transpose(grad_gates), grad_down)
 
 

time: 151 us -> 147 us (0.974)
  waiting for transfers between devices: 87.1 us -> 84.2 us
    ppermute x1 -> x2, waiting for transfers between devices: 28 us -> 24.8 us  [across(): return lax.ppermute(value, 'expert', pairs)]
    ppermute x6, waiting for transfers between devices: 16.8 us -> 18.8 us  [shifted(): lax.ppermute(value, 'dp', [(i, (i + by) % groups) for i in range(groups)])]
    all_to_all x3, starting transfers between devices: 19.8 us -> 17.9 us  [exchanged(): lax.all_to_all(split, 'expert', split_axis=0, concat_axis=0, axis_index_g...]
    all_to_all x3, waiting for transfers between devices: 42.3 us -> 40.6 us  [exchanged(): lax.all_to_all(split, 'expert', split_axis=0, concat_axis=0, axis_index_g...]
    ppermute x1 -> x2, starting transfers between devices: 2.37 us -> 3.33 us  [across(): return lax.ppermute(value, 'expert', pairs)]
  transfers between devices with their start and end apart: 10 -> 11, of which waited for: 6 -> 7; matrix products, arithmetic and copies ran while one was open for 7% -> 6% of each run, Pallas kernels for 13% -> 14%
where the time goes in v9:
time: 147 us; the launch traced here: 146 us
  waiting for transfers between devices  84.2 us (57%)
  Pallas kernels  25.9 us (18%)
  starting transfers between devices  25.7 us (17%)
  matrix products  4.19 us (3%)
  other arithmetic  3.82 us (3%)
  local copies, waits for them, and re-layouts  1.77 us (1%)
    all_to_all x3, waiting for transfers between devices, exchanged(): lax.all_to_all(split, 'expert', split_axis=0, concat_axis=0, axis_index_g...  40.6 us
    ppermute x2, waiting for transfers between devices, across(): return lax.ppermute(value, 'expert', pairs)  24.8 us
    ppermute x6, waiting for transfers between devices, shifted(): lax.ppermute(value, 'dp', [(i, (i + by) % groups) for i in range(groups)])  18.8 us
    all_to_all x3, starting transfers between devices, exchanged(): lax.all_to_all(split, 'expert', split_axis=0, concat_axis=0, axis_index_g...  17.9 us
    pallas_call x1, Pallas kernels, per_device(): pl.pallas_call(functools.partial(forward_kernel, groups), out_shape=[pltp...  6.53 us
    pallas_call x1, Pallas kernels, per_device(): pl.pallas_call(functools.partial(back_kernel, groups, cap), out_shape=[pl...  5.22 us
    pallas_call x1, Pallas kernels, per_device(): pl.pallas_call(functools.partial(backward_kernel, groups, cap), out_shape...  4.73 us
    ppermute x6, starting transfers between devices, shifted(): lax.ppermute(value, 'dp', [(i, (i + by) % groups) for i in range(groups)])  4.5 us
  transfers between devices with their start and end apart: 11, of which 7 were waited for; matrix products, arithmetic and copies ran while one was open for 6% of the time, Pallas kernels for 14%

profile of v9, /device:TPU:11, one launch (start us, length us, event | category | flops | bytes accessed | tf_op | source)
XLA Modules:
  0.0 146.3 jit_solution(13838299960783054832)
XLA Ops:
  0.6 1.3 collective-permute-start.3
  1.9 2.3 %collective-permute-start = (s32[2,128]{1,0:T(2,128)}, s32[2,128]{1,0:T(2,128)S(1)}, u32[]{:S(2)}, u32[]{:S(2)}) collective-permute-start(s32[2,128]{1,0:T(2,128)} %bitcast.32), channel_id=1, source_target_pairs={{0,8},{1,9},{2,10},{3,11},{4,12},{5,13},{6,14},{7,15},{8,0},{9,1},... | collective-permute-start | bytes 3080 | tf_op jit(solution)/shard_map/ppermute | solution.py:285
  4.2 0.2 collective-permute-start.4
  4.5 1.0 constant_dynamic-slice_fusion
  5.4 1.3 collective-permute-start.2
  6.7 0.0 collective-permute-done.refs_1_
  6.7 1.0 collective-permute-start.1
  7.8 3.7 %pad_maximum_fusion = bf16[2048,768]{1,0:T(8,128)(2,1)} fusion(bf16[1024,768]{1,0:T(8,128)(2,1)} %bitcast.25, bf16[1024,768]{1,0:T(8,128)(2,1)} %bitcast.29), kind=kLoop, calls=%fused_computation | loop fusion | flops 6291456 | bytes 6291456 | tf_op jit(solution)/shard_map/concatenate | solution.py:304
  11.5 0.0 collective-permute-done.3.refs_1_
  11.5 0.3 collective-permute-done.2.refs_5_
  11.8 1.2 collective-permute-start.5
  13.0 3.1 %dispatch_scaled.1 = bf16[768,1024]{1,0:T(8,128)(2,1)} custom-call(s32[1]{0:T(128)} %bitcast.place_ref, s32[2,128]{1,0:T(2,128)} %bitcast.33, s32[2,128]{1,0:T(2,128)S(1)} %collective-permute-done.3.refs_1_, f32[2,128]{1,0:T(2,128)} %bitcast.21, f32[2,128]{1,0:T(2,128)S(1)} %collective-permute-done.4.refs_3_, bf16[128,2048]{1,0:T(8,128)(2,1)} %refs_4_.1, ...), custom_call_target="tpu_custom_call" | custom-call | tf_op jit(solution)/shard_map/dispatch_scaled/pallas_call | solution.py:320
  16.2 6.6 %all-to-all-start.1 = ((bf16[16,48,1024]{2,1,0:T(8,128)(2,1)}), bf16[16,48,1024]{2,1,0:T(8,128)(2,1)S(1)}, u32[]{:S(2)}, u32[]{:S(2)}) async-start(bf16[16,48,1024]{2,1,0:T(8,128)(2,1)} %bitcast.24), calls=%async_computation.1 | async-start | bytes 3145728 | tf_op jit(solution)/shard_map/all_to_all | solution.py:290
  22.7 0.1 pad_add_fusion.place_ref
  22.8 24.8 %collective-permute-done.1.refs_3_ = bf16[128,2048]{1,0:T(8,128)(2,1)S(1)} collective-permute-done((bf16[128,2048]{1,0:T(8,128)(2,1)}, bf16[128,2048]{1,0:T(8,128)(2,1)S(1)}, u32[]{:S(2)}, u32[]{:S(2)}) %collective-permute-start.1) | collective-permute-done | bytes 524320 | tf_op jit(solution)/shard_map/ppermute | solution.py:285
  47.6 0.8 copy-done.2
  48.4 3.6 %dispatch_tokens.1 = (bf16[384,2048]{1,0:T(8,128)(2,1)}, s32[2,128]{1,0:T(2,128)S(1)}) custom-call(s32[2]{0:T(128)S(1)} %pad_add_fusion.place_ref, s32[2,128]{1,0:T(2,128)} %bitcast.34, s32[2,128]{1,0:T(2,128)S(1)} %collective-permute-done.refs_1_, bf16[128,2048]{1,0:T(8,128)(2,1)} %refs_2_.1, bf16[128,2048]{1,0:T(8,128)(2,1)} %copy-done.2), custom_call_target="tpu_custom_call" | custom-call | flops 30000001024 | bytes 30000000 | tf_op jit(solution)/shard_map/dispatch_tokens/pallas_call | solution.py:348
  52.0 13.9 %all-to-all-done.1 = bf16[16,48,1024]{2,1,0:T(8,128)(2,1)S(1)} async-done(((bf16[16,48,1024]{2,1,0:T(8,128)(2,1)}), bf16[16,48,1024]{2,1,0:T(8,128)(2,1)S(1)}, u32[]{:S(2)}, u32[]{:S(2)}) %all-to-all-start.1) | async-done | bytes 1572896 | tf_op jit(solution)/shard_map/all_to_all | solution.py:290
  65.9 4.0 %all-to-all-start = ((bf16[8,48,2048]{2,1,0:T(8,128)(2,1)}), bf16[8,48,2048]{2,1,0:T(8,128)(2,1)S(1)}, u32[]{:S(2)}, u32[]{:S(2)}) async-start(bf16[8,48,2048]{2,1,0:T(8,128)(2,1)} %bitcast.27), calls=%async_computation | async-start | bytes 3145728 | tf_op jit(solution)/shard_map/all_to_all | solution.py:290
  69.9 5.2 %back.1 = (f32[384,768]{1,0:T(8,128)}, bf16[384,768]{1,0:T(8,128)(2,1)}, bf16[768,1024]{1,0:T(8,128)(2,1)}) custom-call(s32[2]{0:T(128)S(1)} %pad_add_fusion.place_ref, bf16[768,1024]{1,0:T(8,128)(2,1)S(1)} %bitcast.18, bf16[768,1024]{1,0:T(8,128)(2,1)} %bitcast.28), custom_call_target="tpu_custom_call" | custom-call | tf_op jit(solution)/shard_map/back/pallas_call | solution.py:394
  75.1 0.2 collective-permute-start.6
  75.3 4.0 %collective-permute-done.5.refs_0_ = bf16[2048,768]{1,0:T(8,128)(2,1)} collective-permute-done((bf16[2048,768]{1,0:T(8,128)(2,1)}, bf16[2048,768]{1,0:T(8,128)(2,1)}, u32[]{:S(2)}, u32[]{:S(2)}) %collective-permute-start.5) | collective-permute-done | bytes 3145760 | tf_op jit(solution)/shard_map/ppermute | solution.py:281
  79.3 1.4 ready.1
  80.7 7.4 %all-to-all-done = bf16[8,48,2048]{2,1,0:T(8,128)(2,1)S(1)} async-done(((bf16[8,48,2048]{2,1,0:T(8,128)(2,1)}), bf16[8,48,2048]{2,1,0:T(8,128)(2,1)S(1)}, u32[]{:S(2)}, u32[]{:S(2)}) %all-to-all-start) | async-done | bytes 1572896 | tf_op jit(solution)/shard_map/all_to_all | solution.py:290
  88.1 6.5 %forward.1 = (f32[384,768]{1,0:T(8,128)S(1)}, f32[384,768]{1,0:T(8,128)S(1)}, f32[384,768]{1,0:T(8,128)S(1)}, bf16[384,768]{1,0:T(8,128)(2,1)}, bf16[3,1024,768]...) custom-call(bf16[384,2048]{1,0:T(8,128)(2,1)S(1)} %bitcast.19, bf16[1024,768]{1,0:T(8,128)(2,1)S(1)} %get-tuple-element.32.gate_ref, ...), custom_call_target="tpu_custom_call" | custom-call | tf_op jit(solution)/shard_map/forward/pallas_call | solution.py:406
  94.6 4.7 %backward.1 = bf16[384,2176]{1,0:T(8,128)(2,1)} custom-call(s32[1]{0:T(128)} %bitcast.1.half_ref, f32[384,768]{1,0:T(8,128)S(1)} %get-tuple-element.39.act_ref, f32[384,768]{1,0:T(8,128)S(1)} %get-tuple-element.40.slope_ref, f32[384,768]{1,0:T(8,128)S(1)} %get-tuple-element.41.value_ref, bf16[1024,768]{1,0:T(8,128)(2,1)S(1)} %get-tuple-element.32.gate_ref, ...), custom_call_target="tpu_custom_call" | custom-call | tf_op jit(solution)/shard_map/backward/pallas_call | solution.py:426
  99.4 7.3 %all-to-all-start.2 = ((bf16[16,24,2176]{2,1,0:T(8,128)(2,1)}), bf16[16,24,2176]{2,1,0:T(8,128)(2,1)S(1)}, u32[]{:S(2)}, u32[]{:S(2)}) async-start(bf16[16,24,2176]{2,1,0:T(8,128)(2,1)} %bitcast.23), calls=%async_computation.2 | async-start | bytes 3342336 | tf_op jit(solution)/shard_map/all_to_all | solution.py:290
  106.7 0.2 collective-permute-start.7
  107.0 14.5 %collective-permute-done.7 = bf16[384,768]{1,0:T(8,128)(2,1)S(1)} collective-permute-done((bf16[384,768]{1,0:T(8,128)(2,1)}, bf16[384,768]{1,0:T(8,128)(2,1)S(1)}, u32[]{:S(2)}, u32[]{:S(2)}) %collective-permute-start.7) | collective-permute-done | bytes 589856 | tf_op jit(solution)/shard_map/ppermute | solution.py:281
  121.5 4.2 %convolution_bitcast_fusion = f32[1,768,1024]{2,1,0:T(8,128)} fusion(bf16[768,1024]{1,0:T(8,128)(2,1)S(1)} %copy-done.1, bf16[384,768]{1,0:T(8,128)(2,1)S(1)} %collective-permute-done.7, bf16[384,768]{1,0:T(8,128)(2,1)} %get-tuple-element.47), kind=kOutput, calls=%fused_computation.1 | convolution fusion | flops 1210318848 | bytes 5898240 | tf_op jit(solution)/shard_map/dot_general | solution.py:23
  125.7 19.3 %all-to-all-done.2 = bf16[16,24,2176]{2,1,0:T(8,128)(2,1)S(1)} async-done(((bf16[16,24,2176]{2,1,0:T(8,128)(2,1)}), bf16[16,24,2176]{2,1,0:T(8,128)(2,1)S(1)}, u32[]{:S(2)}, u32[]{:S(2)}) %all-to-all-start.2) | async-done | bytes 1671200 | tf_op jit(solution)/shard_map/all_to_all | solution.py:290
  145.0 1.3 combine.1
  (7 shorter events, 0.0 us)
Async XLA Ops:
  0.6 10.9 %collective-permute-start.3 = (s32[2,128]{1,0:T(2,128)}, s32[2,128]{1,0:T(2,128)S(1)}, u32[]{:S(2)}, u32[]{:S(2)}) collective-permute-start(s32[2,128]{1,0:T(2,128)} %bitcast.31), channel_id=1, source_target_pairs={{0,16},{16,0},{1,17},{17,1},{2,18},{18,2},{3,19},{19,3},{4,20},{20... | collective-permute-start | bytes 3080 | tf_op jit(solution)/shard_map/ppermute | solution.py:281
  1.9 4.8 %collective-permute-start = (s32[2,128]{1,0:T(2,128)}, s32[2,128]{1,0:T(2,128)S(1)}, u32[]{:S(2)}, u32[]{:S(2)}) collective-permute-start(s32[2,128]{1,0:T(2,128)} %bitcast.32), channel_id=1, source_target_pairs={{0,8},{1,9},{2,10},{3,11},{4,12},{5,13},{6,14},{7,15},{8,0},{9,1},... | collective-permute-start | bytes 3080 | tf_op jit(solution)/shard_map/ppermute | solution.py:285
  4.2 7.3 %collective-permute-start.4 = (f32[2,128]{1,0:T(2,128)}, f32[2,128]{1,0:T(2,128)S(1)}, u32[]{:S(2)}, u32[]{:S(2)}) collective-permute-start(f32[2,128]{1,0:T(2,128)} %bitcast.20), channel_id=1, source_target_pairs={{0,16},{16,0},{1,17},{17,1},{2,18},{18,2},{3,19},{19,3},{4,20},{20... | collective-permute-start | bytes 3080 | tf_op jit(solution)/shard_map/ppermute | solution.py:281
  5.4 6.4 %collective-permute-start.2 = (bf16[128,1024]{1,0:T(8,128)(2,1)S(1)}, bf16[128,1024]{1,0:T(8,128)(2,1)S(1)}, u32[]{:S(2)}, u32[]{:S(2)}) collective-permute-start(bf16[128,1024]{1,0:T(8,128)(2,1)S(1)} %constant_dynamic-slice_fusion), channel_id=1, source_target_pairs={{0,16},{16,0},{1,17},{17,1},{2,18},{18,2},{3,19},{19,3},{4,20},{20... | collective-permute-start | bytes 786440 | tf_op jit(solution)/shard_map/ppermute | solution.py:281
  6.7 40.9 %collective-permute-start.1 = (bf16[128,2048]{1,0:T(8,128)(2,1)}, bf16[128,2048]{1,0:T(8,128)(2,1)S(1)}, u32[]{:S(2)}, u32[]{:S(2)}) collective-permute-start(bf16[128,2048]{1,0:T(8,128)(2,1)} %refs_2_.1), channel_id=1, source_target_pairs={{0,8},{1,9},{2,10},{3,11},{4,12},{5,13},{6,14},{7,15},{8,0},{9,1},... | collective-permute-start | bytes 1572872 | tf_op jit(solution)/shard_map/ppermute | solution.py:285
  11.8 67.5 %collective-permute-start.5 = (bf16[2048,768]{1,0:T(8,128)(2,1)}, bf16[2048,768]{1,0:T(8,128)(2,1)}, u32[]{:S(2)}, u32[]{:S(2)}) collective-permute-start(bf16[2048,768]{1,0:T(8,128)(2,1)} %pad_maximum_fusion), channel_id=1, source_target_pairs={{0,16},{16,0},{1,17},{17,1},{2,18},{18,2},{3,19},{19,3},{4,20},{20... | collective-permute-start | bytes 9437192 | tf_op jit(solution)/shard_map/ppermute | solution.py:281
  16.2 49.8 %all-to-all-start.1 = ((bf16[16,48,1024]{2,1,0:T(8,128)(2,1)}), bf16[16,48,1024]{2,1,0:T(8,128)(2,1)S(1)}, u32[]{:S(2)}, u32[]{:S(2)}) async-start(bf16[16,48,1024]{2,1,0:T(8,128)(2,1)} %bitcast.24), calls=%async_computation.1 | async-start | bytes 3145728 | tf_op jit(solution)/shard_map/all_to_all | solution.py:290
  47.6 0.8 copy-start.2
  65.9 22.2 %all-to-all-start = ((bf16[8,48,2048]{2,1,0:T(8,128)(2,1)}), bf16[8,48,2048]{2,1,0:T(8,128)(2,1)S(1)}, u32[]{:S(2)}, u32[]{:S(2)}) async-start(bf16[8,48,2048]{2,1,0:T(8,128)(2,1)} %bitcast.27), calls=%async_computation | async-start | bytes 3145728 | tf_op jit(solution)/shard_map/all_to_all | solution.py:290
  75.1 19.5 %collective-permute-start.6 = (bf16[384,768]{1,0:T(8,128)(2,1)}, bf16[384,768]{1,0:T(8,128)(2,1)}, u32[]{:S(2)}, u32[]{:S(2)}) collective-permute-start(bf16[384,768]{1,0:T(8,128)(2,1)} %get-tuple-element.44), channel_id=1, source_target_pairs={{0,16},{16,0},{1,17},{17,1},{2,18},{18,2},{3,19},{19,3},{4,20},{20... | collective-permute-start | bytes 1769480 | tf_op jit(solution)/shard_map/ppermute | solution.py:281
  99.4 22.1 %copy-start.1 = (bf16[768,1024]{1,0:T(8,128)(2,1)S(1)}, bf16[768,1024]{1,0:T(8,128)(2,1)}, u32[]{:S(2)}) copy-start(bf16[768,1024]{1,0:T(8,128)(2,1)} %get-tuple-element.48) | copy-start | bytes 4718596
  99.4 45.6 %all-to-all-start.2 = ((bf16[16,24,2176]{2,1,0:T(8,128)(2,1)}), bf16[16,24,2176]{2,1,0:T(8,128)(2,1)S(1)}, u32[]{:S(2)}, u32[]{:S(2)}) async-start(bf16[16,24,2176]{2,1,0:T(8,128)(2,1)} %bitcast.23), calls=%async_computation.2 | async-start | bytes 3342336 | tf_op jit(solution)/shard_map/all_to_all | solution.py:290
  106.7 14.8 %collective-permute-start.7 = (bf16[384,768]{1,0:T(8,128)(2,1)}, bf16[384,768]{1,0:T(8,128)(2,1)S(1)}, u32[]{:S(2)}, u32[]{:S(2)}) collective-permute-start(bf16[384,768]{1,0:T(8,128)(2,1)} %get-tuple-element.47), channel_id=1, source_target_pairs={{0,16},{16,0},{1,17},{17,1},{2,18},{18,2},{3,19},{19,3},{4,20},{20... | collective-permute-start | bytes 1769480 | tf_op jit(solution)/shard_map/ppermute | solution.py:281
  121.5 23.5 %copy-start = (f32[128,2]{0,1:T(2,128)S(1)}, f32[128,2]{0,1:T(2,128)}, u32[]{:S(2)}) copy-start(f32[128,2]{0,1:T(2,128)} %param.9) | copy-start | bytes 3076

commit v10 on v9

--- a/solution.py
+++ b/solution.py
@@ -86,29 +86,35 @@
 
 def dispatch_scaled(experts, cap, groups, place_ref, *refs):
     routes_refs, gate_refs = refs[:groups], refs[groups : 2 * groups]
-    grad_refs, (out_ref, pick_ref, scale_ref) = refs[2 * groups : 3 * groups], refs[3 * groups :]
-    count = grad_refs[0].shape[0]
-    slots = out_ref.shape[0]
-
-    @pl.when(pl.program_id(0) == 0)
+    grad_refs, (out_ref, pos_ref) = refs[2 * groups : 3 * groups], refs[3 * groups :]
+    top, count = routes_refs[0].shape
+    step = pl.program_id(0)
+
+    @pl.when(step == 0)
     def _():
-        rows = lax.broadcasted_iota(jnp.int32, (slots, count), 0)
-        total = jnp.zeros((slots, 1), jnp.float32)
         for q in range(groups):
             pos = slot_positions(routes_refs[q][...], experts, groups * cap, q * cap)
-            hit = jnp.zeros((slots, count), jnp.float32)
-            weight = jnp.zeros((slots, count), jnp.float32)
             for k, p in enumerate(pos):
-                here = rows == p
-                hit = hit + jnp.where(here, 1.0, 0.0)
-                weight = weight + jnp.where(here, gate_refs[q][k : k + 1, :], 0.0)
-            pick_ref[:, q * count : (q + 1) * count] = hit.astype(jnp.bfloat16)
-            total = total + jnp.sum(weight, axis=1, keepdims=True)
-        scale_ref[...] = jnp.broadcast_to(total, scale_ref.shape)
-
+                pos_ref[q * top + k : q * top + k + 1, :] = p
+
+    block = out_ref.shape[0]
+    rows = lax.broadcasted_iota(jnp.int32, (block, count), 0) + step * block
+    total = jnp.zeros((block, 1), jnp.float32)
+    picks = []
+    for q in range(groups):
+        hit = jnp.zeros((block, count), jnp.float32)
+        weight = jnp.zeros((block, count), jnp.float32)
+        for k in range(top):
+            here = rows == pos_ref[q * top + k : q * top + k + 1, :]
+            hit = hit + jnp.where(here, 1.0, 0.0)
+            weight = weight + jnp.where(here, gate_refs[q][k : k + 1, :], 0.0)
+        picks.append(hit.astype(jnp.bfloat16))
+        total = total + jnp.sum(weight, axis=1, keepdims=True)
     grads = jnp.concatenate([ref[...] for ref in grad_refs], axis=0)
-    rows = jnp.dot(pick_ref[...], grads, preferred_element_type=jnp.float32)
-    out_ref[...] = (scale_ref[:, :1] * rows).astype(out_ref.dtype)
+    picked = jnp.dot(
+        jnp.concatenate(picks, axis=1), grads, preferred_element_type=jnp.float32
+    )
+    out_ref[...] = (total * picked).astype(out_ref.dtype)
 
 
 def ready_kernel(gate_ref, *refs):
@@ -181,15 +187,19 @@
         value_ref[:, cols] = hidden_f
         hidden_ref[:, cols] = hidden_f.astype(hidden_ref.dtype)
 
+    ahead = 2
+    for copies in stages[:ahead]:
+        for copy in copies:
+            copy.start()
     complete = None
     for at, i in enumerate(order):
         k = i % groups
         if at > 0:
             for copy in stages[at - 1]:
                 copy.wait()
-        if at < len(stages):
-            for copy in stages[at]:
-                copy.start()
+            if at - 1 + ahead < len(stages):
+                for copy in stages[at - 1 + ahead]:
+                    copy.start()
         sum_ref = gate_sum_ref if i < groups else up_sum_ref
         for cols in spans:
             part = jnp.dot(
@@ -314,8 +324,8 @@
     def in_hbm(value):
         return pltpu.with_memory_space_constraint(value, pltpu.HBM)
 
-    block = tile_of(share, 512)
-    steps = share // block
+    steps = 4
+    block = groups * slots // steps
     small_spec = pl.BlockSpec((top, count), lambda c, g: (0, 0))
     scaled = pl.pallas_call(
         functools.partial(dispatch_scaled, experts, cap, groups),
@@ -324,13 +334,10 @@
             num_scalar_prefetch=1,
             grid=(steps,),
             in_specs=[small_spec] * (2 * groups)
-            + [pl.BlockSpec((count, block), lambda c, g: (0, g[0] * steps + c))]
-            + [pl.BlockSpec((count, block), lambda c, g: (0, c))] * (groups - 1),
-            out_specs=pl.BlockSpec((groups * slots, block), lambda c, g: (0, c)),
-            scratch_shapes=[
-                pltpu.VMEM((groups * slots, groups * count), jnp.bfloat16),
-                pltpu.VMEM((groups * slots, LANES), jnp.float32),
-            ],
+            + [pl.BlockSpec((count, share), lambda c, g: (0, g[0]))]
+            + [pl.BlockSpec((count, share), lambda c, g: (0, 0))] * (groups - 1),
+            out_specs=pl.BlockSpec((block, share), lambda c, g: (c, 0)),
+            scratch_shapes=[pltpu.VMEM((groups * top, count), jnp.int32)],
         ),
         compiler_params=params,
         name="dispatch_scaled",

time: 147 us -> 146 us (level)
  transfers between devices with their start and end apart: 11 -> 11, of which waited for: 7 -> 7; matrix products, arithmetic and copies ran while one was open for 6% -> 6% of each run, Pallas kernels for 14% -> 13%
where the time goes in v10:
time: 146 us
  waiting for transfers between devices  83.8 us (57%)
  starting transfers between devices  25.7 us (18%)
  Pallas kernels  25.7 us (18%)
  matrix products  4.19 us (3%)
  other arithmetic  3.82 us (3%)
  local copies, waits for them, and re-layouts  1.77 us (1%)
    all_to_all x3, waiting for transfers between devices, exchanged(): lax.all_to_all(split, 'expert', split_axis=0, concat_axis=0, axis_index_g...  41 us
    ppermute x2, waiting for transfers between devices, across(): return lax.ppermute(value, 'expert', pairs)  24 us
    ppermute x6, waiting for transfers between devices, shifted(): lax.ppermute(value, 'dp', [(i, (i + by) % groups) for i in range(groups)])  18.8 us
    all_to_all x3, starting transfers between devices, exchanged(): lax.all_to_all(split, 'expert', split_axis=0, concat_axis=0, axis_index_g...  17.9 us
    pallas_call x1, Pallas kernels, per_device(): pl.pallas_call(functools.partial(forward_kernel, groups), out_shape=[pltp...  5.87 us
    pallas_call x1, Pallas kernels, per_device(): pl.pallas_call(functools.partial(back_kernel, groups, cap), out_shape=[pl...  5.22 us
    pallas_call x1, Pallas kernels, per_device(): pl.pallas_call(functools.partial(backward_kernel, groups, cap), out_shape...  4.73 us
    ppermute x6, starting transfers between devices, shifted(): lax.ppermute(value, 'dp', [(i, (i + by) % groups) for i in range(groups)])  4.51 us
  transfers between devices with their start and end apart: 11, of which 7 were waited for; matrix products, arithmetic and copies ran while one was open for 6% of the time, Pallas kernels for 13%

profile of v10, /device:TPU:11, one launch (start us, length us, event | category | flops | bytes accessed | tf_op | source)
XLA Modules:
  0.0 145.6 jit_solution(12357755124156470131)
XLA Ops:
  0.6 1.3 collective-permute-start.3
  1.9 2.3 %collective-permute-start = (s32[2,128]{1,0:T(2,128)}, s32[2,128]{1,0:T(2,128)S(1)}, u32[]{:S(2)}, u32[]{:S(2)}) collective-permute-start(s32[2,128]{1,0:T(2,128)} %bitcast.32), channel_id=1, source_target_pairs={{0,8},{1,9},{2,10},{3,11},{4,12},{5,13},{6,14},{7,15},{8,0},{9,1},... | collective-permute-start | bytes 3080 | tf_op jit(solution)/shard_map/ppermute | solution.py:295
  4.2 0.2 collective-permute-start.4
  4.5 1.0 constant_dynamic-slice_fusion
  5.4 1.3 collective-permute-start.2
  6.7 0.0 collective-permute-done.refs_1_
  6.7 1.0 collective-permute-start.1
  7.8 3.7 %pad_maximum_fusion = bf16[2048,768]{1,0:T(8,128)(2,1)} fusion(bf16[1024,768]{1,0:T(8,128)(2,1)} %bitcast.25, bf16[1024,768]{1,0:T(8,128)(2,1)} %bitcast.29), kind=kLoop, calls=%fused_computation | loop fusion | flops 6291456 | bytes 6291456 | tf_op jit(solution)/shard_map/concatenate | solution.py:314
  11.5 0.0 collective-permute-done.3.refs_1_
  11.5 0.3 collective-permute-done.2.refs_5_
  11.8 1.2 collective-permute-start.5
  13.0 3.6 %dispatch_scaled.1 = bf16[768,1024]{1,0:T(8,128)(2,1)} custom-call(s32[1]{0:T(128)} %bitcast.place_ref, s32[2,128]{1,0:T(2,128)} %bitcast.33, s32[2,128]{1,0:T(2,128)S(1)} %collective-permute-done.3.refs_1_, f32[2,128]{1,0:T(2,128)} %bitcast.21, f32[2,128]{1,0:T(2,128)S(1)} %collective-permute-done.4.refs_3_, bf16[128,2048]{1,0:T(8,128)(2,1)} %refs_4_.1, ...), custom_call_target="tpu_custom_call" | custom-call | tf_op jit(solution)/shard_map/dispatch_scaled/pallas_call | solution.py:330
  16.6 6.6 %all-to-all-start.1 = ((bf16[16,48,1024]{2,1,0:T(8,128)(2,1)}), bf16[16,48,1024]{2,1,0:T(8,128)(2,1)S(1)}, u32[]{:S(2)}, u32[]{:S(2)}) async-start(bf16[16,48,1024]{2,1,0:T(8,128)(2,1)} %bitcast.24), calls=%async_computation.1 | async-start | bytes 3145728 | tf_op jit(solution)/shard_map/all_to_all | solution.py:300
  23.2 0.1 pad_add_fusion.place_ref
  23.2 24.0 %collective-permute-done.1.refs_3_ = bf16[128,2048]{1,0:T(8,128)(2,1)S(1)} collective-permute-done((bf16[128,2048]{1,0:T(8,128)(2,1)}, bf16[128,2048]{1,0:T(8,128)(2,1)S(1)}, u32[]{:S(2)}, u32[]{:S(2)}) %collective-permute-start.1) | collective-permute-done | bytes 524320 | tf_op jit(solution)/shard_map/ppermute | solution.py:295
  47.3 0.8 copy-done.2
  48.1 3.6 %dispatch_tokens.1 = (bf16[384,2048]{1,0:T(8,128)(2,1)}, s32[2,128]{1,0:T(2,128)S(1)}) custom-call(s32[2]{0:T(128)S(1)} %pad_add_fusion.place_ref, s32[2,128]{1,0:T(2,128)} %bitcast.34, s32[2,128]{1,0:T(2,128)S(1)} %collective-permute-done.refs_1_, bf16[128,2048]{1,0:T(8,128)(2,1)} %refs_2_.1, bf16[128,2048]{1,0:T(8,128)(2,1)} %copy-done.2), custom_call_target="tpu_custom_call" | custom-call | flops 30000001024 | bytes 30000000 | tf_op jit(solution)/shard_map/dispatch_tokens/pallas_call | solution.py:355
  51.7 14.2 %all-to-all-done.1 = bf16[16,48,1024]{2,1,0:T(8,128)(2,1)S(1)} async-done(((bf16[16,48,1024]{2,1,0:T(8,128)(2,1)}), bf16[16,48,1024]{2,1,0:T(8,128)(2,1)S(1)}, u32[]{:S(2)}, u32[]{:S(2)}) %all-to-all-start.1) | async-done | bytes 1572896 | tf_op jit(solution)/shard_map/all_to_all | solution.py:300
  65.9 4.0 %all-to-all-start = ((bf16[8,48,2048]{2,1,0:T(8,128)(2,1)}), bf16[8,48,2048]{2,1,0:T(8,128)(2,1)S(1)}, u32[]{:S(2)}, u32[]{:S(2)}) async-start(bf16[8,48,2048]{2,1,0:T(8,128)(2,1)} %bitcast.27), calls=%async_computation | async-start | bytes 3145728 | tf_op jit(solution)/shard_map/all_to_all | solution.py:300
  69.9 5.2 %back.1 = (f32[384,768]{1,0:T(8,128)}, bf16[384,768]{1,0:T(8,128)(2,1)}, bf16[768,1024]{1,0:T(8,128)(2,1)}) custom-call(s32[2]{0:T(128)S(1)} %pad_add_fusion.place_ref, bf16[768,1024]{1,0:T(8,128)(2,1)S(1)} %bitcast.18, bf16[768,1024]{1,0:T(8,128)(2,1)} %bitcast.28), custom_call_target="tpu_custom_call" | custom-call | tf_op jit(solution)/shard_map/back/pallas_call | solution.py:401
  75.1 0.2 collective-permute-start.6
  75.3 4.0 %collective-permute-done.5.refs_0_ = bf16[2048,768]{1,0:T(8,128)(2,1)} collective-permute-done((bf16[2048,768]{1,0:T(8,128)(2,1)}, bf16[2048,768]{1,0:T(8,128)(2,1)}, u32[]{:S(2)}, u32[]{:S(2)}) %collective-permute-start.5) | collective-permute-done | bytes 3145760 | tf_op jit(solution)/shard_map/ppermute | solution.py:291
  79.3 1.4 ready.1
  80.7 7.4 %all-to-all-done = bf16[8,48,2048]{2,1,0:T(8,128)(2,1)S(1)} async-done(((bf16[8,48,2048]{2,1,0:T(8,128)(2,1)}), bf16[8,48,2048]{2,1,0:T(8,128)(2,1)S(1)}, u32[]{:S(2)}, u32[]{:S(2)}) %all-to-all-start) | async-done | bytes 1572896 | tf_op jit(solution)/shard_map/all_to_all | solution.py:300
  88.1 5.9 %forward.1 = (f32[384,768]{1,0:T(8,128)S(1)}, f32[384,768]{1,0:T(8,128)S(1)}, f32[384,768]{1,0:T(8,128)S(1)}, bf16[384,768]{1,0:T(8,128)(2,1)}, bf16[3,1024,768]...) custom-call(bf16[384,2048]{1,0:T(8,128)(2,1)S(1)} %bitcast.19, bf16[1024,768]{1,0:T(8,128)(2,1)S(1)} %get-tuple-element.32.gate_ref, ...), custom_call_target="tpu_custom_call" | custom-call | tf_op jit(solution)/shard_map/forward/pallas_call | solution.py:413
  94.0 4.7 %backward.1 = bf16[384,2176]{1,0:T(8,128)(2,1)} custom-call(s32[1]{0:T(128)} %bitcast.1.half_ref, f32[384,768]{1,0:T(8,128)S(1)} %get-tuple-element.39.act_ref, f32[384,768]{1,0:T(8,128)S(1)} %get-tuple-element.40.slope_ref, f32[384,768]{1,0:T(8,128)S(1)} %get-tuple-element.41.value_ref, bf16[1024,768]{1,0:T(8,128)(2,1)S(1)} %get-tuple-element.32.gate_ref, ...), custom_call_target="tpu_custom_call" | custom-call | tf_op jit(solution)/shard_map/backward/pallas_call | solution.py:433
  98.7 7.3 %all-to-all-start.2 = ((bf16[16,24,2176]{2,1,0:T(8,128)(2,1)}), bf16[16,24,2176]{2,1,0:T(8,128)(2,1)S(1)}, u32[]{:S(2)}, u32[]{:S(2)}) async-start(bf16[16,24,2176]{2,1,0:T(8,128)(2,1)} %bitcast.23), calls=%async_computation.2 | async-start | bytes 3342336 | tf_op jit(solution)/shard_map/all_to_all | solution.py:300
  106.1 0.2 collective-permute-start.7
  106.3 14.5 %collective-permute-done.7 = bf16[384,768]{1,0:T(8,128)(2,1)S(1)} collective-permute-done((bf16[384,768]{1,0:T(8,128)(2,1)}, bf16[384,768]{1,0:T(8,128)(2,1)S(1)}, u32[]{:S(2)}, u32[]{:S(2)}) %collective-permute-start.7) | collective-permute-done | bytes 589856 | tf_op jit(solution)/shard_map/ppermute | solution.py:291
  120.8 4.2 %convolution_bitcast_fusion = f32[1,768,1024]{2,1,0:T(8,128)} fusion(bf16[768,1024]{1,0:T(8,128)(2,1)S(1)} %copy-done.1, bf16[384,768]{1,0:T(8,128)(2,1)S(1)} %collective-permute-done.7, bf16[384,768]{1,0:T(8,128)(2,1)} %get-tuple-element.47), kind=kOutput, calls=%fused_computation.1 | convolution fusion | flops 1210318848 | bytes 5898240 | tf_op jit(solution)/shard_map/dot_general | solution.py:23
  125.0 19.3 %all-to-all-done.2 = bf16[16,24,2176]{2,1,0:T(8,128)(2,1)S(1)} async-done(((bf16[16,24,2176]{2,1,0:T(8,128)(2,1)}), bf16[16,24,2176]{2,1,0:T(8,128)(2,1)S(1)}, u32[]{:S(2)}, u32[]{:S(2)}) %all-to-all-start.2) | async-done | bytes 1671200 | tf_op jit(solution)/shard_map/all_to_all | solution.py:300
  144.4 1.3 combine.1
  (7 shorter events, 0.0 us)
Async XLA Ops:
  0.6 10.9 %collective-permute-start.3 = (s32[2,128]{1,0:T(2,128)}, s32[2,128]{1,0:T(2,128)S(1)}, u32[]{:S(2)}, u32[]{:S(2)}) collective-permute-start(s32[2,128]{1,0:T(2,128)} %bitcast.31), channel_id=1, source_target_pairs={{0,16},{16,0},{1,17},{17,1},{2,18},{18,2},{3,19},{19,3},{4,20},{20... | collective-permute-start | bytes 3080 | tf_op jit(solution)/shard_map/ppermute | solution.py:291
  1.9 4.8 %collective-permute-start = (s32[2,128]{1,0:T(2,128)}, s32[2,128]{1,0:T(2,128)S(1)}, u32[]{:S(2)}, u32[]{:S(2)}) collective-permute-start(s32[2,128]{1,0:T(2,128)} %bitcast.32), channel_id=1, source_target_pairs={{0,8},{1,9},{2,10},{3,11},{4,12},{5,13},{6,14},{7,15},{8,0},{9,1},... | collective-permute-start | bytes 3080 | tf_op jit(solution)/shard_map/ppermute | solution.py:295
  4.2 7.3 %collective-permute-start.4 = (f32[2,128]{1,0:T(2,128)}, f32[2,128]{1,0:T(2,128)S(1)}, u32[]{:S(2)}, u32[]{:S(2)}) collective-permute-start(f32[2,128]{1,0:T(2,128)} %bitcast.20), channel_id=1, source_target_pairs={{0,16},{16,0},{1,17},{17,1},{2,18},{18,2},{3,19},{19,3},{4,20},{20... | collective-permute-start | bytes 3080 | tf_op jit(solution)/shard_map/ppermute | solution.py:291
  5.4 6.4 %collective-permute-start.2 = (bf16[128,1024]{1,0:T(8,128)(2,1)S(1)}, bf16[128,1024]{1,0:T(8,128)(2,1)S(1)}, u32[]{:S(2)}, u32[]{:S(2)}) collective-permute-start(bf16[128,1024]{1,0:T(8,128)(2,1)S(1)} %constant_dynamic-slice_fusion), channel_id=1, source_target_pairs={{0,16},{16,0},{1,17},{17,1},{2,18},{18,2},{3,19},{19,3},{4,20},{20... | collective-permute-start | bytes 786440 | tf_op jit(solution)/shard_map/ppermute | solution.py:291
  6.7 40.5 %collective-permute-start.1 = (bf16[128,2048]{1,0:T(8,128)(2,1)}, bf16[128,2048]{1,0:T(8,128)(2,1)S(1)}, u32[]{:S(2)}, u32[]{:S(2)}) collective-permute-start(bf16[128,2048]{1,0:T(8,128)(2,1)} %refs_2_.1), channel_id=1, source_target_pairs={{0,8},{1,9},{2,10},{3,11},{4,12},{5,13},{6,14},{7,15},{8,0},{9,1},... | collective-permute-start | bytes 1572872 | tf_op jit(solution)/shard_map/ppermute | solution.py:295
  11.8 67.5 %collective-permute-start.5 = (bf16[2048,768]{1,0:T(8,128)(2,1)}, bf16[2048,768]{1,0:T(8,128)(2,1)}, u32[]{:S(2)}, u32[]{:S(2)}) collective-permute-start(bf16[2048,768]{1,0:T(8,128)(2,1)} %pad_maximum_fusion), channel_id=1, source_target_pairs={{0,16},{16,0},{1,17},{17,1},{2,18},{18,2},{3,19},{19,3},{4,20},{20... | collective-permute-start | bytes 9437192 | tf_op jit(solution)/shard_map/ppermute | solution.py:291
  16.6 49.3 %all-to-all-start.1 = ((bf16[16,48,1024]{2,1,0:T(8,128)(2,1)}), bf16[16,48,1024]{2,1,0:T(8,128)(2,1)S(1)}, u32[]{:S(2)}, u32[]{:S(2)}) async-start(bf16[16,48,1024]{2,1,0:T(8,128)(2,1)} %bitcast.24), calls=%async_computation.1 | async-start | bytes 3145728 | tf_op jit(solution)/shard_map/all_to_all | solution.py:300
  47.3 0.8 copy-start.2
  65.9 22.2 %all-to-all-start = ((bf16[8,48,2048]{2,1,0:T(8,128)(2,1)}), bf16[8,48,2048]{2,1,0:T(8,128)(2,1)S(1)}, u32[]{:S(2)}, u32[]{:S(2)}) async-start(bf16[8,48,2048]{2,1,0:T(8,128)(2,1)} %bitcast.27), calls=%async_computation | async-start | bytes 3145728 | tf_op jit(solution)/shard_map/all_to_all | solution.py:300
  75.1 18.9 %collective-permute-start.6 = (bf16[384,768]{1,0:T(8,128)(2,1)}, bf16[384,768]{1,0:T(8,128)(2,1)}, u32[]{:S(2)}, u32[]{:S(2)}) collective-permute-start(bf16[384,768]{1,0:T(8,128)(2,1)} %get-tuple-element.44), channel_id=1, source_target_pairs={{0,16},{16,0},{1,17},{17,1},{2,18},{18,2},{3,19},{19,3},{4,20},{20... | collective-permute-start | bytes 1769480 | tf_op jit(solution)/shard_map/ppermute | solution.py:291
  98.7 22.1 %copy-start.1 = (bf16[768,1024]{1,0:T(8,128)(2,1)S(1)}, bf16[768,1024]{1,0:T(8,128)(2,1)}, u32[]{:S(2)}) copy-start(bf16[768,1024]{1,0:T(8,128)(2,1)} %get-tuple-element.48) | copy-start | bytes 4718596
  98.7 45.6 %all-to-all-start.2 = ((bf16[16,24,2176]{2,1,0:T(8,128)(2,1)}), bf16[16,24,2176]{2,1,0:T(8,128)(2,1)S(1)}, u32[]{:S(2)}, u32[]{:S(2)}) async-start(bf16[16,24,2176]{2,1,0:T(8,128)(2,1)} %bitcast.23), calls=%async_computation.2 | async-start | bytes 3342336 | tf_op jit(solution)/shard_map/all_to_all | solution.py:300
  106.1 14.8 %collective-permute-start.7 = (bf16[384,768]{1,0:T(8,128)(2,1)}, bf16[384,768]{1,0:T(8,128)(2,1)S(1)}, u32[]{:S(2)}, u32[]{:S(2)}) collective-permute-start(bf16[384,768]{1,0:T(8,128)(2,1)} %get-tuple-element.47), channel_id=1, source_target_pairs={{0,16},{16,0},{1,17},{17,1},{2,18},{18,2},{3,19},{19,3},{4,20},{20... | collective-permute-start | bytes 1769480 | tf_op jit(solution)/shard_map/ppermute | solution.py:291
  120.8 23.5 %copy-start = (f32[128,2]{0,1:T(2,128)S(1)}, f32[128,2]{0,1:T(2,128)}, u32[]{:S(2)}) copy-start(f32[128,2]{0,1:T(2,128)} %param.9) | copy-start | bytes 3076

commit v11 on v9

--- a/solution.py
+++ b/solution.py
@@ -49,17 +49,16 @@
     ]
 
 
-def by_half(value, cap, half, paired):
+def block_labels(routes, experts):
+    half = experts // 2
+    return jnp.where(routes < half, 2 * routes, 2 * (routes - half) + 1)
+
+
+def rows_of(ref, groups, cap, which):
+    value = ref[...].astype(jnp.float32)
     count, width = value.shape
-    if paired:
-        value = value.reshape(count // (2 * cap), 2, cap, width)
-        own, other = value[:, 0], value[:, 1]
-    else:
-        value = value.reshape(2, count // (2 * cap), cap, width)
-        own, other = value[0], value[1]
-    first = jnp.where(half == 0, own, other)
-    second = jnp.where(half == 0, other, own)
-    return jnp.stack([first, second], axis=0 if paired else 1).reshape(count, width)
+    value = value.reshape(count // (groups * cap), groups, cap, width)[:, which]
+    return value.reshape(count // groups, width).astype(ref.dtype)
 
 
 def dispatch_tokens(experts, cap, place_ref, *refs):
@@ -71,11 +70,13 @@
         rows = lax.broadcasted_iota(jnp.int32, (pick_ref.shape[0], count), 0)
         for c, ref in enumerate(routes_refs):
             near = ref[...] - place_ref[1] * (experts // 2)
-            pos = slot_positions(near, experts // 2, 2 * cap, c * cap)
+            side = place_ref[1] if c == 0 else 1 - place_ref[1]
+            pos = slot_positions(near, experts // 2, 2 * cap, side * cap)
             pick_ref[:, c * count : (c + 1) * count] = sum(
                 jnp.where(rows == p, 1.0, 0.0) for p in pos
             ).astype(jnp.bfloat16)
-        for k, p in enumerate(slot_positions(routes_refs[0][...], experts, cap, 0)):
+        labels = block_labels(routes_refs[0][...], experts)
+        for k, p in enumerate(slot_positions(labels, experts, cap, 0)):
             pos_ref[k : k + 1, :] = p
 
     values = jnp.concatenate([ref[...] for ref in tokens_refs], axis=0)
@@ -95,7 +96,8 @@
         rows = lax.broadcasted_iota(jnp.int32, (slots, count), 0)
         total = jnp.zeros((slots, 1), jnp.float32)
         for q in range(groups):
-            pos = slot_positions(routes_refs[q][...], experts, groups * cap, q * cap)
+            labels = block_labels(routes_refs[q][...], experts)
+            pos = slot_positions(labels, experts, groups * cap, q * cap)
             hit = jnp.zeros((slots, count), jnp.float32)
             weight = jnp.zeros((slots, count), jnp.float32)
             for k, p in enumerate(pos):
@@ -128,14 +130,11 @@
         copy.wait()
 
 
-def back_kernel(groups, cap, place_ref, rows_ref, down_ref, own_ref, *rest):
+def back_kernel(groups, cap, rows_ref, down_ref, own_ref, *rest):
     others, all_ref = rest[: groups - 1], rest[groups - 1]
     slots, hidden = own_ref.shape
-    count, share = rows_ref.shape
-    rows = rows_ref[...].astype(jnp.float32).reshape(count // (groups * cap), groups, cap, share)
     for q in range(groups):
-        ordered = by_half(rows[:, q].reshape(slots, share), cap, place_ref[1], False)
-        all_ref[q * slots : (q + 1) * slots, :] = ordered.astype(all_ref.dtype)
+        all_ref[q * slots : (q + 1) * slots, :] = rows_of(rows_ref, groups, cap, q)
     step = tile_of(hidden, 256)
 
     @pl.loop(0, hidden // step)
@@ -181,15 +180,19 @@
         value_ref[:, cols] = hidden_f
         hidden_ref[:, cols] = hidden_f.astype(hidden_ref.dtype)
 
+    ahead = 2
+    for copies in stages[:ahead]:
+        for copy in copies:
+            copy.start()
     complete = None
     for at, i in enumerate(order):
         k = i % groups
         if at > 0:
             for copy in stages[at - 1]:
                 copy.wait()
-        if at < len(stages):
-            for copy in stages[at]:
-                copy.start()
+            if at - 1 + ahead < len(stages):
+                for copy in stages[at - 1 + ahead]:
+                    copy.start()
         sum_ref = gate_sum_ref if i < groups else up_sum_ref
         for cols in spans:
             part = jnp.dot(
@@ -205,18 +208,17 @@
 
 
 def backward_kernel(
-    groups, cap, half_ref, act_ref, slope_ref, value_ref, gate_ref, held_ref, *refs
+    groups, act_ref, slope_ref, value_ref, gate_ref, held_ref, *refs
 ):
     parts, (out_ref, d_gate_ref, d_up_ref, rows_ref, out_sems) = refs[:groups], refs[groups:]
     share = held_ref.shape[1]
     width = groups * share
     block = tile_of(share, 512)
-    half = half_ref[0]
     back = sum(part[...].astype(jnp.float32) for part in parts)
     score = jnp.sum(back * value_ref[...], axis=1, keepdims=True)
-    d_gate_ref[...] = by_half(back * slope_ref[...], cap, half, True).astype(jnp.bfloat16)
-    d_up_ref[...] = by_half(back * act_ref[...], cap, half, True).astype(jnp.bfloat16)
-    score = by_half(jnp.broadcast_to(score, (score.shape[0], LANES)), cap, half, True)
+    d_gate_ref[...] = (back * slope_ref[...]).astype(jnp.bfloat16)
+    d_up_ref[...] = (back * act_ref[...]).astype(jnp.bfloat16)
+    score = jnp.broadcast_to(score, (score.shape[0], LANES))
     rows_ref[:, width:] = score.astype(rows_ref.dtype)
     outs = []
 
@@ -274,18 +276,19 @@
     params = pltpu.CompilerParams(vmem_limit_bytes=VMEM_BYTES)
     half = lax.div(lax.axis_index("expert"), experts // 2)
     place = jnp.stack([group, half]).astype(jnp.int32)
-    place_group, place_half = group.reshape(1), half.reshape(1)
+    place_group = group.reshape(1)
     halves = [list(range(experts // 2)), list(range(experts // 2, experts))]
+    pairs = [[expert for pair in zip(*halves) for expert in pair]]
 
     def shifted(value, by):
         return lax.ppermute(value, "dp", [(i, (i + by) % groups) for i in range(groups)])
 
     def across(value):
-        pairs = [(i, (i + experts // 2) % experts) for i in range(experts)]
-        return lax.ppermute(value, "expert", pairs)
-
-    def exchanged(rows, among=None):
-        count = experts if among is None else len(among[0])
+        swaps = [(i, (i + experts // 2) % experts) for i in range(experts)]
+        return lax.ppermute(value, "expert", swaps)
+
+    def exchanged(rows, among):
+        count = len(among[0])
         split = rows.reshape(count, rows.shape[0] // count, rows.shape[1])
         moved = lax.all_to_all(
             split, "expert", split_axis=0, concat_axis=0, axis_index_groups=among, tiled=True
@@ -343,7 +346,7 @@
         in_hbm(grad_out),
         *grads,
     )
-    scaled_rows = exchanged(scaled)
+    scaled_rows = exchanged(scaled, pairs)
 
     sent, pos = pl.pallas_call(
         functools.partial(dispatch_tokens, experts, cap),
@@ -396,10 +399,9 @@
         out_shape=[pltpu.HBM((slots, hidden), jnp.float32)]
         + [pltpu.HBM((slots, hidden), jnp.bfloat16)] * (groups - 1)
         + [pltpu.HBM((groups * slots, share), jnp.bfloat16)],
-        in_specs=[place_spec, pl.BlockSpec(), pl.BlockSpec()],
         compiler_params=params,
         name="back",
-    )(place, scaled_rows, in_hbm(w_down[0]))
+    )(scaled_rows, in_hbm(w_down[0]))
     scaled_all = rest[-1]
     back_parts = [shifted(rest[k - 1], -k) for k in range(1, groups)]
 
@@ -424,9 +426,9 @@
 
     pieces = groups * (share // tile_of(share, 512))
     returning = pl.pallas_call(
-        functools.partial(backward_kernel, groups, cap),
+        functools.partial(backward_kernel, groups),
         out_shape=pltpu.HBM((slots, width + LANES), jnp.bfloat16),
-        in_specs=[place_spec] + [whole_spec] * (5 + groups),
+        in_specs=[whole_spec] * (5 + groups),
         out_specs=any_spec,
         scratch_shapes=[
             pltpu.VMEM((slots, hidden), jnp.bfloat16),
@@ -436,8 +438,8 @@
         ],
         compiler_params=params,
         name="backward",
-    )(place_half, *factors, gate_held, held, back_kept, *back_parts)
-    returned = exchanged(returning)
+    )(*factors, gate_held, held, back_kept, *back_parts)
+    returned = exchanged(returning, pairs)
 
     hiddens = [hidden_own] + [shifted(hidden_own, k) for k in range(1, groups)]
     grad_down = contract_first(jnp.concatenate(hiddens, axis=0), scaled_all)[None]

time: 147 us -> 148 us (level)
  the two profiles are of different devices: /device:TPU:11 before, /device:TPU:0 now
where the time goes in v11:
time: 148 us; the launch traced here: 147 us
  waiting for transfers between devices  88.3 us (60%)
  Pallas kernels  25 us (17%)
  starting transfers between devices  23.3 us (16%)
  matrix products  4.19 us (3%)
  other arithmetic  3.82 us (3%)
  local copies, waits for them, and re-layouts  1.77 us (1%)
    all_to_all x3, waiting for transfers between devices, exchanged(): lax.all_to_all(split, 'expert', split_axis=0, concat_axis=0, axis_index_g...  51.8 us
    ppermute x6, waiting for transfers between devices, shifted(): lax.ppermute(value, 'dp', [(i, (i + by) % groups) for i in range(groups)])  24.7 us
    ppermute x2, waiting for transfers between devices, across(): return lax.ppermute(value, 'expert', swaps)  11.9 us
    all_to_all x3, starting transfers between devices, exchanged(): lax.all_to_all(split, 'expert', split_axis=0, concat_axis=0, axis_index_g...  11.3 us
    ppermute x6, starting transfers between devices, shifted(): lax.ppermute(value, 'dp', [(i, (i + by) % groups) for i in range(groups)])  7.76 us
    pallas_call x1, Pallas kernels, per_device(): pl.pallas_call(functools.partial(forward_kernel, groups), out_shape=[pltp...  5.87 us
    pallas_call x1, Pallas kernels, per_device(): pl.pallas_call(functools.partial(back_kernel, groups, cap), out_shape=[pl...  5.03 us
    pallas_call x1, Pallas kernels, per_device(): pl.pallas_call(functools.partial(backward_kernel, groups), out_shape=pltp...  4.67 us
  transfers between devices with their start and end apart: 11, of which 7 were waited for; matrix products, arithmetic and copies ran while one was open for 6% of the time, Pallas kernels for 13%

profile of v11, /device:TPU:0, one launch (start us, length us, event | category | flops | bytes accessed | tf_op | source)
XLA Modules:
  0.0 147.1 jit_solution(1650500869566237472)
XLA Ops:
  0.6 3.0 %collective-permute-start.3 = (s32[2,128]{1,0:T(2,128)}, s32[2,128]{1,0:T(2,128)S(1)}, u32[]{:S(2)}, u32[]{:S(2)}) collective-permute-start(s32[2,128]{1,0:T(2,128)} %bitcast.31), channel_id=1, source_target_pairs={{0,16},{16,0},{1,17},{17,1},{2,18},{18,2},{3,19},{19,3},{4,20},{20... | collective-permute-start | bytes 3080 | tf_op jit(solution)/shard_map/ppermute | solution.py:284
  3.7 2.6 %collective-permute-start = (s32[2,128]{1,0:T(2,128)}, s32[2,128]{1,0:T(2,128)S(1)}, u32[]{:S(2)}, u32[]{:S(2)}) collective-permute-start(s32[2,128]{1,0:T(2,128)} %bitcast.32), channel_id=1, source_target_pairs={{0,8},{1,9},{2,10},{3,11},{4,12},{5,13},{6,14},{7,15},{8,0},{9,1},... | collective-permute-start | bytes 3080 | tf_op jit(solution)/shard_map/ppermute | solution.py:288
  6.3 0.5 collective-permute-start.4
  6.8 1.0 constant_dynamic-slice_fusion
  7.7 1.6 %collective-permute-start.2 = (bf16[128,1024]{1,0:T(8,128)(2,1)S(1)}, bf16[128,1024]{1,0:T(8,128)(2,1)S(1)}, u32[]{:S(2)}, u32[]{:S(2)}) collective-permute-start(bf16[128,1024]{1,0:T(8,128)(2,1)S(1)} %constant_dynamic-slice_fusion), channel_id=1, source_target_pairs={{0,16},{16,0},{1,17},{17,1},{2,18},{18,2},{3,19},{19,3},{4,20},{20... | collective-permute-start | bytes 786440 | tf_op jit(solution)/shard_map/ppermute | solution.py:284
  9.3 0.0 collective-permute-done.refs_1_
  9.3 1.6 %collective-permute-start.1 = (bf16[128,2048]{1,0:T(8,128)(2,1)}, bf16[128,2048]{1,0:T(8,128)(2,1)S(1)}, u32[]{:S(2)}, u32[]{:S(2)}) collective-permute-start(bf16[128,2048]{1,0:T(8,128)(2,1)} %refs_2_.1), channel_id=1, source_target_pairs={{0,8},{1,9},{2,10},{3,11},{4,12},{5,13},{6,14},{7,15},{8,0},{9,1},... | collective-permute-start | bytes 1572872 | tf_op jit(solution)/shard_map/ppermute | solution.py:288
  10.9 3.7 %pad_maximum_fusion = bf16[2048,768]{1,0:T(8,128)(2,1)} fusion(bf16[1024,768]{1,0:T(8,128)(2,1)} %bitcast.25, bf16[1024,768]{1,0:T(8,128)(2,1)} %bitcast.29), kind=kLoop, calls=%fused_computation | loop fusion | flops 6291456 | bytes 6291456 | tf_op jit(solution)/shard_map/concatenate | solution.py:307
  14.7 0.0 collective-permute-done.3.refs_1_
  14.7 0.3 collective-permute-done.2.refs_5_
  15.0 1.5 %collective-permute-start.5 = (bf16[2048,768]{1,0:T(8,128)(2,1)}, bf16[2048,768]{1,0:T(8,128)(2,1)}, u32[]{:S(2)}, u32[]{:S(2)}) collective-permute-start(bf16[2048,768]{1,0:T(8,128)(2,1)} %pad_maximum_fusion), channel_id=1, source_target_pairs={{0,16},{16,0},{1,17},{17,1},{2,18},{18,2},{3,19},{19,3},{4,20},{20... | collective-permute-start | bytes 9437192 | tf_op jit(solution)/shard_map/ppermute | solution.py:284
  16.5 3.1 %dispatch_scaled.1 = bf16[768,1024]{1,0:T(8,128)(2,1)} custom-call(s32[1]{0:T(128)} %bitcast.place_ref, s32[2,128]{1,0:T(2,128)} %bitcast.33, s32[2,128]{1,0:T(2,128)S(1)} %collective-permute-done.3.refs_1_, f32[2,128]{1,0:T(2,128)} %bitcast.21, f32[2,128]{1,0:T(2,128)S(1)} %collective-permute-done.4.refs_3_, bf16[128,2048]{1,0:T(8,128)(2,1)} %refs_4_.1, ...), custom_call_target="tpu_custom_call" | custom-call | tf_op jit(solution)/shard_map/dispatch_scaled/pallas_call | solution.py:323
  19.6 3.9 %all-to-all-start.1 = ((bf16[16,48,1024]{2,1,0:T(8,128)(2,1)}), bf16[16,48,1024]{2,1,0:T(8,128)(2,1)S(1)}, u32[]{:S(2)}, u32[]{:S(2)}) async-start(bf16[16,48,1024]{2,1,0:T(8,128)(2,1)} %bitcast.24), calls=%async_computation.1 | async-start | bytes 3145728 | tf_op jit(solution)/shard_map/all_to_all | solution.py:293
  23.5 0.1 pad_add_fusion.place_ref
  23.6 11.9 %collective-permute-done.1.refs_3_ = bf16[128,2048]{1,0:T(8,128)(2,1)S(1)} collective-permute-done((bf16[128,2048]{1,0:T(8,128)(2,1)}, bf16[128,2048]{1,0:T(8,128)(2,1)S(1)}, u32[]{:S(2)}, u32[]{:S(2)}) %collective-permute-start.1) | collective-permute-done | bytes 524320 | tf_op jit(solution)/shard_map/ppermute | solution.py:288
  35.5 0.8 copy-done.2
  36.3 3.6 %dispatch_tokens.1 = (bf16[384,2048]{1,0:T(8,128)(2,1)}, s32[2,128]{1,0:T(2,128)S(1)}) custom-call(s32[2]{0:T(128)S(1)} %pad_add_fusion.place_ref, s32[2,128]{1,0:T(2,128)} %bitcast.34, s32[2,128]{1,0:T(2,128)S(1)} %collective-permute-done.refs_1_, bf16[128,2048]{1,0:T(8,128)(2,1)} %refs_2_.1, bf16[128,2048]{1,0:T(8,128)(2,1)} %copy-done.2), custom_call_target="tpu_custom_call" | custom-call | flops 30000001024 | bytes 30000000 | tf_op jit(solution)/shard_map/dispatch_tokens/pallas_call | solution.py:351
  39.9 28.1 %all-to-all-done.1 = bf16[16,48,1024]{2,1,0:T(8,128)(2,1)S(1)} async-done(((bf16[16,48,1024]{2,1,0:T(8,128)(2,1)}), bf16[16,48,1024]{2,1,0:T(8,128)(2,1)S(1)}, u32[]{:S(2)}, u32[]{:S(2)}) %all-to-all-start.1) | async-done | bytes 1572896 | tf_op jit(solution)/shard_map/all_to_all | solution.py:293
  68.0 3.6 %all-to-all-start = ((bf16[8,48,2048]{2,1,0:T(8,128)(2,1)}), bf16[8,48,2048]{2,1,0:T(8,128)(2,1)S(1)}, u32[]{:S(2)}, u32[]{:S(2)}) async-start(bf16[8,48,2048]{2,1,0:T(8,128)(2,1)} %bitcast.28), calls=%async_computation | async-start | bytes 3145728 | tf_op jit(solution)/shard_map/all_to_all | solution.py:293
  71.6 5.0 %back.1 = (f32[384,768]{1,0:T(8,128)}, bf16[384,768]{1,0:T(8,128)(2,1)}, bf16[768,1024]{1,0:T(8,128)(2,1)}) custom-call(bf16[768,1024]{1,0:T(8,128)(2,1)S(1)} %bitcast.18, bf16[768,1024]{1,0:T(8,128)(2,1)} %bitcast.27), custom_call_target="tpu_custom_call" | custom-call | tf_op jit(solution)/shard_map/back/pallas_call | solution.py:397
  76.6 0.6 collective-permute-start.6
  77.2 9.2 %collective-permute-done.5.refs_0_ = bf16[2048,768]{1,0:T(8,128)(2,1)} collective-permute-done((bf16[2048,768]{1,0:T(8,128)(2,1)}, bf16[2048,768]{1,0:T(8,128)(2,1)}, u32[]{:S(2)}, u32[]{:S(2)}) %collective-permute-start.5) | collective-permute-done | bytes 3145760 | tf_op jit(solution)/shard_map/ppermute | solution.py:284
  86.4 1.4 ready.1
  87.8 3.8 %all-to-all-done = bf16[8,48,2048]{2,1,0:T(8,128)(2,1)S(1)} async-done(((bf16[8,48,2048]{2,1,0:T(8,128)(2,1)}), bf16[8,48,2048]{2,1,0:T(8,128)(2,1)S(1)}, u32[]{:S(2)}, u32[]{:S(2)}) %all-to-all-start) | async-done | bytes 1572896 | tf_op jit(solution)/shard_map/all_to_all | solution.py:293
  91.6 5.9 %forward.1 = (f32[384,768]{1,0:T(8,128)S(1)}, f32[384,768]{1,0:T(8,128)S(1)}, f32[384,768]{1,0:T(8,128)S(1)}, bf16[384,768]{1,0:T(8,128)(2,1)}, bf16[3,1024,768]...) custom-call(bf16[384,2048]{1,0:T(8,128)(2,1)S(1)} %bitcast.19, bf16[1024,768]{1,0:T(8,128)(2,1)S(1)} %get-tuple-element.32.gate_ref, ...), custom_call_target="tpu_custom_call" | custom-call | tf_op jit(solution)/shard_map/forward/pallas_call | solution.py:408
  97.5 4.7 %backward.1 = bf16[384,2176]{1,0:T(8,128)(2,1)} custom-call(f32[384,768]{1,0:T(8,128)S(1)} %get-tuple-element.39.act_ref, f32[384,768]{1,0:T(8,128)S(1)} %get-tuple-element.40.slope_ref, f32[384,768]{1,0:T(8,128)S(1)} %get-tuple-element.41.value_ref, bf16[1024,768]{1,0:T(8,128)(2,1)S(1)} %get-tuple-element.32.gate_ref, ...), custom_call_target="tpu_custom_call" | custom-call | tf_op jit(solution)/shard_map/backward/pallas_call | solution.py:428
  102.2 3.9 %all-to-all-start.2 = ((bf16[16,24,2176]{2,1,0:T(8,128)(2,1)}), bf16[16,24,2176]{2,1,0:T(8,128)(2,1)S(1)}, u32[]{:S(2)}, u32[]{:S(2)}) async-start(bf16[16,24,2176]{2,1,0:T(8,128)(2,1)} %bitcast.23), calls=%async_computation.2 | async-start | bytes 3342336 | tf_op jit(solution)/shard_map/all_to_all | solution.py:293
  106.0 0.6 collective-permute-start.7
  106.6 15.2 %collective-permute-done.7 = bf16[384,768]{1,0:T(8,128)(2,1)S(1)} collective-permute-done((bf16[384,768]{1,0:T(8,128)(2,1)}, bf16[384,768]{1,0:T(8,128)(2,1)S(1)}, u32[]{:S(2)}, u32[]{:S(2)}) %collective-permute-start.7) | collective-permute-done | bytes 589856 | tf_op jit(solution)/shard_map/ppermute | solution.py:284
  121.8 4.2 %convolution_bitcast_fusion = f32[1,768,1024]{2,1,0:T(8,128)} fusion(bf16[768,1024]{1,0:T(8,128)(2,1)S(1)} %copy-done.1, bf16[384,768]{1,0:T(8,128)(2,1)S(1)} %collective-permute-done.7, bf16[384,768]{1,0:T(8,128)(2,1)} %get-tuple-element.47), kind=kOutput, calls=%fused_computation.1 | convolution fusion | flops 1210318848 | bytes 5898240 | tf_op jit(solution)/shard_map/dot_general | solution.py:23
  126.0 19.8 %all-to-all-done.2 = bf16[16,24,2176]{2,1,0:T(8,128)(2,1)S(1)} async-done(((bf16[16,24,2176]{2,1,0:T(8,128)(2,1)}), bf16[16,24,2176]{2,1,0:T(8,128)(2,1)S(1)}, u32[]{:S(2)}, u32[]{:S(2)}) %all-to-all-start.2) | async-done | bytes 1671200 | tf_op jit(solution)/shard_map/all_to_all | solution.py:293
  145.8 1.3 combine.1
  (7 shorter events, 0.0 us)
Async XLA Ops:
  0.6 14.1 %collective-permute-start.3 = (s32[2,128]{1,0:T(2,128)}, s32[2,128]{1,0:T(2,128)S(1)}, u32[]{:S(2)}, u32[]{:S(2)}) collective-permute-start(s32[2,128]{1,0:T(2,128)} %bitcast.31), channel_id=1, source_target_pairs={{0,16},{16,0},{1,17},{17,1},{2,18},{18,2},{3,19},{19,3},{4,20},{20... | collective-permute-start | bytes 3080 | tf_op jit(solution)/shard_map/ppermute | solution.py:284
  3.7 5.7 %collective-permute-start = (s32[2,128]{1,0:T(2,128)}, s32[2,128]{1,0:T(2,128)S(1)}, u32[]{:S(2)}, u32[]{:S(2)}) collective-permute-start(s32[2,128]{1,0:T(2,128)} %bitcast.32), channel_id=1, source_target_pairs={{0,8},{1,9},{2,10},{3,11},{4,12},{5,13},{6,14},{7,15},{8,0},{9,1},... | collective-permute-start | bytes 3080 | tf_op jit(solution)/shard_map/ppermute | solution.py:288
  6.3 8.4 %collective-permute-start.4 = (f32[2,128]{1,0:T(2,128)}, f32[2,128]{1,0:T(2,128)S(1)}, u32[]{:S(2)}, u32[]{:S(2)}) collective-permute-start(f32[2,128]{1,0:T(2,128)} %bitcast.20), channel_id=1, source_target_pairs={{0,16},{16,0},{1,17},{17,1},{2,18},{18,2},{3,19},{19,3},{4,20},{20... | collective-permute-start | bytes 3080 | tf_op jit(solution)/shard_map/ppermute | solution.py:284
  7.7 7.3 %collective-permute-start.2 = (bf16[128,1024]{1,0:T(8,128)(2,1)S(1)}, bf16[128,1024]{1,0:T(8,128)(2,1)S(1)}, u32[]{:S(2)}, u32[]{:S(2)}) collective-permute-start(bf16[128,1024]{1,0:T(8,128)(2,1)S(1)} %constant_dynamic-slice_fusion), channel_id=1, source_target_pairs={{0,16},{16,0},{1,17},{17,1},{2,18},{18,2},{3,19},{19,3},{4,20},{20... | collective-permute-start | bytes 786440 | tf_op jit(solution)/shard_map/ppermute | solution.py:284
  9.3 26.2 %collective-permute-start.1 = (bf16[128,2048]{1,0:T(8,128)(2,1)}, bf16[128,2048]{1,0:T(8,128)(2,1)S(1)}, u32[]{:S(2)}, u32[]{:S(2)}) collective-permute-start(bf16[128,2048]{1,0:T(8,128)(2,1)} %refs_2_.1), channel_id=1, source_target_pairs={{0,8},{1,9},{2,10},{3,11},{4,12},{5,13},{6,14},{7,15},{8,0},{9,1},... | collective-permute-start | bytes 1572872 | tf_op jit(solution)/shard_map/ppermute | solution.py:288
  15.0 71.4 %collective-permute-start.5 = (bf16[2048,768]{1,0:T(8,128)(2,1)}, bf16[2048,768]{1,0:T(8,128)(2,1)}, u32[]{:S(2)}, u32[]{:S(2)}) collective-permute-start(bf16[2048,768]{1,0:T(8,128)(2,1)} %pad_maximum_fusion), channel_id=1, source_target_pairs={{0,16},{16,0},{1,17},{17,1},{2,18},{18,2},{3,19},{19,3},{4,20},{20... | collective-permute-start | bytes 9437192 | tf_op jit(solution)/shard_map/ppermute | solution.py:284
  19.6 48.4 %all-to-all-start.1 = ((bf16[16,48,1024]{2,1,0:T(8,128)(2,1)}), bf16[16,48,1024]{2,1,0:T(8,128)(2,1)S(1)}, u32[]{:S(2)}, u32[]{:S(2)}) async-start(bf16[16,48,1024]{2,1,0:T(8,128)(2,1)} %bitcast.24), calls=%async_computation.1 | async-start | bytes 3145728 | tf_op jit(solution)/shard_map/all_to_all | solution.py:293
  35.5 0.8 copy-start.2
  68.0 23.6 %all-to-all-start = ((bf16[8,48,2048]{2,1,0:T(8,128)(2,1)}), bf16[8,48,2048]{2,1,0:T(8,128)(2,1)S(1)}, u32[]{:S(2)}, u32[]{:S(2)}) async-start(bf16[8,48,2048]{2,1,0:T(8,128)(2,1)} %bitcast.28), calls=%async_computation | async-start | bytes 3145728 | tf_op jit(solution)/shard_map/all_to_all | solution.py:293
  76.6 20.8 %collective-permute-start.6 = (bf16[384,768]{1,0:T(8,128)(2,1)}, bf16[384,768]{1,0:T(8,128)(2,1)}, u32[]{:S(2)}, u32[]{:S(2)}) collective-permute-start(bf16[384,768]{1,0:T(8,128)(2,1)} %get-tuple-element.44), channel_id=1, source_target_pairs={{0,16},{16,0},{1,17},{17,1},{2,18},{18,2},{3,19},{19,3},{4,20},{20... | collective-permute-start | bytes 1769480 | tf_op jit(solution)/shard_map/ppermute | solution.py:284
  102.2 19.6 %copy-start.1 = (bf16[768,1024]{1,0:T(8,128)(2,1)S(1)}, bf16[768,1024]{1,0:T(8,128)(2,1)}, u32[]{:S(2)}) copy-start(bf16[768,1024]{1,0:T(8,128)(2,1)} %get-tuple-element.48) | copy-start | bytes 4718596
  102.2 43.6 %all-to-all-start.2 = ((bf16[16,24,2176]{2,1,0:T(8,128)(2,1)}), bf16[16,24,2176]{2,1,0:T(8,128)(2,1)S(1)}, u32[]{:S(2)}, u32[]{:S(2)}) async-start(bf16[16,24,2176]{2,1,0:T(8,128)(2,1)} %bitcast.23), calls=%async_computation.2 | async-start | bytes 3342336 | tf_op jit(solution)/shard_map/all_to_all | solution.py:293
  106.0 15.8 %collective-permute-start.7 = (bf16[384,768]{1,0:T(8,128)(2,1)}, bf16[384,768]{1,0:T(8,128)(2,1)S(1)}, u32[]{:S(2)}, u32[]{:S(2)}) collective-permute-start(bf16[384,768]{1,0:T(8,128)(2,1)} %get-tuple-element.47), channel_id=1, source_target_pairs={{0,16},{16,0},{1,17},{17,1},{2,18},{18,2},{3,19},{19,3},{4,20},{20... | collective-permute-start | bytes 1769480 | tf_op jit(solution)/shard_map/ppermute | solution.py:284
  121.8 24.0 %copy-start = (f32[128,2]{0,1:T(2,128)S(1)}, f32[128,2]{0,1:T(2,128)}, u32[]{:S(2)}) copy-start(f32[128,2]{0,1:T(2,128)} %param.9) | copy-start | bytes 3076

commit v12 on v9

--- a/solution.py
+++ b/solution.py
@@ -181,15 +181,19 @@
         value_ref[:, cols] = hidden_f
         hidden_ref[:, cols] = hidden_f.astype(hidden_ref.dtype)
 
+    ahead = 3
+    for copies in stages[:ahead]:
+        for copy in copies:
+            copy.start()
     complete = None
     for at, i in enumerate(order):
         k = i % groups
         if at > 0:
             for copy in stages[at - 1]:
                 copy.wait()
-        if at < len(stages):
-            for copy in stages[at]:
-                copy.start()
+            if at - 1 + ahead < len(stages):
+                for copy in stages[at - 1 + ahead]:
+                    copy.start()
         sum_ref = gate_sum_ref if i < groups else up_sum_ref
         for cols in spans:
             part = jnp.dot(

time: 147 us -> 146 us (level)
  transfers between devices with their start and end apart: 11 -> 11, of which waited for: 7 -> 7; matrix products, arithmetic and copies ran while one was open for 6% -> 6% of each run, Pallas kernels for 14% -> 13%
where the time goes in v12:
time: 146 us; the launch traced here: 145 us
  waiting for transfers between devices  84.2 us (58%)
  starting transfers between devices  25.7 us (18%)
  Pallas kernels  24.6 us (17%)
  matrix products  4.19 us (3%)
  other arithmetic  3.82 us (3%)
  local copies, waits for them, and re-layouts  1.77 us (1%)
    all_to_all x3, waiting for transfers between devices, exchanged(): lax.all_to_all(split, 'expert', split_axis=0, concat_axis=0, axis_index_g...  40.6 us
    ppermute x2, waiting for transfers between devices, across(): return lax.ppermute(value, 'expert', pairs)  24.8 us
    ppermute x6, waiting for transfers between devices, shifted(): lax.ppermute(value, 'dp', [(i, (i + by) % groups) for i in range(groups)])  18.8 us
    all_to_all x3, starting transfers between devices, exchanged(): lax.all_to_all(split, 'expert', split_axis=0, concat_axis=0, axis_index_g...  17.9 us
    pallas_call x1, Pallas kernels, per_device(): pl.pallas_call(functools.partial(forward_kernel, groups), out_shape=[pltp...  5.25 us
    pallas_call x1, Pallas kernels, per_device(): pl.pallas_call(functools.partial(back_kernel, groups, cap), out_shape=[pl...  5.22 us
    pallas_call x1, Pallas kernels, per_device(): pl.pallas_call(functools.partial(backward_kernel, groups, cap), out_shape...  4.74 us
    ppermute x6, starting transfers between devices, shifted(): lax.ppermute(value, 'dp', [(i, (i + by) % groups) for i in range(groups)])  4.5 us
  transfers between devices with their start and end apart: 11, of which 7 were waited for; matrix products, arithmetic and copies ran while one was open for 6% of the time, Pallas kernels for 13%

profile of v12, /device:TPU:11, one launch (start us, length us, event | category | flops | bytes accessed | tf_op | source)
XLA Modules:
  0.0 145.0 jit_solution(7893639685895090218)
XLA Ops:
  0.6 1.3 collective-permute-start.3
  1.9 2.3 %collective-permute-start = (s32[2,128]{1,0:T(2,128)}, s32[2,128]{1,0:T(2,128)S(1)}, u32[]{:S(2)}, u32[]{:S(2)}) collective-permute-start(s32[2,128]{1,0:T(2,128)} %bitcast.32), channel_id=1, source_target_pairs={{0,8},{1,9},{2,10},{3,11},{4,12},{5,13},{6,14},{7,15},{8,0},{9,1},... | collective-permute-start | bytes 3080 | tf_op jit(solution)/shard_map/ppermute | solution.py:289
  4.2 0.2 collective-permute-start.4
  4.5 1.0 constant_dynamic-slice_fusion
  5.4 1.3 collective-permute-start.2
  6.7 0.0 collective-permute-done.refs_1_
  6.7 1.0 collective-permute-start.1
  7.8 3.7 %pad_maximum_fusion = bf16[2048,768]{1,0:T(8,128)(2,1)} fusion(bf16[1024,768]{1,0:T(8,128)(2,1)} %bitcast.25, bf16[1024,768]{1,0:T(8,128)(2,1)} %bitcast.29), kind=kLoop, calls=%fused_computation | loop fusion | flops 6291456 | bytes 6291456 | tf_op jit(solution)/shard_map/concatenate | solution.py:308
  11.5 0.0 collective-permute-done.3.refs_1_
  11.5 0.3 collective-permute-done.2.refs_5_
  11.8 1.2 collective-permute-start.5
  13.0 3.1 %dispatch_scaled.1 = bf16[768,1024]{1,0:T(8,128)(2,1)} custom-call(s32[1]{0:T(128)} %bitcast.place_ref, s32[2,128]{1,0:T(2,128)} %bitcast.33, s32[2,128]{1,0:T(2,128)S(1)} %collective-permute-done.3.refs_1_, f32[2,128]{1,0:T(2,128)} %bitcast.21, f32[2,128]{1,0:T(2,128)S(1)} %collective-permute-done.4.refs_3_, bf16[128,2048]{1,0:T(8,128)(2,1)} %refs_4_.1, ...), custom_call_target="tpu_custom_call" | custom-call | tf_op jit(solution)/shard_map/dispatch_scaled/pallas_call | solution.py:324
  16.2 6.6 %all-to-all-start.1 = ((bf16[16,48,1024]{2,1,0:T(8,128)(2,1)}), bf16[16,48,1024]{2,1,0:T(8,128)(2,1)S(1)}, u32[]{:S(2)}, u32[]{:S(2)}) async-start(bf16[16,48,1024]{2,1,0:T(8,128)(2,1)} %bitcast.24), calls=%async_computation.1 | async-start | bytes 3145728 | tf_op jit(solution)/shard_map/all_to_all | solution.py:294
  22.7 0.1 pad_add_fusion.place_ref
  22.8 24.8 %collective-permute-done.1.refs_3_ = bf16[128,2048]{1,0:T(8,128)(2,1)S(1)} collective-permute-done((bf16[128,2048]{1,0:T(8,128)(2,1)}, bf16[128,2048]{1,0:T(8,128)(2,1)S(1)}, u32[]{:S(2)}, u32[]{:S(2)}) %collective-permute-start.1) | collective-permute-done | bytes 524320 | tf_op jit(solution)/shard_map/ppermute | solution.py:289
  47.6 0.8 copy-done.2
  48.4 3.6 %dispatch_tokens.1 = (bf16[384,2048]{1,0:T(8,128)(2,1)}, s32[2,128]{1,0:T(2,128)S(1)}) custom-call(s32[2]{0:T(128)S(1)} %pad_add_fusion.place_ref, s32[2,128]{1,0:T(2,128)} %bitcast.34, s32[2,128]{1,0:T(2,128)S(1)} %collective-permute-done.refs_1_, bf16[128,2048]{1,0:T(8,128)(2,1)} %refs_2_.1, bf16[128,2048]{1,0:T(8,128)(2,1)} %copy-done.2), custom_call_target="tpu_custom_call" | custom-call | flops 30000001024 | bytes 30000000 | tf_op jit(solution)/shard_map/dispatch_tokens/pallas_call | solution.py:352
  52.0 13.9 %all-to-all-done.1 = bf16[16,48,1024]{2,1,0:T(8,128)(2,1)S(1)} async-done(((bf16[16,48,1024]{2,1,0:T(8,128)(2,1)}), bf16[16,48,1024]{2,1,0:T(8,128)(2,1)S(1)}, u32[]{:S(2)}, u32[]{:S(2)}) %all-to-all-start.1) | async-done | bytes 1572896 | tf_op jit(solution)/shard_map/all_to_all | solution.py:294
  65.9 4.0 %all-to-all-start = ((bf16[8,48,2048]{2,1,0:T(8,128)(2,1)}), bf16[8,48,2048]{2,1,0:T(8,128)(2,1)S(1)}, u32[]{:S(2)}, u32[]{:S(2)}) async-start(bf16[8,48,2048]{2,1,0:T(8,128)(2,1)} %bitcast.27), calls=%async_computation | async-start | bytes 3145728 | tf_op jit(solution)/shard_map/all_to_all | solution.py:294
  69.9 5.2 %back.1 = (f32[384,768]{1,0:T(8,128)}, bf16[384,768]{1,0:T(8,128)(2,1)}, bf16[768,1024]{1,0:T(8,128)(2,1)}) custom-call(s32[2]{0:T(128)S(1)} %pad_add_fusion.place_ref, bf16[768,1024]{1,0:T(8,128)(2,1)S(1)} %bitcast.18, bf16[768,1024]{1,0:T(8,128)(2,1)} %bitcast.28), custom_call_target="tpu_custom_call" | custom-call | tf_op jit(solution)/shard_map/back/pallas_call | solution.py:398
  75.1 0.2 collective-permute-start.6
  75.3 4.0 %collective-permute-done.5.refs_0_ = bf16[2048,768]{1,0:T(8,128)(2,1)} collective-permute-done((bf16[2048,768]{1,0:T(8,128)(2,1)}, bf16[2048,768]{1,0:T(8,128)(2,1)}, u32[]{:S(2)}, u32[]{:S(2)}) %collective-permute-start.5) | collective-permute-done | bytes 3145760 | tf_op jit(solution)/shard_map/ppermute | solution.py:285
  79.3 1.4 ready.1
  80.7 7.4 %all-to-all-done = bf16[8,48,2048]{2,1,0:T(8,128)(2,1)S(1)} async-done(((bf16[8,48,2048]{2,1,0:T(8,128)(2,1)}), bf16[8,48,2048]{2,1,0:T(8,128)(2,1)S(1)}, u32[]{:S(2)}, u32[]{:S(2)}) %all-to-all-start) | async-done | bytes 1572896 | tf_op jit(solution)/shard_map/all_to_all | solution.py:294
  88.1 5.3 %forward.1 = (f32[384,768]{1,0:T(8,128)S(1)}, f32[384,768]{1,0:T(8,128)S(1)}, f32[384,768]{1,0:T(8,128)S(1)}, bf16[384,768]{1,0:T(8,128)(2,1)}, bf16[3,1024,768]...) custom-call(bf16[384,2048]{1,0:T(8,128)(2,1)S(1)} %bitcast.19, bf16[1024,768]{1,0:T(8,128)(2,1)S(1)} %get-tuple-element.32.gate_ref, ...), custom_call_target="tpu_custom_call" | custom-call | tf_op jit(solution)/shard_map/forward/pallas_call | solution.py:410
  93.4 4.7 %backward.1 = bf16[384,2176]{1,0:T(8,128)(2,1)} custom-call(s32[1]{0:T(128)} %bitcast.1.half_ref, f32[384,768]{1,0:T(8,128)S(1)} %get-tuple-element.39.act_ref, f32[384,768]{1,0:T(8,128)S(1)} %get-tuple-element.40.slope_ref, f32[384,768]{1,0:T(8,128)S(1)} %get-tuple-element.41.value_ref, bf16[1024,768]{1,0:T(8,128)(2,1)S(1)} %get-tuple-element.32.gate_ref, ...), custom_call_target="tpu_custom_call" | custom-call | tf_op jit(solution)/shard_map/backward/pallas_call | solution.py:430
  98.1 7.3 %all-to-all-start.2 = ((bf16[16,24,2176]{2,1,0:T(8,128)(2,1)}), bf16[16,24,2176]{2,1,0:T(8,128)(2,1)S(1)}, u32[]{:S(2)}, u32[]{:S(2)}) async-start(bf16[16,24,2176]{2,1,0:T(8,128)(2,1)} %bitcast.23), calls=%async_computation.2 | async-start | bytes 3342336 | tf_op jit(solution)/shard_map/all_to_all | solution.py:294
  105.4 0.2 collective-permute-start.7
  105.7 14.5 %collective-permute-done.7 = bf16[384,768]{1,0:T(8,128)(2,1)S(1)} collective-permute-done((bf16[384,768]{1,0:T(8,128)(2,1)}, bf16[384,768]{1,0:T(8,128)(2,1)S(1)}, u32[]{:S(2)}, u32[]{:S(2)}) %collective-permute-start.7) | collective-permute-done | bytes 589856 | tf_op jit(solution)/shard_map/ppermute | solution.py:285
  120.2 4.2 %convolution_bitcast_fusion = f32[1,768,1024]{2,1,0:T(8,128)} fusion(bf16[768,1024]{1,0:T(8,128)(2,1)S(1)} %copy-done.1, bf16[384,768]{1,0:T(8,128)(2,1)S(1)} %collective-permute-done.7, bf16[384,768]{1,0:T(8,128)(2,1)} %get-tuple-element.47), kind=kOutput, calls=%fused_computation.1 | convolution fusion | flops 1210318848 | bytes 5898240 | tf_op jit(solution)/shard_map/dot_general | solution.py:23
  124.4 19.3 %all-to-all-done.2 = bf16[16,24,2176]{2,1,0:T(8,128)(2,1)S(1)} async-done(((bf16[16,24,2176]{2,1,0:T(8,128)(2,1)}), bf16[16,24,2176]{2,1,0:T(8,128)(2,1)S(1)}, u32[]{:S(2)}, u32[]{:S(2)}) %all-to-all-start.2) | async-done | bytes 1671200 | tf_op jit(solution)/shard_map/all_to_all | solution.py:294
  143.7 1.3 combine.1
  (7 shorter events, 0.0 us)
Async XLA Ops:
  0.6 10.9 %collective-permute-start.3 = (s32[2,128]{1,0:T(2,128)}, s32[2,128]{1,0:T(2,128)S(1)}, u32[]{:S(2)}, u32[]{:S(2)}) collective-permute-start(s32[2,128]{1,0:T(2,128)} %bitcast.31), channel_id=1, source_target_pairs={{0,16},{16,0},{1,17},{17,1},{2,18},{18,2},{3,19},{19,3},{4,20},{20... | collective-permute-start | bytes 3080 | tf_op jit(solution)/shard_map/ppermute | solution.py:285
  1.9 4.8 %collective-permute-start = (s32[2,128]{1,0:T(2,128)}, s32[2,128]{1,0:T(2,128)S(1)}, u32[]{:S(2)}, u32[]{:S(2)}) collective-permute-start(s32[2,128]{1,0:T(2,128)} %bitcast.32), channel_id=1, source_target_pairs={{0,8},{1,9},{2,10},{3,11},{4,12},{5,13},{6,14},{7,15},{8,0},{9,1},... | collective-permute-start | bytes 3080 | tf_op jit(solution)/shard_map/ppermute | solution.py:289
  4.2 7.3 %collective-permute-start.4 = (f32[2,128]{1,0:T(2,128)}, f32[2,128]{1,0:T(2,128)S(1)}, u32[]{:S(2)}, u32[]{:S(2)}) collective-permute-start(f32[2,128]{1,0:T(2,128)} %bitcast.20), channel_id=1, source_target_pairs={{0,16},{16,0},{1,17},{17,1},{2,18},{18,2},{3,19},{19,3},{4,20},{20... | collective-permute-start | bytes 3080 | tf_op jit(solution)/shard_map/ppermute | solution.py:285
  5.4 6.4 %collective-permute-start.2 = (bf16[128,1024]{1,0:T(8,128)(2,1)S(1)}, bf16[128,1024]{1,0:T(8,128)(2,1)S(1)}, u32[]{:S(2)}, u32[]{:S(2)}) collective-permute-start(bf16[128,1024]{1,0:T(8,128)(2,1)S(1)} %constant_dynamic-slice_fusion), channel_id=1, source_target_pairs={{0,16},{16,0},{1,17},{17,1},{2,18},{18,2},{3,19},{19,3},{4,20},{20... | collective-permute-start | bytes 786440 | tf_op jit(solution)/shard_map/ppermute | solution.py:285
  6.7 40.9 %collective-permute-start.1 = (bf16[128,2048]{1,0:T(8,128)(2,1)}, bf16[128,2048]{1,0:T(8,128)(2,1)S(1)}, u32[]{:S(2)}, u32[]{:S(2)}) collective-permute-start(bf16[128,2048]{1,0:T(8,128)(2,1)} %refs_2_.1), channel_id=1, source_target_pairs={{0,8},{1,9},{2,10},{3,11},{4,12},{5,13},{6,14},{7,15},{8,0},{9,1},... | collective-permute-start | bytes 1572872 | tf_op jit(solution)/shard_map/ppermute | solution.py:289
  11.8 67.5 %collective-permute-start.5 = (bf16[2048,768]{1,0:T(8,128)(2,1)}, bf16[2048,768]{1,0:T(8,128)(2,1)}, u32[]{:S(2)}, u32[]{:S(2)}) collective-permute-start(bf16[2048,768]{1,0:T(8,128)(2,1)} %pad_maximum_fusion), channel_id=1, source_target_pairs={{0,16},{16,0},{1,17},{17,1},{2,18},{18,2},{3,19},{19,3},{4,20},{20... | collective-permute-start | bytes 9437192 | tf_op jit(solution)/shard_map/ppermute | solution.py:285
  16.2 49.8 %all-to-all-start.1 = ((bf16[16,48,1024]{2,1,0:T(8,128)(2,1)}), bf16[16,48,1024]{2,1,0:T(8,128)(2,1)S(1)}, u32[]{:S(2)}, u32[]{:S(2)}) async-start(bf16[16,48,1024]{2,1,0:T(8,128)(2,1)} %bitcast.24), calls=%async_computation.1 | async-start | bytes 3145728 | tf_op jit(solution)/shard_map/all_to_all | solution.py:294
  47.6 0.8 copy-start.2
  65.9 22.2 %all-to-all-start = ((bf16[8,48,2048]{2,1,0:T(8,128)(2,1)}), bf16[8,48,2048]{2,1,0:T(8,128)(2,1)S(1)}, u32[]{:S(2)}, u32[]{:S(2)}) async-start(bf16[8,48,2048]{2,1,0:T(8,128)(2,1)} %bitcast.27), calls=%async_computation | async-start | bytes 3145728 | tf_op jit(solution)/shard_map/all_to_all | solution.py:294
  75.1 18.3 %collective-permute-start.6 = (bf16[384,768]{1,0:T(8,128)(2,1)}, bf16[384,768]{1,0:T(8,128)(2,1)}, u32[]{:S(2)}, u32[]{:S(2)}) collective-permute-start(bf16[384,768]{1,0:T(8,128)(2,1)} %get-tuple-element.44), channel_id=1, source_target_pairs={{0,16},{16,0},{1,17},{17,1},{2,18},{18,2},{3,19},{19,3},{4,20},{20... | collective-permute-start | bytes 1769480 | tf_op jit(solution)/shard_map/ppermute | solution.py:285
  98.1 22.1 %copy-start.1 = (bf16[768,1024]{1,0:T(8,128)(2,1)S(1)}, bf16[768,1024]{1,0:T(8,128)(2,1)}, u32[]{:S(2)}) copy-start(bf16[768,1024]{1,0:T(8,128)(2,1)} %get-tuple-element.48) | copy-start | bytes 4718596
  98.1 45.6 %all-to-all-start.2 = ((bf16[16,24,2176]{2,1,0:T(8,128)(2,1)}), bf16[16,24,2176]{2,1,0:T(8,128)(2,1)S(1)}, u32[]{:S(2)}, u32[]{:S(2)}) async-start(bf16[16,24,2176]{2,1,0:T(8,128)(2,1)} %bitcast.23), calls=%async_computation.2 | async-start | bytes 3342336 | tf_op jit(solution)/shard_map/all_to_all | solution.py:294
  105.4 14.8 %collective-permute-start.7 = (bf16[384,768]{1,0:T(8,128)(2,1)}, bf16[384,768]{1,0:T(8,128)(2,1)S(1)}, u32[]{:S(2)}, u32[]{:S(2)}) collective-permute-start(bf16[384,768]{1,0:T(8,128)(2,1)} %get-tuple-element.47), channel_id=1, source_target_pairs={{0,16},{16,0},{1,17},{17,1},{2,18},{18,2},{3,19},{19,3},{4,20},{20... | collective-permute-start | bytes 1769480 | tf_op jit(solution)/shard_map/ppermute | solution.py:285
  120.2 23.5 %copy-start = (f32[128,2]{0,1:T(2,128)S(1)}, f32[128,2]{0,1:T(2,128)}, u32[]{:S(2)}) copy-start(f32[128,2]{0,1:T(2,128)} %param.9) | copy-start | bytes 3076

commit v13 on v12

--- a/solution.py
+++ b/solution.py
@@ -318,7 +318,7 @@
     def in_hbm(value):
         return pltpu.with_memory_space_constraint(value, pltpu.HBM)
 
-    block = tile_of(share, 512)
+    block = tile_of(share, 1024)
     steps = share // block
     small_spec = pl.BlockSpec((top, count), lambda c, g: (0, 0))
     scaled = pl.pallas_call(

time: 146 us -> 146 us (level)
  no operation moved by 1% of the time
where the time goes in v13:
time: 146 us; the launch traced here: 145 us
  waiting for transfers between devices  84.3 us (58%)
  starting transfers between devices  25.7 us (18%)
  Pallas kernels  24.6 us (17%)
  matrix products  4.19 us (3%)
  other arithmetic  3.82 us (3%)
  local copies, waits for them, and re-layouts  1.77 us (1%)
    all_to_all x3, waiting for transfers between devices, exchanged(): lax.all_to_all(split, 'expert', split_axis=0, concat_axis=0, axis_index_g...  40.6 us
    ppermute x2, waiting for transfers between devices, across(): return lax.ppermute(value, 'expert', pairs)  24.9 us
    ppermute x6, waiting for transfers between devices, shifted(): lax.ppermute(value, 'dp', [(i, (i + by) % groups) for i in range(groups)])  18.8 us
    all_to_all x3, starting transfers between devices, exchanged(): lax.all_to_all(split, 'expert', split_axis=0, concat_axis=0, axis_index_g...  17.9 us
    pallas_call x1, Pallas kernels, per_device(): pl.pallas_call(functools.partial(forward_kernel, groups), out_shape=[pltp...  5.25 us
    pallas_call x1, Pallas kernels, per_device(): pl.pallas_call(functools.partial(back_kernel, groups, cap), out_shape=[pl...  5.22 us
    pallas_call x1, Pallas kernels, per_device(): pl.pallas_call(functools.partial(backward_kernel, groups, cap), out_shape...  4.74 us
    ppermute x6, starting transfers between devices, shifted(): lax.ppermute(value, 'dp', [(i, (i + by) % groups) for i in range(groups)])  4.5 us
  transfers between devices with their start and end apart: 11, of which 7 were waited for; matrix products, arithmetic and copies ran while one was open for 6% of the time, Pallas kernels for 13%

profile of v13, /device:TPU:11, one launch (start us, length us, event | category | flops | bytes accessed | tf_op | source)
XLA Modules:
  0.0 145.0 jit_solution(11193562408693640808)
XLA Ops:
  0.6 1.3 collective-permute-start.3
  1.9 2.3 %collective-permute-start = (s32[2,128]{1,0:T(2,128)}, s32[2,128]{1,0:T(2,128)S(1)}, u32[]{:S(2)}, u32[]{:S(2)}) collective-permute-start(s32[2,128]{1,0:T(2,128)} %bitcast.32), channel_id=1, source_target_pairs={{0,8},{1,9},{2,10},{3,11},{4,12},{5,13},{6,14},{7,15},{8,0},{9,1},... | collective-permute-start | bytes 3080 | tf_op jit(solution)/shard_map/ppermute | solution.py:289
  4.2 0.2 collective-permute-start.4
  4.5 1.0 constant_dynamic-slice_fusion
  5.4 1.3 collective-permute-start.2
  6.7 0.0 collective-permute-done.refs_1_
  6.7 1.0 collective-permute-start.1
  7.8 3.7 %pad_maximum_fusion = bf16[2048,768]{1,0:T(8,128)(2,1)} fusion(bf16[1024,768]{1,0:T(8,128)(2,1)} %bitcast.25, bf16[1024,768]{1,0:T(8,128)(2,1)} %bitcast.29), kind=kLoop, calls=%fused_computation | loop fusion | flops 6291456 | bytes 6291456 | tf_op jit(solution)/shard_map/concatenate | solution.py:308
  11.5 0.0 collective-permute-done.3.refs_1_
  11.5 0.3 collective-permute-done.2.refs_5_
  11.8 1.2 collective-permute-start.5
  13.0 3.1 %dispatch_scaled.1 = bf16[768,1024]{1,0:T(8,128)(2,1)} custom-call(s32[1]{0:T(128)} %bitcast.place_ref, s32[2,128]{1,0:T(2,128)} %bitcast.33, s32[2,128]{1,0:T(2,128)S(1)} %collective-permute-done.3.refs_1_, f32[2,128]{1,0:T(2,128)} %bitcast.21, f32[2,128]{1,0:T(2,128)S(1)} %collective-permute-done.4.refs_3_, bf16[128,2048]{1,0:T(8,128)(2,1)} %refs_4_.1, ...), custom_call_target="tpu_custom_call" | custom-call | tf_op jit(solution)/shard_map/dispatch_scaled/pallas_call | solution.py:324
  16.1 6.6 %all-to-all-start.1 = ((bf16[16,48,1024]{2,1,0:T(8,128)(2,1)}), bf16[16,48,1024]{2,1,0:T(8,128)(2,1)S(1)}, u32[]{:S(2)}, u32[]{:S(2)}) async-start(bf16[16,48,1024]{2,1,0:T(8,128)(2,1)} %bitcast.24), calls=%async_computation.1 | async-start | bytes 3145728 | tf_op jit(solution)/shard_map/all_to_all | solution.py:294
  22.7 0.1 pad_add_fusion.place_ref
  22.8 24.8 %collective-permute-done.1.refs_3_ = bf16[128,2048]{1,0:T(8,128)(2,1)S(1)} collective-permute-done((bf16[128,2048]{1,0:T(8,128)(2,1)}, bf16[128,2048]{1,0:T(8,128)(2,1)S(1)}, u32[]{:S(2)}, u32[]{:S(2)}) %collective-permute-start.1) | collective-permute-done | bytes 524320 | tf_op jit(solution)/shard_map/ppermute | solution.py:289
  47.6 0.8 copy-done.2
  48.4 3.6 %dispatch_tokens.1 = (bf16[384,2048]{1,0:T(8,128)(2,1)}, s32[2,128]{1,0:T(2,128)S(1)}) custom-call(s32[2]{0:T(128)S(1)} %pad_add_fusion.place_ref, s32[2,128]{1,0:T(2,128)} %bitcast.34, s32[2,128]{1,0:T(2,128)S(1)} %collective-permute-done.refs_1_, bf16[128,2048]{1,0:T(8,128)(2,1)} %refs_2_.1, bf16[128,2048]{1,0:T(8,128)(2,1)} %copy-done.2), custom_call_target="tpu_custom_call" | custom-call | flops 30000001024 | bytes 30000000 | tf_op jit(solution)/shard_map/dispatch_tokens/pallas_call | solution.py:352
  52.0 13.9 %all-to-all-done.1 = bf16[16,48,1024]{2,1,0:T(8,128)(2,1)S(1)} async-done(((bf16[16,48,1024]{2,1,0:T(8,128)(2,1)}), bf16[16,48,1024]{2,1,0:T(8,128)(2,1)S(1)}, u32[]{:S(2)}, u32[]{:S(2)}) %all-to-all-start.1) | async-done | bytes 1572896 | tf_op jit(solution)/shard_map/all_to_all | solution.py:294
  65.9 4.0 %all-to-all-start = ((bf16[8,48,2048]{2,1,0:T(8,128)(2,1)}), bf16[8,48,2048]{2,1,0:T(8,128)(2,1)S(1)}, u32[]{:S(2)}, u32[]{:S(2)}) async-start(bf16[8,48,2048]{2,1,0:T(8,128)(2,1)} %bitcast.27), calls=%async_computation | async-start | bytes 3145728 | tf_op jit(solution)/shard_map/all_to_all | solution.py:294
  69.9 5.2 %back.1 = (f32[384,768]{1,0:T(8,128)}, bf16[384,768]{1,0:T(8,128)(2,1)}, bf16[768,1024]{1,0:T(8,128)(2,1)}) custom-call(s32[2]{0:T(128)S(1)} %pad_add_fusion.place_ref, bf16[768,1024]{1,0:T(8,128)(2,1)S(1)} %bitcast.18, bf16[768,1024]{1,0:T(8,128)(2,1)} %bitcast.28), custom_call_target="tpu_custom_call" | custom-call | tf_op jit(solution)/shard_map/back/pallas_call | solution.py:398
  75.1 0.2 collective-permute-start.6
  75.3 4.0 %collective-permute-done.5.refs_0_ = bf16[2048,768]{1,0:T(8,128)(2,1)} collective-permute-done((bf16[2048,768]{1,0:T(8,128)(2,1)}, bf16[2048,768]{1,0:T(8,128)(2,1)}, u32[]{:S(2)}, u32[]{:S(2)}) %collective-permute-start.5) | collective-permute-done | bytes 3145760 | tf_op jit(solution)/shard_map/ppermute | solution.py:285
  79.3 1.4 ready.1
  80.7 7.4 %all-to-all-done = bf16[8,48,2048]{2,1,0:T(8,128)(2,1)S(1)} async-done(((bf16[8,48,2048]{2,1,0:T(8,128)(2,1)}), bf16[8,48,2048]{2,1,0:T(8,128)(2,1)S(1)}, u32[]{:S(2)}, u32[]{:S(2)}) %all-to-all-start) | async-done | bytes 1572896 | tf_op jit(solution)/shard_map/all_to_all | solution.py:294
  88.1 5.3 %forward.1 = (f32[384,768]{1,0:T(8,128)S(1)}, f32[384,768]{1,0:T(8,128)S(1)}, f32[384,768]{1,0:T(8,128)S(1)}, bf16[384,768]{1,0:T(8,128)(2,1)}, bf16[3,1024,768]...) custom-call(bf16[384,2048]{1,0:T(8,128)(2,1)S(1)} %bitcast.19, bf16[1024,768]{1,0:T(8,128)(2,1)S(1)} %get-tuple-element.32.gate_ref, ...), custom_call_target="tpu_custom_call" | custom-call | tf_op jit(solution)/shard_map/forward/pallas_call | solution.py:410
  93.4 4.7 %backward.1 = bf16[384,2176]{1,0:T(8,128)(2,1)} custom-call(s32[1]{0:T(128)} %bitcast.1.half_ref, f32[384,768]{1,0:T(8,128)S(1)} %get-tuple-element.39.act_ref, f32[384,768]{1,0:T(8,128)S(1)} %get-tuple-element.40.slope_ref, f32[384,768]{1,0:T(8,128)S(1)} %get-tuple-element.41.value_ref, bf16[1024,768]{1,0:T(8,128)(2,1)S(1)} %get-tuple-element.32.gate_ref, ...), custom_call_target="tpu_custom_call" | custom-call | tf_op jit(solution)/shard_map/backward/pallas_call | solution.py:430
  98.1 7.3 %all-to-all-start.2 = ((bf16[16,24,2176]{2,1,0:T(8,128)(2,1)}), bf16[16,24,2176]{2,1,0:T(8,128)(2,1)S(1)}, u32[]{:S(2)}, u32[]{:S(2)}) async-start(bf16[16,24,2176]{2,1,0:T(8,128)(2,1)} %bitcast.23), calls=%async_computation.2 | async-start | bytes 3342336 | tf_op jit(solution)/shard_map/all_to_all | solution.py:294
  105.4 0.2 collective-permute-start.7
  105.7 14.5 %collective-permute-done.7 = bf16[384,768]{1,0:T(8,128)(2,1)S(1)} collective-permute-done((bf16[384,768]{1,0:T(8,128)(2,1)}, bf16[384,768]{1,0:T(8,128)(2,1)S(1)}, u32[]{:S(2)}, u32[]{:S(2)}) %collective-permute-start.7) | collective-permute-done | bytes 589856 | tf_op jit(solution)/shard_map/ppermute | solution.py:285
  120.2 4.2 %convolution_bitcast_fusion = f32[1,768,1024]{2,1,0:T(8,128)} fusion(bf16[768,1024]{1,0:T(8,128)(2,1)S(1)} %copy-done.1, bf16[384,768]{1,0:T(8,128)(2,1)S(1)} %collective-permute-done.7, bf16[384,768]{1,0:T(8,128)(2,1)} %get-tuple-element.47), kind=kOutput, calls=%fused_computation.1 | convolution fusion | flops 1210318848 | bytes 5898240 | tf_op jit(solution)/shard_map/dot_general | solution.py:23
  124.4 19.3 %all-to-all-done.2 = bf16[16,24,2176]{2,1,0:T(8,128)(2,1)S(1)} async-done(((bf16[16,24,2176]{2,1,0:T(8,128)(2,1)}), bf16[16,24,2176]{2,1,0:T(8,128)(2,1)S(1)}, u32[]{:S(2)}, u32[]{:S(2)}) %all-to-all-start.2) | async-done | bytes 1671200 | tf_op jit(solution)/shard_map/all_to_all | solution.py:294
  143.7 1.3 combine.1
  (7 shorter events, 0.0 us)
Async XLA Ops:
  0.6 10.9 %collective-permute-start.3 = (s32[2,128]{1,0:T(2,128)}, s32[2,128]{1,0:T(2,128)S(1)}, u32[]{:S(2)}, u32[]{:S(2)}) collective-permute-start(s32[2,128]{1,0:T(2,128)} %bitcast.31), channel_id=1, source_target_pairs={{0,16},{16,0},{1,17},{17,1},{2,18},{18,2},{3,19},{19,3},{4,20},{20... | collective-permute-start | bytes 3080 | tf_op jit(solution)/shard_map/ppermute | solution.py:285
  1.9 4.8 %collective-permute-start = (s32[2,128]{1,0:T(2,128)}, s32[2,128]{1,0:T(2,128)S(1)}, u32[]{:S(2)}, u32[]{:S(2)}) collective-permute-start(s32[2,128]{1,0:T(2,128)} %bitcast.32), channel_id=1, source_target_pairs={{0,8},{1,9},{2,10},{3,11},{4,12},{5,13},{6,14},{7,15},{8,0},{9,1},... | collective-permute-start | bytes 3080 | tf_op jit(solution)/shard_map/ppermute | solution.py:289
  4.2 7.3 %collective-permute-start.4 = (f32[2,128]{1,0:T(2,128)}, f32[2,128]{1,0:T(2,128)S(1)}, u32[]{:S(2)}, u32[]{:S(2)}) collective-permute-start(f32[2,128]{1,0:T(2,128)} %bitcast.20), channel_id=1, source_target_pairs={{0,16},{16,0},{1,17},{17,1},{2,18},{18,2},{3,19},{19,3},{4,20},{20... | collective-permute-start | bytes 3080 | tf_op jit(solution)/shard_map/ppermute | solution.py:285
  5.4 6.4 %collective-permute-start.2 = (bf16[128,1024]{1,0:T(8,128)(2,1)S(1)}, bf16[128,1024]{1,0:T(8,128)(2,1)S(1)}, u32[]{:S(2)}, u32[]{:S(2)}) collective-permute-start(bf16[128,1024]{1,0:T(8,128)(2,1)S(1)} %constant_dynamic-slice_fusion), channel_id=1, source_target_pairs={{0,16},{16,0},{1,17},{17,1},{2,18},{18,2},{3,19},{19,3},{4,20},{20... | collective-permute-start | bytes 786440 | tf_op jit(solution)/shard_map/ppermute | solution.py:285
  6.7 40.9 %collective-permute-start.1 = (bf16[128,2048]{1,0:T(8,128)(2,1)}, bf16[128,2048]{1,0:T(8,128)(2,1)S(1)}, u32[]{:S(2)}, u32[]{:S(2)}) collective-permute-start(bf16[128,2048]{1,0:T(8,128)(2,1)} %refs_2_.1), channel_id=1, source_target_pairs={{0,8},{1,9},{2,10},{3,11},{4,12},{5,13},{6,14},{7,15},{8,0},{9,1},... | collective-permute-start | bytes 1572872 | tf_op jit(solution)/shard_map/ppermute | solution.py:289
  11.8 67.5 %collective-permute-start.5 = (bf16[2048,768]{1,0:T(8,128)(2,1)}, bf16[2048,768]{1,0:T(8,128)(2,1)}, u32[]{:S(2)}, u32[]{:S(2)}) collective-permute-start(bf16[2048,768]{1,0:T(8,128)(2,1)} %pad_maximum_fusion), channel_id=1, source_target_pairs={{0,16},{16,0},{1,17},{17,1},{2,18},{18,2},{3,19},{19,3},{4,20},{20... | collective-permute-start | bytes 9437192 | tf_op jit(solution)/shard_map/ppermute | solution.py:285
  16.1 49.8 %all-to-all-start.1 = ((bf16[16,48,1024]{2,1,0:T(8,128)(2,1)}), bf16[16,48,1024]{2,1,0:T(8,128)(2,1)S(1)}, u32[]{:S(2)}, u32[]{:S(2)}) async-start(bf16[16,48,1024]{2,1,0:T(8,128)(2,1)} %bitcast.24), calls=%async_computation.1 | async-start | bytes 3145728 | tf_op jit(solution)/shard_map/all_to_all | solution.py:294
  47.6 0.8 copy-start.2
  65.9 22.2 %all-to-all-start = ((bf16[8,48,2048]{2,1,0:T(8,128)(2,1)}), bf16[8,48,2048]{2,1,0:T(8,128)(2,1)S(1)}, u32[]{:S(2)}, u32[]{:S(2)}) async-start(bf16[8,48,2048]{2,1,0:T(8,128)(2,1)} %bitcast.27), calls=%async_computation | async-start | bytes 3145728 | tf_op jit(solution)/shard_map/all_to_all | solution.py:294
  75.1 18.3 %collective-permute-start.6 = (bf16[384,768]{1,0:T(8,128)(2,1)}, bf16[384,768]{1,0:T(8,128)(2,1)}, u32[]{:S(2)}, u32[]{:S(2)}) collective-permute-start(bf16[384,768]{1,0:T(8,128)(2,1)} %get-tuple-element.44), channel_id=1, source_target_pairs={{0,16},{16,0},{1,17},{17,1},{2,18},{18,2},{3,19},{19,3},{4,20},{20... | collective-permute-start | bytes 1769480 | tf_op jit(solution)/shard_map/ppermute | solution.py:285
  98.1 22.1 %copy-start.1 = (bf16[768,1024]{1,0:T(8,128)(2,1)S(1)}, bf16[768,1024]{1,0:T(8,128)(2,1)}, u32[]{:S(2)}) copy-start(bf16[768,1024]{1,0:T(8,128)(2,1)} %get-tuple-element.48) | copy-start | bytes 4718596
  98.1 45.6 %all-to-all-start.2 = ((bf16[16,24,2176]{2,1,0:T(8,128)(2,1)}), bf16[16,24,2176]{2,1,0:T(8,128)(2,1)S(1)}, u32[]{:S(2)}, u32[]{:S(2)}) async-start(bf16[16,24,2176]{2,1,0:T(8,128)(2,1)} %bitcast.23), calls=%async_computation.2 | async-start | bytes 3342336 | tf_op jit(solution)/shard_map/all_to_all | solution.py:294
  105.4 14.8 %collective-permute-start.7 = (bf16[384,768]{1,0:T(8,128)(2,1)}, bf16[384,768]{1,0:T(8,128)(2,1)S(1)}, u32[]{:S(2)}, u32[]{:S(2)}) collective-permute-start(bf16[384,768]{1,0:T(8,128)(2,1)} %get-tuple-element.47), channel_id=1, source_target_pairs={{0,16},{16,0},{1,17},{17,1},{2,18},{18,2},{3,19},{19,3},{4,20},{20... | collective-permute-start | bytes 1769480 | tf_op jit(solution)/shard_map/ppermute | solution.py:285
  120.2 23.5 %copy-start = (f32[128,2]{0,1:T(2,128)S(1)}, f32[128,2]{0,1:T(2,128)}, u32[]{:S(2)}) copy-start(f32[128,2]{0,1:T(2,128)} %param.9) | copy-start | bytes 3076
